TPU v7x, 32 devices: a whole 2x2x4 slice. The times are simulated.
32 devices in a mesh: segment: 4 (over z), dp: 8 (over y, x, core).
Axes of the slice: x: 2, y: 2, z: 4, core: 2. Of those that a mesh axis runs over, the one named last changes fastest.
Arguments:
- tokens: bfloat16 [4, 256, 6144], P(None, 'dp'), may hold values from -18 to 18
- norm_gain: bfloat16 [6144], replicated, may hold values from 0.099609375 to 1.8984375
- router_weight: bfloat16 [6144, 4], replicated, may hold values from -0.078125 to 0.078125
- expert_ids: int32 [4, 256, 2], P(None, 'dp'), may hold values from 0 to 3, all different within a row; in each aligned block of 32 rows (0 to 31, 32 to 63, ..., all dimensions but the last counted through in order) at most 20 rows name the same one
- w_gate: bfloat16 [4, 6144, 8192], P('segment', None, 'dp'), may hold values from -0.078125 to 0.078125
- w_up: bfloat16 [4, 6144, 8192], P('segment', None, 'dp'), may hold values from -0.078125 to 0.078125
- w_down: bfloat16 [4, 8192, 6144], P('segment', 'dp'), may hold values from -0.0625 to 0.0625
Outputs:
- scored: bfloat16 [4, 256, 6144], P(None, 'dp', 'segment')
Inputs may be any that keep to these rules, and one draw needn't show every extreme that they name: `expert_ids`: each token names two different experts. In each micro-batch the 32 rows of one device name each expert at most 20 times, and in every draw some expert is named exactly 20 times by some device's rows.
All inputs are finite; a program needn't handle non-finite values.
Results may differ from a plain program's by a relative error of at most 0.0035.
Values may be sent and summed in bfloat16 or wider, within the bound.
No kernel may reach another device: no remote copies, remote signals or barrier semaphores. Data moves between devices by JAX's collectives and lax.ppermute only.
A program may use at most 128 MiB of HBM per device.

v0:
```python
import jax
import jax.numpy as jnp
from jax import lax
from jax.sharding import PartitionSpec as P

epsilon = 1e-05


def rms_normed(tokens, norm_gain):
    widened = tokens.astype(jnp.float32)
    inverse_rms = lax.rsqrt(jnp.mean(widened * widened, axis=-1, keepdims=True) + epsilon)
    return (widened, (widened * inverse_rms * norm_gain.astype(jnp.float32)).astype(jnp.bfloat16))


def pair_gates(pair_ids, logits):
    expert_range = jnp.arange(logits.shape[-1], dtype=jnp.int32)
    first_logit = jnp.sum(jnp.where(pair_ids[..., 0:1] == expert_range, logits, 0.0), axis=-1)
    second_logit = jnp.sum(jnp.where(pair_ids[..., 1:2] == expert_range, logits, 0.0), axis=-1)
    return (jax.nn.sigmoid(first_logit - second_logit), jax.nn.sigmoid(second_logit - first_logit))


def expert_weight(pair_ids, first_gate, second_gate, expert):
    return jnp.where(pair_ids[..., 0] == expert, first_gate, 0.0) + jnp.where(
        pair_ids[..., 1] == expert, second_gate, 0.0
    )


def slot_table(pair_ids, expert, slot_count):
    chosen = jnp.any(pair_ids == expert, axis=-1)
    hit_count = chosen.astype(jnp.int32)
    position = jnp.cumsum(hit_count, axis=-1) - hit_count
    slot_range = jnp.arange(slot_count, dtype=jnp.int32)
    dispatch = chosen[..., None, :] & (position[..., None, :] == slot_range[:, None])
    return (position, dispatch)


def per_device(tokens, norm_gain, router_weight, expert_ids, w_gate, w_up, w_down):
    micro_count, tok_rows, model_width = tokens.shape
    expert_count = router_weight.shape[1]
    slot_count = 2 * tok_rows // expert_count + tok_rows // 8
    segment_count = lax.axis_size("segment")
    segment_index = lax.axis_index("segment")
    slice_width = model_width // segment_count
    gate_matrix = w_gate[0]
    up_matrix = w_up[0]
    down_matrix = w_down[0]
    widened, normed = rms_normed(tokens, norm_gain)
    logits = jnp.dot(
        normed.reshape(-1, model_width), router_weight, preferred_element_type=jnp.float32
    )
    logits = logits.reshape(micro_count, tok_rows, expert_count)
    first_gate, second_gate = pair_gates(expert_ids, logits)
    outputs = []
    positions = []
    for micro_index in range(micro_count):
        position, dispatch = slot_table(expert_ids[micro_index], segment_index, slot_count)
        routed = jnp.dot(
            dispatch.astype(jnp.bfloat16), normed[micro_index], preferred_element_type=jnp.float32
        ).astype(jnp.bfloat16)
        piece_rows = lax.all_gather(routed, "dp", axis=0, tiled=True)
        gate_proj = jnp.dot(piece_rows, gate_matrix, preferred_element_type=jnp.float32)
        up_proj = jnp.dot(piece_rows, up_matrix, preferred_element_type=jnp.float32)
        hidden = (jax.nn.silu(gate_proj) * up_proj).astype(jnp.bfloat16)
        outputs.append(
            lax.psum_scatter(
                jnp.dot(hidden, down_matrix, preferred_element_type=jnp.float32),
                "dp",
                scatter_dimension=0,
                tiled=True,
            )
        )
        positions.append(position)
    own_part = lax.dynamic_slice_in_dim(widened, segment_index * slice_width, slice_width, 2)
    placed = []
    for micro_index in range(micro_count):
        weight = expert_weight(
            expert_ids[micro_index],
            first_gate[micro_index],
            second_gate[micro_index],
            segment_index,
        )
        taken = jnp.take(
            outputs[micro_index], jnp.clip(positions[micro_index], 0, slot_count - 1), axis=0
        )
        placed.append(weight[:, None] * taken)
    summed = lax.psum_scatter(jnp.stack(placed), "segment", scatter_dimension=2, tiled=True)
    return (own_part + summed).astype(jnp.bfloat16)


def solution(mesh):
    placed = (
        P(None, "dp", None),
        P(),
        P(),
        P(None, "dp", None),
        P("segment", None, "dp"),
        P("segment", None, "dp"),
        P("segment", "dp", None),
    )
    return jax.shard_map(
        per_device, mesh=mesh, in_specs=placed, out_specs=P(None, "dp", "segment"), check_vma=False
    )
```

profile of v0, /device:TPU:0, one launch (start us, length us, event | category | flops | bytes accessed | tf_op | source)
XLA Modules:
  0.0 537.9 jit_solution(12949608959793282160)
XLA Ops:
  18.1 27.0 %all-gather.13.cloned.1.call-done = bf16[8,20,6144]{2,1,0:T(8,128)(2,1)} async-done(((bf16[1,20,6144]{2,1,0:T(8,128)(2,1)}), bf16[8,20,6144]{2,1,0:T(8,128)(2,1)}) %all-gather.13.cloned.1.call-update) | async-done | bytes 1966096 | tf_op jit(solution)/shard_map/all_gather | solution.py:60
  45.1 2.6 reshape.195
  47.7 28.3 %all-gather.9.cloned.1.call-done = bf16[8,20,6144]{2,1,0:T(8,128)(2,1)} async-done(((bf16[1,20,6144]{2,1,0:T(8,128)(2,1)}), bf16[8,20,6144]{2,1,0:T(8,128)(2,1)}) %all-gather.9.cloned.1.call-update) | async-done | bytes 1966096 | tf_op jit(solution)/shard_map/all_gather | solution.py:60
  76.0 4.0 reshape.191
  80.1 26.9 %all-gather.11.cloned.1.call-done = bf16[8,20,6144]{2,1,0:T(8,128)(2,1)} async-done(((bf16[1,20,6144]{2,1,0:T(8,128)(2,1)}), bf16[8,20,6144]{2,1,0:T(8,128)(2,1)}) %all-gather.11.cloned.1.call-update) | async-done | bytes 1966096 | tf_op jit(solution)/shard_map/all_gather | solution.py:60
  107.0 4.0 reshape.193
  111.0 7.7 %fusion.24 = f32[160,1024]{1,0:T(8,128)S(1)} fusion(bf16[160,6144]{1,0:T(8,128)(2,1)} %reshape.193, bf16[1,6144,1024]{2,1,0:T(8,128)(2,1)} %param.13), kind=kOutput, calls=%fused_computation.24 | convolution fusion | flops 2013265920 | bytes 15204352 | tf_op jit(solution)/shard_map/dot_general | solution.py:61
  118.7 6.9 %fusion.26 = f32[160,1024]{1,0:T(8,128)S(1)} fusion(bf16[160,6144]{1,0:T(8,128)(2,1)S(1)} %copy-done.3, bf16[1,6144,1024]{2,1,0:T(8,128)(2,1)} %param.13), kind=kOutput, calls=%fused_computation.26 | convolution fusion | flops 2013265920 | bytes 15204352 | tf_op jit(solution)/shard_map/dot_general | solution.py:61
  125.6 3.1 fusion.22
  128.7 9.1 %all-gather.15.cloned.1.call-done = bf16[8,20,6144]{2,1,0:T(8,128)(2,1)} async-done(((bf16[1,20,6144]{2,1,0:T(8,128)(2,1)}), bf16[8,20,6144]{2,1,0:T(8,128)(2,1)}) %all-gather.15.cloned.1.call-update) | async-done | bytes 1966096 | tf_op jit(solution)/shard_map/all_gather | solution.py:60
  137.8 4.0 reshape.197
  141.7 8.2 %fusion.20 = f32[160,1024]{1,0:T(8,128)} fusion(bf16[160,6144]{1,0:T(8,128)(2,1)} %reshape.197, bf16[1,6144,1024]{2,1,0:T(8,128)(2,1)} %param.13), kind=kOutput, calls=%fused_computation.20 | convolution fusion | flops 2013265920 | bytes 15204352 | tf_op jit(solution)/shard_map/dot_general | solution.py:61
  150.0 15.1 %fusion.4 = f32[160,6144]{1,0:T(8,128)} fusion(bf16[1,1024,6144]{2,1,0:T(8,128)(2,1)} %param.15, bf16[160,6144]{1,0:T(8,128)(2,1)} %reshape.197, bf16[1,6144,1024]{2,1,0:T(8,128)(2,1)} %param.14, f32[160,1024]{1,0:T(8,128)} %fusion.20), kind=kOutput, calls=%fused_computation.4 | convolution fusion | flops 4027514880 | bytes 31719424 | tf_op jit(solution)/shard_map/dot_general | solution.py:66
  165.1 14.6 %fusion.6 = f32[160,6144]{1,0:T(8,128)} fusion(bf16[1,1024,6144]{2,1,0:T(8,128)(2,1)} %param.15, bf16[160,6144]{1,0:T(8,128)(2,1)S(1)} %reshape.195, bf16[1,6144,1024]{2,1,0:T(8,128)(2,1)} %param.14, f32[160,1024]{1,0:T(8,128)} %fusion.22), kind=kOutput, calls=%fused_computation.6 | convolution fusion | flops 4027514880 | bytes 31719424 | tf_op jit(solution)/shard_map/dot_general | solution.py:66
  179.7 15.4 %fusion.10 = f32[160,6144]{1,0:T(8,128)} fusion(bf16[1,1024,6144]{2,1,0:T(8,128)(2,1)} %param.15, bf16[160,6144]{1,0:T(8,128)(2,1)} %reshape.191, bf16[1,6144,1024]{2,1,0:T(8,128)(2,1)} %param.14, f32[160,1024]{1,0:T(8,128)S(1)} %fusion.26), kind=kOutput, calls=%fused_computation.10 | convolution fusion | flops 4027514880 | bytes 31719424 | tf_op jit(solution)/shard_map/dot_general | solution.py:66
  195.0 14.4 %fusion.8 = f32[160,6144]{1,0:T(8,128)} fusion(bf16[1,1024,6144]{2,1,0:T(8,128)(2,1)} %param.15, bf16[160,6144]{1,0:T(8,128)(2,1)S(1)} %copy-done.4, bf16[1,6144,1024]{2,1,0:T(8,128)(2,1)} %param.14, f32[160,1024]{1,0:T(8,128)S(1)} %fusion.24), kind=kOutput, calls=%fused_computation.8 | convolution fusion | flops 4027514880 | bytes 31719424 | tf_op jit(solution)/shard_map/dot_general | solution.py:66
  209.5 186.0 %fusion.114 = (f32[24,6144]{1,0:T(8,128)S(1)}, f32[24,6144]{1,0:T(8,128)S(1)}, f32[24,6144]{1,0:T(8,128)S(1)}, f32[24,6144]{1,0:T(8,128)}) fusion(f32[160,6144]{1,0:T(8,128)} %fusion.4, f32[160,6144]{1,0:T(8,128)} %fusion.6, f32[160,6144]{1,0:T(8,128)} %fusion.8, f32[160,6144]{1,0:T(8,128)} %fusion.10), kind=kCustom, calls=%all-reduce-scatter.4 | all-reduce-scatter fusion | flops 4718593 | bytes 18088448
  398.1 2.9 collective-permute-start.7
  401.0 4.3 collective-permute-start.4
  405.3 2.2 collective-permute-start.2
  408.5 2.3 collective-permute-start
  410.8 2.0 collective-permute-start.1
  413.6 1.9 collective-permute-start.5
  415.5 4.4 concatenate.3
  420.0 2.6 collective-permute-start.3
  422.6 6.9 %concatenate.2 = f32[52,6144]{1,0:T(8,128)S(1)} concatenate(f32[4,6144]{1,0:T(4,128)} %collective-permute-done.5, f32[24,6144]{1,0:T(8,128)} %collective-permute-done.4, f32[24,6144]{1,0:T(8,128)} %copy-done.7), dimensions={0} | concatenate | bytes 2555904
  429.6 6.0 %concatenate.1 = f32[52,6144]{1,0:T(8,128)S(1)} concatenate(f32[4,6144]{1,0:T(4,128)S(1)} %collective-permute-done.3, f32[24,6144]{1,0:T(8,128)} %collective-permute-done.2, f32[24,6144]{1,0:T(8,128)} %copy-done.6), dimensions={0} | concatenate | bytes 2555904
  435.7 10.2 %concatenate = f32[52,6144]{1,0:T(8,128)} concatenate(f32[4,6144]{1,0:T(4,128)} %collective-permute-done.1, f32[24,6144]{1,0:T(8,128)} %collective-permute-done, f32[24,6144]{1,0:T(8,128)} %get-tuple-element.19), dimensions={0} | concatenate | bytes 2555904
  453.8 1.9 pad_maximum_fusion
  457.1 2.0 convert_element_type.116
  459.1 70.1 %reduce-scatter.10.cloned.1.call-done = f32[4,32,1536]{2,1,0:T(8,128)} async-done(((f32[4,32,6144]{2,1,0:T(8,128)}), f32[4,32,1536]{2,1,0:T(8,128)}) %reduce-scatter.10.cloned.1.call-update) | async-done | bytes 786448 | tf_op jit(solution)/shard_map/reduce_scatter | solution.py:86
  529.2 2.2 add_convert_fusion
  (103 shorter events, 24.6 us)
Async XLA Ops:
  6.5 10.4 %copy-start = (bf16[6144,4]{0,1:T(4,128)(2,1)S(1)}, bf16[6144,4]{0,1:T(4,128)(2,1)}, u32[]{:S(2)}) copy-start(bf16[6144,4]{0,1:T(4,128)(2,1)} %param.11) | copy-start | bytes 147460
  6.5 38.6 %all-gather.13.cloned.1.call-start = ((), (), s32[]{:S(2)}) async-start(), calls=%async_computation.4 | async-start | bytes 2654208 | tf_op jit(solution)/shard_map/all_gather | solution.py:60
  10.4 6.5 %copy-start.10 = (s32[4,32,2]{1,2,0:T(2,128)S(1)}, s32[4,32,2]{1,2,0:T(2,128)}, u32[]{:S(2)}) copy-start(s32[4,32,2]{1,2,0:T(2,128)} %param.12) | copy-start | bytes 3076
  13.2 62.8 %all-gather.9.cloned.1.call-start = ((), (), s32[]{:S(2)}) async-start(), calls=%async_computation.2 | async-start | bytes 2654208 | tf_op jit(solution)/shard_map/all_gather | solution.py:60
  14.8 92.2 %all-gather.11.cloned.1.call-start = ((), (), s32[]{:S(2)}) async-start(), calls=%async_computation.3 | async-start | bytes 2654208 | tf_op jit(solution)/shard_map/all_gather | solution.py:60
  15.8 121.9 %all-gather.15.cloned.1.call-start = ((), (), s32[]{:S(2)}) async-start(), calls=%async_computation.5 | async-start | bytes 2654208 | tf_op jit(solution)/shard_map/all_gather | solution.py:60
  16.8 512.3 %reduce-scatter.10.cloned.1.call-start = ((), (), s32[]{:S(2)}) async-start(), calls=%async_computation.1 | async-start | bytes 3932160 | tf_op jit(solution)/shard_map/reduce_scatter | solution.py:86
  111.0 7.7 %copy-start.3 = (bf16[160,6144]{1,0:T(8,128)(2,1)S(1)}, bf16[160,6144]{1,0:T(8,128)(2,1)}, u32[]{:S(2)}) copy-start(bf16[160,6144]{1,0:T(8,128)(2,1)} %reshape.191) | copy-start | bytes 5898244
  111.0 14.6 %slice-start = ((s8[12582912]{0:T(1024)(128)(4,1)}), s8[4194304]{0:T(1024)(128)(4,1)S(1)}, s32[]{:S(2)}) async-start(s8[12582912]{0:T(1024)(128)(4,1)} %bitcast.169), calls=%async_computation.6 | async-start | bytes 8388608
  111.0 14.6 %slice-start.1 = ((s8[12582912]{0:T(1024)(128)(4,1)}), s8[4194304]{0:T(1024)(128)(4,1)S(1)}, s32[]{:S(2)}) async-start(s8[12582912]{0:T(1024)(128)(4,1)} %bitcast.169), calls=%async_computation.7 | async-start | bytes 8388608
  118.6 7.0 %slice-start.2 = ((s8[12582912]{0:T(1024)(128)(4,1)}), s8[4194304]{0:T(1024)(128)(4,1)S(1)}, s32[]{:S(2)}) async-start(s8[12582912]{0:T(1024)(128)(4,1)} %bitcast.169), calls=%async_computation.8 | async-start | bytes 8388608
  179.7 15.4 %copy-start.4 = (bf16[160,6144]{1,0:T(8,128)(2,1)S(1)}, bf16[160,6144]{1,0:T(8,128)(2,1)}, u32[]{:S(2)}) copy-start(bf16[160,6144]{1,0:T(8,128)(2,1)} %reshape.193) | copy-start | bytes 5898244
  209.5 187.3 %copy-start.11 = (u32[32]{0:T(128)S(1)}, u32[32]{0:T(128)}, u32[]{:S(2)}) copy-start(u32[32]{0:T(128)} %constant.50) | copy-start | bytes 388
  395.4 27.2 %copy-start.7 = (f32[24,6144]{1,0:T(8,128)}, f32[24,6144]{1,0:T(8,128)S(1)}, u32[]{:S(2)}) copy-start(f32[24,6144]{1,0:T(8,128)S(1)} %get-tuple-element.17) | copy-start | bytes 1769476
  395.4 34.1 %copy-start.6 = (f32[24,6144]{1,0:T(8,128)}, f32[24,6144]{1,0:T(8,128)S(1)}, u32[]{:S(2)}) copy-start(f32[24,6144]{1,0:T(8,128)S(1)} %get-tuple-element.18) | copy-start | bytes 1769476
  395.4 17.3 %collective-permute-start.6 = (f32[24,6144]{1,0:T(8,128)S(1)}, f32[24,6144]{1,0:T(8,128)S(1)}, u32[]{:S(2)}, u32[]{:S(2)}) collective-permute-start(f32[24,6144]{1,0:T(8,128)S(1)} %get-tuple-element.16), channel_id=1, source_target_pairs={{0,1},{1,2},{2,3},{3,4},{4,5},{5,6},{6,7},{8,9},{9,10},{10,11},{11... | collective-permute-start | bytes 1769480
  398.1 12.7 %collective-permute-start.7 = (f32[4,6144]{1,0:T(4,128)S(1)}, f32[4,6144]{1,0:T(4,128)S(1)}, u32[]{:S(2)}, u32[]{:S(2)}) collective-permute-start(f32[4,6144]{1,0:T(4,128)S(1)} %slice.123), channel_id=1, source_target_pairs={{0,2},{1,3},{2,4},{3,5},{4,6},{5,7},{8,10},{9,11},{10,12},{11,13},... | collective-permute-start | bytes 294920
  401.0 21.6 %collective-permute-start.4 = (f32[24,6144]{1,0:T(8,128)S(1)}, f32[24,6144]{1,0:T(8,128)}, u32[]{:S(2)}, u32[]{:S(2)}) collective-permute-start(f32[24,6144]{1,0:T(8,128)S(1)} %get-tuple-element.17), channel_id=1, source_target_pairs={{0,1},{1,2},{2,3},{3,4},{4,5},{5,6},{6,7},{8,9},{9,10},{10,11},{11... | collective-permute-start | bytes 1769480
  405.3 24.3 %collective-permute-start.2 = (f32[24,6144]{1,0:T(8,128)S(1)}, f32[24,6144]{1,0:T(8,128)}, u32[]{:S(2)}, u32[]{:S(2)}) collective-permute-start(f32[24,6144]{1,0:T(8,128)S(1)} %get-tuple-element.18), channel_id=1, source_target_pairs={{0,1},{1,2},{2,3},{3,4},{4,5},{5,6},{6,7},{8,9},{9,10},{10,11},{11... | collective-permute-start | bytes 1769480
  408.5 27.2 %collective-permute-start = (f32[24,6144]{1,0:T(8,128)}, f32[24,6144]{1,0:T(8,128)}, u32[]{:S(2)}, u32[]{:S(2)}) collective-permute-start(f32[24,6144]{1,0:T(8,128)} %get-tuple-element.19), channel_id=1, source_target_pairs={{0,1},{1,2},{2,3},{3,4},{4,5},{5,6},{6,7},{8,9},{9,10},{10,11},{11... | collective-permute-start | bytes 1769480
  410.8 2.0 copy-start.9
  410.8 24.9 %collective-permute-start.1 = (f32[4,6144]{1,0:T(4,128)S(1)}, f32[4,6144]{1,0:T(4,128)}, u32[]{:S(2)}, u32[]{:S(2)}) collective-permute-start(f32[4,6144]{1,0:T(4,128)S(1)} %slice.120), channel_id=1, source_target_pairs={{0,2},{1,3},{2,4},{3,5},{4,6},{5,7},{8,10},{9,11},{10,12},{11,13},... | collective-permute-start | bytes 294920
  412.8 0.8 copy-start.8
  413.6 6.4 %collective-permute-start.5 = (f32[4,6144]{1,0:T(4,128)S(1)}, f32[4,6144]{1,0:T(4,128)}, u32[]{:S(2)}, u32[]{:S(2)}) collective-permute-start(f32[4,6144]{1,0:T(4,128)S(1)} %slice.122), channel_id=1, source_target_pairs={{0,2},{1,3},{2,4},{3,5},{4,6},{5,7},{8,10},{9,11},{10,12},{11,13},... | collective-permute-start | bytes 294920
  420.0 9.6 %collective-permute-start.3 = (f32[4,6144]{1,0:T(4,128)S(1)}, f32[4,6144]{1,0:T(4,128)S(1)}, u32[]{:S(2)}, u32[]{:S(2)}) collective-permute-start(f32[4,6144]{1,0:T(4,128)S(1)} %slice.121), channel_id=1, source_target_pairs={{0,2},{1,3},{2,4},{3,5},{4,6},{5,7},{8,10},{9,11},{10,12},{11,13},... | collective-permute-start | bytes 294920
  451.3 2.1 copy-start.5
  455.7 1.4 copy-start.2
  457.1 74.3 %copy-start.1 = (bf16[6144,4]{0,1:T(4,128)(2,1)S(1)}, bf16[6144,4]{0,1:T(4,128)(2,1)}, u32[]{:S(2)}) copy-start(bf16[6144,4]{0,1:T(4,128)(2,1)} %param.11) | copy-start | bytes 147460
Sparse Core Ops, SparseCore 0:
  13.4 31.7 all-gather.12
  47.0 29.0 all-gather.8
  77.9 29.0 all-gather.10
  108.7 29.0 all-gather.14
  455.8 73.2 reduce-scatter.9
where the time goes:
time: 539 us; the launch traced here: 538 us
  blocking collectives  186 us (35%)
  waiting for transfers between devices  161 us (30%)
  matrix products  90.3 us (17%)
  local copies, waits for them, and re-layouts  52.6 us (10%)
  starting transfers between devices  19.6 us (4%)
  between operations  14.2 us (3%)
  other arithmetic  13.7 us (3%)
    unnamed x1, blocking collectives  186 us
    all_gather x4, waiting for transfers between devices, per_device(): piece_rows = lax.all_gather(routed, 'dp', axis=0, tiled=True)  91.3 us
    reduce_scatter x1, waiting for transfers between devices, per_device(): lax.psum_scatter(jnp.stack(placed), 'segment', scatter_dimension=2, tiled...  70.1 us
    dot_general x4, matrix products, per_device(): jnp.dot(hidden, down_matrix, preferred_element_type=jnp.float32)  59.5 us
    unnamed x47, local copies, waits for them, and re-layouts  47.3 us
    dot_general x4, matrix products, per_device(): jnp.dot(piece_rows, gate_matrix, preferred_element_type=jnp.float32)  25.9 us
    unnamed x8, starting transfers between devices  19.5 us
  transfers between devices with their start and end apart: 13, of which 5 were waited for; matrix products, arithmetic and copies ran while one was open for 10% of the time, Pallas kernels for 0%

commit v1 on v0

v1 whole, which is shorter than its diff:
```python
import functools

import jax
import jax.numpy as jnp
from jax import lax
from jax.experimental import pallas as pl
from jax.experimental.pallas import tpu as pltpu
from jax.sharding import PartitionSpec as P

epsilon = 1e-05
F32 = jnp.float32
BF16 = jnp.bfloat16
VMEM_LIMIT = 56 * 1024 * 1024


def exchange(array, axis, distance):
    count = lax.axis_size(axis)
    return lax.ppermute(array, axis, [(i, i ^ distance) for i in range(count)])


def chunk_rows(slot_total):
    units = slot_total // 16
    first = (units + 1) // 2
    return (first * 16, (units - first) * 16)


def route_kernel(rows, slots, expert_count, chunks, *refs):
    me, tokens_ref, gain_ref, router_ref, ids_ref, ids_row_ref = refs[:6]
    routed_refs, gates_ref = refs[6:-1], refs[-1]
    token_count = tokens_ref.shape[0]
    widened = tokens_ref[...].astype(F32)
    inverse_rms = lax.rsqrt(jnp.mean(widened * widened, axis=-1, keepdims=True) + epsilon)
    normed = (widened * inverse_rms * gain_ref[...].astype(F32)).astype(BF16)
    chosen = jnp.any(ids_row_ref[...] == me[0], axis=0, keepdims=True)
    earlier = lax.broadcasted_iota(jnp.int32, (token_count, token_count), 0)
    later = lax.broadcasted_iota(jnp.int32, (token_count, token_count), 1)
    same = lax.div(earlier, rows) == lax.div(later, rows)
    before = jnp.where((earlier < later) & same, 1.0, 0.0).astype(BF16)
    hits = jnp.where(chosen, 1.0, 0.0).astype(BF16)
    position = jnp.dot(
        jnp.broadcast_to(hits, (16, token_count)), before, preferred_element_type=F32
    )[0:1].astype(jnp.int32)
    token = lax.broadcasted_iota(jnp.int32, (1, token_count), 1)
    slot = lax.div(token, rows) * slots + position
    start = 0
    for routed_ref, size in zip(routed_refs, chunks):
        wanted = lax.broadcasted_iota(jnp.int32, (size, token_count), 0) + start
        dispatch = jnp.where((wanted == slot) & chosen, 1.0, 0.0).astype(BF16)
        routed_ref[...] = jnp.dot(dispatch, normed, preferred_element_type=F32).astype(BF16)
        start += size
    logits = lax.dot_general(
        normed, router_ref[...], (((1,), (1,)), ((), ())), preferred_element_type=F32
    )
    expert = lax.broadcasted_iota(jnp.int32, (token_count, expert_count), 1)
    first = jnp.sum(jnp.where(ids_ref[:, 0:1] == expert, logits, 0.0), axis=-1, keepdims=True)
    second = jnp.sum(jnp.where(ids_ref[:, 1:2] == expert, logits, 0.0), axis=-1, keepdims=True)
    gates_ref[:, 0:1] = jax.nn.sigmoid(first - second)
    gates_ref[:, 1:2] = jax.nn.sigmoid(second - first)


def route(me, tokens, norm_gain, router_weight, ids, rows, slots, chunks):
    token_count, width = tokens.shape
    expert_count = router_weight.shape[1]
    vmem = pl.BlockSpec(memory_space=pltpu.VMEM)
    out = pl.pallas_call(
        functools.partial(route_kernel, rows, slots, expert_count, chunks),
        out_shape=tuple(jax.ShapeDtypeStruct((c, width), BF16) for c in chunks)
        + (jax.ShapeDtypeStruct((token_count, 2), F32),),
        in_specs=[pl.BlockSpec(memory_space=pltpu.SMEM)] + [vmem] * 5,
        out_specs=(vmem,) * (len(chunks) + 1),
        compiler_params=pltpu.CompilerParams(vmem_limit_bytes=VMEM_LIMIT),
        name="route",
    )(me, tokens, norm_gain.reshape(1, width), router_weight.T, ids, ids.T)
    return out[:-1], out[-1]


def expert_kernel(block_count, up_steps, tile, *refs):
    blocks = refs[:block_count]
    gate_ref, up_ref, down_ref, kept_ref, sent_ref, rows_ref, hidden_ref, sems = refs[block_count:]
    size = blocks[0].shape[0]
    half = block_count // 2 * size
    step = pl.program_id(0)

    @pl.when(step == 0)
    def _():
        copies = [
            pltpu.make_async_copy(b, rows_ref.at[pl.ds(i * size, size)], sems.at[i])
            for i, b in enumerate(blocks)
        ]
        for c in copies:
            c.start()
        for c in copies:
            c.wait()

    @pl.when(step < up_steps)
    def _():
        gate = jnp.dot(rows_ref[...], gate_ref[...], preferred_element_type=F32)
        up = jnp.dot(rows_ref[...], up_ref[...], preferred_element_type=F32)
        hidden = gate / (1.0 + jnp.exp(-gate)) * up
        hidden_ref[:, pl.ds(pl.multiple_of(step * tile, tile), tile)] = hidden.astype(BF16)

    @pl.when(step >= up_steps)
    def _():
        out = jnp.dot(hidden_ref[...], down_ref[...], preferred_element_type=F32)
        kept_ref[...] = out[:half]
        sent_ref[...] = out[half:].astype(BF16)


def expert(blocks, gate_matrix, up_matrix, down_matrix):
    count, (size, width) = len(blocks), blocks[0].shape
    units = gate_matrix.shape[1]
    rows = count * size
    tile, down_tile = 256, 1024
    up_steps, down_steps = units // tile, width // down_tile
    up_spec = pl.BlockSpec((width, tile), lambda i: (0, jnp.minimum(i, up_steps - 1)))
    down_index = lambda i: (0, jnp.maximum(i - up_steps, 0))
    return pl.pallas_call(
        functools.partial(expert_kernel, count, up_steps, tile),
        out_shape=(
            jax.ShapeDtypeStruct((rows // 2, width), F32),
            jax.ShapeDtypeStruct((rows // 2, width), BF16),
        ),
        grid=(up_steps + down_steps,),
        in_specs=[pl.BlockSpec(memory_space=pl.ANY)] * count
        + [up_spec, up_spec, pl.BlockSpec((units, down_tile), down_index)],
        out_specs=(
            pl.BlockSpec((rows // 2, down_tile), down_index),
            pl.BlockSpec((rows // 2, down_tile), down_index),
        ),
        scratch_shapes=[
            pltpu.VMEM((rows, width), BF16),
            pltpu.VMEM((rows, units), BF16),
            pltpu.SemaphoreType.DMA((count,)),
        ],
        cost_estimate=pl.CostEstimate(
            flops=6 * rows * width * units,
            bytes_accessed=6 * width * units + 5 * rows * width,
            transcendentals=rows * units,
        ),
        compiler_params=pltpu.CompilerParams(vmem_limit_bytes=VMEM_LIMIT),
        name="expert",
    )(*blocks, gate_matrix, up_matrix, down_matrix)


def combine_kernel(rows, slots, count, chunks, *refs):
    me, own_ref, ids_ref, gates_ref = refs[:4]
    taken_refs, out_ref = refs[4:-1], refs[-1]
    token_count = own_ref.shape[0]
    later = lax.broadcasted_iota(jnp.int32, (token_count, token_count), 0)
    earlier = lax.broadcasted_iota(jnp.int32, (token_count, token_count), 1)
    same = lax.div(earlier, rows) == lax.div(later, rows)
    before = jnp.where((earlier < later) & same, 1.0, 0.0).astype(BF16)
    token = lax.broadcasted_iota(jnp.int32, (token_count, 1), 0)
    total = own_ref[...].astype(F32)
    for k in range(count):
        which = me[0] ^ k
        first, second = ids_ref[:, 0:1] == which, ids_ref[:, 1:2] == which
        chosen = first | second
        hits = jnp.where(chosen, 1.0, 0.0).astype(BF16)
        position = jnp.dot(
            before, jnp.broadcast_to(hits, (token_count, 128)), preferred_element_type=F32
        )[:, 0:1].astype(jnp.int32)
        slot = lax.div(token, rows) * slots + position
        weight = jnp.where(first, gates_ref[:, 0:1], 0.0) + jnp.where(
            second, gates_ref[:, 1:2], 0.0
        )
        start, placed = 0, None
        for c, size in enumerate(chunks):
            held = lax.broadcasted_iota(jnp.int32, (token_count, size), 1) + start
            pick = jnp.where((held == slot) & chosen, 1.0, 0.0).astype(BF16)
            part = jnp.dot(pick, taken_refs[c * count + k][...], preferred_element_type=F32)
            placed = part if placed is None else placed + part
            start += size
        total += weight * placed
    out_ref[...] = total.astype(BF16)


def combine(me, own, ids, gates, taken, rows, slots, chunks):
    count = len(taken) // len(chunks)
    vmem = pl.BlockSpec(memory_space=pltpu.VMEM)
    return pl.pallas_call(
        functools.partial(combine_kernel, rows, slots, count, chunks),
        out_shape=jax.ShapeDtypeStruct(own.shape, BF16),
        in_specs=[pl.BlockSpec(memory_space=pltpu.SMEM)] + [vmem] * (3 + len(taken)),
        out_specs=vmem,
        compiler_params=pltpu.CompilerParams(vmem_limit_bytes=VMEM_LIMIT),
        name="combine",
    )(me, own, ids, gates, *taken)


def gather_blocks(own, bits):
    held = {0: own}
    if len(bits) == 2:
        a, b = bits
        half = own.shape[0] // 2
        held[a], held[b] = exchange(own, "dp", a), exchange(own, "dp", b)
        low, high = exchange(held[b][:half], "dp", a), exchange(held[a][half:], "dp", b)
        return held, (low, high)
    for bit in bits:
        held.update({k | bit: exchange(v, "dp", bit) for k, v in list(held.items())})
    return held, None


def reduce_lane(terms, bits):
    terms = dict(terms)
    for bit in bits:
        leaving = sorted(k for k in terms if k & bit)
        outgoing = jnp.stack([sum(t.astype(F32) for t in terms[k]).astype(BF16) for k in leaving])
        incoming = exchange(outgoing, "dp", bit)
        for i, k in enumerate(leaving):
            terms[k ^ bit] = terms[k ^ bit] + [incoming[i]]
            del terms[k]
    return sum(t.astype(F32) for t in terms[0])


def per_device(tokens, norm_gain, router_weight, expert_ids, w_gate, w_up, w_down):
    micro_count, rows, width = tokens.shape
    expert_count = router_weight.shape[1]
    slots = 2 * rows // expert_count + rows // 8
    segment_count = lax.axis_size("segment")
    segment = lax.axis_index("segment")
    me = segment.astype(jnp.int32).reshape(1)
    bits = []
    while 2 ** (len(bits) + 1) < lax.axis_size("dp"):
        bits.append(2 ** (len(bits) + 1))
    slice_width = width // segment_count
    chunks = chunk_rows(micro_count * slots)
    flat = tokens.reshape(-1, width)
    ids = expert_ids.reshape(-1, 2)
    own_part = lax.dynamic_slice_in_dim(flat, segment * slice_width, slice_width, 1)
    routed, gates = route(me, flat, norm_gain, router_weight, ids, rows, slots, chunks)
    taken = []
    for own in routed:
        size = own.shape[0]
        held, halves = gather_blocks(own, bits)
        if halves is not None:
            held[bits[0] | bits[1]] = jnp.concatenate(halves)
        order = sorted(held)
        blocks = [held[k] for k in order]
        blocks = blocks + [exchange(b, "dp", 1) for b in blocks]
        kept, sent = expert(blocks, w_gate[0], w_up[0], w_down[0])
        partner = exchange(sent, "dp", 1)
        lanes = []
        for lane, lane_bits in enumerate((bits, bits[::-1])):
            columns = slice(lane * width // 2, (lane + 1) * width // 2)
            terms = {
                k: [a[i * size : (i + 1) * size, columns] for a in (kept, partner)]
                for i, k in enumerate(order)
            }
            lanes.append(reduce_lane(terms, lane_bits))
        total = jnp.concatenate(lanes, axis=1).astype(BF16)
        for k in range(segment_count):
            part = lax.dynamic_slice_in_dim(
                total, (segment ^ k) * slice_width, slice_width, 1
            )
            taken.append(part if k == 0 else exchange(part, "segment", k))
    out = combine(me, own_part, ids, gates, taken, rows, slots, chunks)
    return out.reshape(micro_count, rows, slice_width)


def solution(mesh):
    placed = (
        P(None, "dp", None),
        P(),
        P(),
        P(None, "dp", None),
        P("segment", None, "dp"),
        P("segment", None, "dp"),
        P("segment", "dp", None),
    )
    return jax.shard_map(
        per_device, mesh=mesh, in_specs=placed, out_specs=P(None, "dp", "segment"), check_vma=False
    )
```

time: 539 us -> 192 us (0.36)
  blocking collectives: 186 us -> 0 us
  matrix products: 90.3 us -> 0 us
  waiting for transfers between devices: 161 us -> 79.2 us
  Pallas kernels: 0 us -> 59.4 us
  local copies, waits for them, and re-layouts: 52.6 us -> 6.04 us
  starting transfers between devices: 19.6 us -> 33.8 us
  between operations: 14.2 us -> 0.34 us
    unnamed x1 -> x0, blocking collectives: 186 us -> none
    all_gather x4 -> x0, waiting for transfers between devices: 91.3 us -> none  [per_device(): piece_rows = lax.all_gather(routed, 'dp', axis=0, tiled=True)]
    dot_general x13 -> x0, matrix products: 90.3 us -> none  [the longest x4 59.5 us: per_device(): jnp.dot(hidden, down_matrix, preferred_element_type=jnp.float32)]
    ppermute x0 -> x32, waiting for transfers between devices: none -> 79.2 us  [exchange(): return lax.ppermute(array, axis, [(i, i ^ distance) for i in range(count)])]
    reduce_scatter x1 -> x0, waiting for transfers between devices: 70.1 us -> none  [per_device(): lax.psum_scatter(jnp.stack(placed), 'segment', scatter_dimension=2, tiled...]
    pallas_call x0 -> x4, Pallas kernels: none -> 59.4 us  [the longest x2 51.4 us: expert(): pl.pallas_call(functools.partial(expert_kernel, count, up_steps, tile), o...]
    unnamed x47 -> x41, local copies, waits for them, and re-layouts: 47.3 us -> 2.25 us
    ppermute x0 -> x32, starting transfers between devices: none -> 33.8 us  [exchange(): return lax.ppermute(array, axis, [(i, i ^ distance) for i in range(count)])]
  transfers between devices with their start and end apart: 13 -> 32, of which waited for: 5 -> 13; matrix products, arithmetic and copies ran while one was open for 10% -> 7% of each run, Pallas kernels for 0% -> 27%
where the time goes in v1:
time: 192 us; the launch traced here: 191 us
  waiting for transfers between devices  79.2 us (41%)
  Pallas kernels  59.4 us (31%)
  starting transfers between devices  33.8 us (18%)
  other arithmetic  12.3 us (6%)
  local copies, waits for them, and re-layouts  6.04 us (3%)
    ppermute x32, waiting for transfers between devices, exchange(): return lax.ppermute(array, axis, [(i, i ^ distance) for i in range(count)])  79.2 us
    pallas_call x2, Pallas kernels, expert(): pl.pallas_call(functools.partial(expert_kernel, count, up_steps, tile), o...  51.4 us
    ppermute x32, starting transfers between devices, exchange(): return lax.ppermute(array, axis, [(i, i ^ distance) for i in range(count)])  33.8 us
    another operation x8, other arithmetic, reduce_lane(): jnp.stack([sum((t.astype(F32) for t in terms[k])).astype(BF16) for k in l...  5.6 us
    another operation x4, other arithmetic  4.61 us
    pallas_call x1, Pallas kernels, combine(): pl.pallas_call(functools.partial(combine_kernel, rows, slots, count, chun...  4.33 us
  transfers between devices with their start and end apart: 32, of which 13 were waited for; matrix products, arithmetic and copies ran while one was open for 7% of the time, Pallas kernels for 27%

profile of v1, /device:TPU:0, one launch (start us, length us, event | category | flops | bytes accessed | tf_op | source)
XLA Modules:
  0.0 190.9 jit_solution(17808989889651008178)
XLA Ops:
  2.7 3.6 %route.1 = (bf16[48,6144]{1,0:T(8,128)(2,1)}, bf16[32,6144]{1,0:T(8,128)(2,1)}, f32[128,2]{1,0:T(8,128)}) custom-call(s32[1]{0:T(128)} %bitcast.refs_0_, bf16[128,6144]{1,0:T(8,128)(2,1)} %bitcast.92, bf16[1,6144]{1,0:T(2,128)(2,1)} %reshape.42.refs_2_, bf16[4,6144]{1,0:T(4,128)(2,1)} %bitcast.97, s32[128,2]{1,0:T(8,128)} %bitcast.95, s32[2,128]{1,0:T(2,128)} %copy.9.refs_5_), custom_call_target="tpu_custom_call" | custom-call | tf_op jit(solution)/shard_map/route/pallas_call | solution.py:65
  6.3 3.0 %collective-permute-start.17 = (bf16[32,6144]{1,0:T(8,128)(2,1)}, bf16[32,6144]{1,0:T(8,128)(2,1)S(1)}, u32[]{:S(2)}, u32[]{:S(2)}) collective-permute-start(bf16[32,6144]{1,0:T(8,128)(2,1)} %get-tuple-element.16.refs_0_), channel_id=1, source_target_pairs={{0,4},{1,5},{2,6},{3,7},{4,0},{5,1},{6,2},{7,3},{8,12},{9,13},{10,... | collective-permute-start | bytes 1179656 | tf_op jit(solution)/shard_map/ppermute | solution.py:18
  9.3 1.5 collective-permute-start.16
  10.8 7.8 %collective-permute-done.17.refs_2_ = bf16[32,6144]{1,0:T(8,128)(2,1)S(1)} collective-permute-done((bf16[32,6144]{1,0:T(8,128)(2,1)}, bf16[32,6144]{1,0:T(8,128)(2,1)S(1)}, u32[]{:S(2)}, u32[]{:S(2)}) %collective-permute-start.17) | collective-permute-done | bytes 393248 | tf_op jit(solution)/shard_map/ppermute | solution.py:18
  18.6 1.8 collective-permute-start.18
  20.4 1.5 collective-permute-start.1
  22.5 2.3 %collective-permute-done.18 = bf16[16,6144]{1,0:T(8,128)(2,1)S(1)} collective-permute-done((bf16[16,6144]{1,0:T(8,128)(2,1)S(1)}, bf16[16,6144]{1,0:T(8,128)(2,1)S(1)}, u32[]{:S(2)}, u32[]{:S(2)}) %collective-permute-start.18) | collective-permute-done | bytes 196640 | tf_op jit(solution)/shard_map/ppermute | solution.py:18
  24.8 2.4 %collective-permute-start.19 = (bf16[16,6144]{1,0:T(8,128)(2,1)S(1)}, bf16[16,6144]{1,0:T(8,128)(2,1)S(1)}, u32[]{:S(2)}, u32[]{:S(2)}) collective-permute-start(bf16[16,6144]{1,0:T(8,128)(2,1)S(1)} %slice.191), channel_id=1, source_target_pairs={{0,4},{1,5},{2,6},{3,7},{4,0},{5,1},{6,2},{7,3},{8,12},{9,13},{10,... | collective-permute-start | bytes 589832 | tf_op jit(solution)/shard_map/ppermute | solution.py:18
  27.2 9.6 %collective-permute-done.1.refs_2_ = bf16[48,6144]{1,0:T(8,128)(2,1)S(1)} collective-permute-done((bf16[48,6144]{1,0:T(8,128)(2,1)}, bf16[48,6144]{1,0:T(8,128)(2,1)S(1)}, u32[]{:S(2)}, u32[]{:S(2)}) %collective-permute-start.1) | collective-permute-done | bytes 589856 | tf_op jit(solution)/shard_map/ppermute | solution.py:18
  36.8 3.8 %collective-permute-done.19 = bf16[16,6144]{1,0:T(8,128)(2,1)S(1)} collective-permute-done((bf16[16,6144]{1,0:T(8,128)(2,1)S(1)}, bf16[16,6144]{1,0:T(8,128)(2,1)S(1)}, u32[]{:S(2)}, u32[]{:S(2)}) %collective-permute-start.19) | collective-permute-done | bytes 196640 | tf_op jit(solution)/shard_map/ppermute | solution.py:18
  41.1 8.2 %collective-permute-done.2 = bf16[24,6144]{1,0:T(8,128)(2,1)S(1)} collective-permute-done((bf16[24,6144]{1,0:T(8,128)(2,1)S(1)}, bf16[24,6144]{1,0:T(8,128)(2,1)S(1)}, u32[]{:S(2)}, u32[]{:S(2)}) %collective-permute-start.2) | collective-permute-done | bytes 294944 | tf_op jit(solution)/shard_map/ppermute | solution.py:18
  49.2 1.5 collective-permute-start.3
  50.8 6.2 %collective-permute-done.3 = bf16[24,6144]{1,0:T(8,128)(2,1)S(1)} collective-permute-done((bf16[24,6144]{1,0:T(8,128)(2,1)S(1)}, bf16[24,6144]{1,0:T(8,128)(2,1)S(1)}, u32[]{:S(2)}, u32[]{:S(2)}) %collective-permute-start.3) | collective-permute-done | bytes 294944 | tf_op jit(solution)/shard_map/ppermute | solution.py:18
  59.5 23.6 %expert.3 = (f32[128,6144]{1,0:T(8,128)}, bf16[128,6144]{1,0:T(8,128)(2,1)}) custom-call(bf16[32,6144]{1,0:T(8,128)(2,1)} %get-tuple-element.16.refs_0_, bf16[32,6144]{1,0:T(8,128)(2,1)} %copy-done.4, bf16[32,6144]{1,0:T(8,128)(2,1)} %copy-done.3, bf16[32,6144]{1,0:T(8,128)(2,1)} %copy-done.5, bf16[32,6144]{1,0:T(8,128)(2,1)} %copy-done.6, ...), custom_call_target="tpu_custom_call" | custom-call | flops 9663676416 | bytes 45613056 | tf_op jit(solution)/shard_map/expert/pallas_call | solution.py:117
  83.3 27.8 %expert.2 = (f32[192,6144]{1,0:T(8,128)}, bf16[192,6144]{1,0:T(8,128)(2,1)}) custom-call(bf16[48,6144]{1,0:T(8,128)(2,1)} %get-tuple-element.13.refs_0_, bf16[48,6144]{1,0:T(8,128)(2,1)} %copy-done.11, bf16[48,6144]{1,0:T(8,128)(2,1)} %copy-done.10, bf16[48,6144]{1,0:T(8,128)(2,1)} %copy-done.12, bf16[48,6144]{1,0:T(8,128)(2,1)} %collective-permute-done.4.refs_4_, ...), custom_call_target="tpu_custom_call" | custom-call | flops 14495514624 | bytes 49545216 | tf_op jit(solution)/shard_map/expert/pallas_call | solution.py:117
  112.8 1.6 collective-permute-start.27
  114.4 1.8 collective-permute-done.8
  116.2 1.7 fusion.10
  117.9 1.6 collective-permute-start.11
  119.5 5.3 %collective-permute-done.27 = bf16[2,32,3072]{2,1,0:T(8,128)(2,1)S(1)} collective-permute-done((bf16[2,32,3072]{2,1,0:T(8,128)(2,1)S(1)}, bf16[2,32,3072]{2,1,0:T(8,128)(2,1)S(1)}, u32[]{:S(2)}, u32[]{:S(2)}) %collective-permute-start.27) | collective-permute-done | bytes 393248 | tf_op jit(solution)/shard_map/ppermute | solution.py:18
  126.5 1.7 collective-permute-start.28
  128.2 8.3 %collective-permute-done.11 = bf16[2,48,3072]{2,1,0:T(8,128)(2,1)S(1)} collective-permute-done((bf16[2,48,3072]{2,1,0:T(8,128)(2,1)S(1)}, bf16[2,48,3072]{2,1,0:T(8,128)(2,1)S(1)}, u32[]{:S(2)}, u32[]{:S(2)}) %collective-permute-start.11) | collective-permute-done | bytes 589856 | tf_op jit(solution)/shard_map/ppermute | solution.py:18
  138.4 1.7 collective-permute-start.12
  141.3 1.6 collective-permute-start.26
  142.9 15.9 %collective-permute-done.12 = bf16[1,48,3072]{2,1,0:T(8,128)(2,1)S(1)} collective-permute-done((bf16[1,48,3072]{2,1,0:T(8,128)(2,1)S(1)}, bf16[1,48,3072]{2,1,0:T(8,128)(2,1)S(1)}, u32[]{:S(2)}, u32[]{:S(2)}) %collective-permute-start.12) | collective-permute-done | bytes 294944 | tf_op jit(solution)/shard_map/ppermute | solution.py:18
  160.2 1.6 collective-permute-start.10
  163.8 1.6 collective-permute-start.29
  165.4 2.6 %collective-permute-start.30 = (bf16[32,1536]{1,0:T(8,128)(2,1)S(1)}, bf16[32,1536]{1,0:T(8,128)(2,1)S(1)}, u32[]{:S(2)}, u32[]{:S(2)}) collective-permute-start(bf16[32,1536]{1,0:T(8,128)(2,1)S(1)} %get-tuple-element.40), channel_id=1, source_target_pairs={{0,16},{8,24},{16,0},{24,8},{1,17},{9,25},{17,1},{25,9},{2,18},{10... | collective-permute-start | bytes 294920 | tf_op jit(solution)/shard_map/ppermute | solution.py:18
  171.2 3.4 %collective-permute-start.14 = (bf16[48,1536]{1,0:T(8,128)(2,1)S(1)}, bf16[48,1536]{1,0:T(8,128)(2,1)S(1)}, u32[]{:S(2)}, u32[]{:S(2)}) collective-permute-start(bf16[48,1536]{1,0:T(8,128)(2,1)S(1)} %get-tuple-element.36), channel_id=1, source_target_pairs={{0,16},{8,24},{16,0},{24,8},{1,17},{9,25},{17,1},{25,9},{2,18},{10... | collective-permute-start | bytes 442376 | tf_op jit(solution)/shard_map/ppermute | solution.py:18
  174.8 1.8 constant_dynamic-slice_fusion.refs_1_
  177.3 8.6 %collective-permute-done.14.refs_6_ = bf16[48,1536]{1,0:T(8,128)(2,1)S(1)} collective-permute-done((bf16[48,1536]{1,0:T(8,128)(2,1)S(1)}, bf16[48,1536]{1,0:T(8,128)(2,1)S(1)}, u32[]{:S(2)}, u32[]{:S(2)}) %collective-permute-start.14) | collective-permute-done | bytes 147488 | tf_op jit(solution)/shard_map/ppermute | solution.py:18
  186.6 4.3 %combine.1 = bf16[128,1536]{1,0:T(8,128)(2,1)} custom-call(s32[1]{0:T(128)} %bitcast.refs_0_, bf16[128,1536]{1,0:T(8,128)(2,1)} %constant_dynamic-slice_fusion.refs_1_, s32[128,2]{1,0:T(8,128)} %bitcast.96, f32[128,2]{1,0:T(8,128)} %get-tuple-element.12.refs_3_, bf16[48,1536]{1,0:T(8,128)(2,1)} %get-tuple-element.34.refs_4_, bf16[48,1536]{1,0:T(8,128)(2,1)} %copy-done.13, ...), custom_call_target="tpu_custom_call" | custom-call | tf_op jit(solution)/shard_map/combine/pallas_call | solution.py:181
  (100 shorter events, 21.0 us)
Async XLA Ops:
  6.3 12.3 %collective-permute-start.17 = (bf16[32,6144]{1,0:T(8,128)(2,1)}, bf16[32,6144]{1,0:T(8,128)(2,1)S(1)}, u32[]{:S(2)}, u32[]{:S(2)}) collective-permute-start(bf16[32,6144]{1,0:T(8,128)(2,1)} %get-tuple-element.16.refs_0_), channel_id=1, source_target_pairs={{0,4},{1,5},{2,6},{3,7},{4,0},{5,1},{6,2},{7,3},{8,12},{9,13},{10,... | collective-permute-start | bytes 1179656 | tf_op jit(solution)/shard_map/ppermute | solution.py:18
  9.3 13.2 %collective-permute-start.16 = (bf16[32,6144]{1,0:T(8,128)(2,1)}, bf16[32,6144]{1,0:T(8,128)(2,1)S(1)}, u32[]{:S(2)}, u32[]{:S(2)}) collective-permute-start(bf16[32,6144]{1,0:T(8,128)(2,1)} %get-tuple-element.16.refs_0_), channel_id=1, source_target_pairs={{0,2},{1,3},{2,0},{3,1},{4,6},{5,7},{6,4},{7,5},{8,10},{9,11},{10,... | collective-permute-start | bytes 1179656 | tf_op jit(solution)/shard_map/ppermute | solution.py:18
  18.6 6.1 %collective-permute-start.18 = (bf16[16,6144]{1,0:T(8,128)(2,1)S(1)}, bf16[16,6144]{1,0:T(8,128)(2,1)S(1)}, u32[]{:S(2)}, u32[]{:S(2)}) collective-permute-start(bf16[16,6144]{1,0:T(8,128)(2,1)S(1)} %slice.190), channel_id=1, source_target_pairs={{0,2},{1,3},{2,0},{3,1},{4,6},{5,7},{6,4},{7,5},{8,10},{9,11},{10,... | collective-permute-start | bytes 589832 | tf_op jit(solution)/shard_map/ppermute | solution.py:18
  20.4 36.6 %collective-permute-start.20 = (bf16[32,6144]{1,0:T(8,128)(2,1)}, bf16[32,6144]{1,0:T(8,128)(2,1)S(1)}, u32[]{:S(2)}, u32[]{:S(2)}) collective-permute-start(bf16[32,6144]{1,0:T(8,128)(2,1)} %get-tuple-element.16.refs_0_), channel_id=1, source_target_pairs={{0,1},{1,0},{2,3},{3,2},{4,5},{5,4},{6,7},{7,6},{8,9},{9,8},{10,11... | collective-permute-start | bytes 1179656 | tf_op jit(solution)/shard_map/ppermute | solution.py:18
  20.4 16.3 %collective-permute-start.1 = (bf16[48,6144]{1,0:T(8,128)(2,1)}, bf16[48,6144]{1,0:T(8,128)(2,1)S(1)}, u32[]{:S(2)}, u32[]{:S(2)}) collective-permute-start(bf16[48,6144]{1,0:T(8,128)(2,1)} %get-tuple-element.13.refs_0_), channel_id=1, source_target_pairs={{0,4},{1,5},{2,6},{3,7},{4,0},{5,1},{6,2},{7,3},{8,12},{9,13},{10,... | collective-permute-start | bytes 1769480 | tf_op jit(solution)/shard_map/ppermute | solution.py:18
  22.0 19.0 %collective-permute-start = (bf16[48,6144]{1,0:T(8,128)(2,1)}, bf16[48,6144]{1,0:T(8,128)(2,1)S(1)}, u32[]{:S(2)}, u32[]{:S(2)}) collective-permute-start(bf16[48,6144]{1,0:T(8,128)(2,1)} %get-tuple-element.13.refs_0_), channel_id=1, source_target_pairs={{0,2},{1,3},{2,0},{3,1},{4,6},{5,7},{6,4},{7,5},{8,10},{9,11},{10,... | collective-permute-start | bytes 1769480 | tf_op jit(solution)/shard_map/ppermute | solution.py:18
  22.5 60.8 %collective-permute-start.4 = (bf16[48,6144]{1,0:T(8,128)(2,1)}, bf16[48,6144]{1,0:T(8,128)(2,1)}, u32[]{:S(2)}, u32[]{:S(2)}) collective-permute-start(bf16[48,6144]{1,0:T(8,128)(2,1)} %get-tuple-element.13.refs_0_), channel_id=1, source_target_pairs={{0,1},{1,0},{2,3},{3,2},{4,5},{5,4},{6,7},{7,6},{8,9},{9,8},{10,11... | collective-permute-start | bytes 1769480 | tf_op jit(solution)/shard_map/ppermute | solution.py:18
  24.8 15.8 %collective-permute-start.19 = (bf16[16,6144]{1,0:T(8,128)(2,1)S(1)}, bf16[16,6144]{1,0:T(8,128)(2,1)S(1)}, u32[]{:S(2)}, u32[]{:S(2)}) collective-permute-start(bf16[16,6144]{1,0:T(8,128)(2,1)S(1)} %slice.191), channel_id=1, source_target_pairs={{0,4},{1,5},{2,6},{3,7},{4,0},{5,1},{6,2},{7,3},{8,12},{9,13},{10,... | collective-permute-start | bytes 589832 | tf_op jit(solution)/shard_map/ppermute | solution.py:18
  36.8 20.9 %collective-permute-start.21 = (bf16[32,6144]{1,0:T(8,128)(2,1)S(1)}, bf16[32,6144]{1,0:T(8,128)(2,1)S(1)}, u32[]{:S(2)}, u32[]{:S(2)}) collective-permute-start(bf16[32,6144]{1,0:T(8,128)(2,1)S(1)} %collective-permute-done.16.refs_1_), channel_id=1, source_target_pairs={{0,1},{1,0},{2,3},{3,2},{4,5},{5,4},{6,7},{7,6},{8,9},{9,8},{10,11... | collective-permute-start | bytes 1179656 | tf_op jit(solution)/shard_map/ppermute | solution.py:18
  40.6 8.6 %collective-permute-start.2 = (bf16[24,6144]{1,0:T(8,128)(2,1)S(1)}, bf16[24,6144]{1,0:T(8,128)(2,1)S(1)}, u32[]{:S(2)}, u32[]{:S(2)}) collective-permute-start(bf16[24,6144]{1,0:T(8,128)(2,1)S(1)} %slice.176), channel_id=1, source_target_pairs={{0,2},{1,3},{2,0},{3,1},{4,6},{5,7},{6,4},{7,5},{8,10},{9,11},{10,... | collective-permute-start | bytes 884744 | tf_op jit(solution)/shard_map/ppermute | solution.py:18
  41.0 16.8 %collective-permute-start.22 = (bf16[32,6144]{1,0:T(8,128)(2,1)S(1)}, bf16[32,6144]{1,0:T(8,128)(2,1)S(1)}, u32[]{:S(2)}, u32[]{:S(2)}) collective-permute-start(bf16[32,6144]{1,0:T(8,128)(2,1)S(1)} %collective-permute-done.17.refs_2_), channel_id=1, source_target_pairs={{0,1},{1,0},{2,3},{3,2},{4,5},{5,4},{6,7},{7,6},{8,9},{9,8},{10,11... | collective-permute-start | bytes 1179656 | tf_op jit(solution)/shard_map/ppermute | solution.py:18
  49.2 7.8 %collective-permute-start.3 = (bf16[24,6144]{1,0:T(8,128)(2,1)S(1)}, bf16[24,6144]{1,0:T(8,128)(2,1)S(1)}, u32[]{:S(2)}, u32[]{:S(2)}) collective-permute-start(bf16[24,6144]{1,0:T(8,128)(2,1)S(1)} %slice.177), channel_id=1, source_target_pairs={{0,4},{1,5},{2,6},{3,7},{4,0},{5,1},{6,2},{7,3},{8,12},{9,13},{10,... | collective-permute-start | bytes 884744 | tf_op jit(solution)/shard_map/ppermute | solution.py:18
  57.0 1.7 collective-permute-start.23
  57.0 26.3 %collective-permute-start.5 = (bf16[48,6144]{1,0:T(8,128)(2,1)S(1)}, bf16[48,6144]{1,0:T(8,128)(2,1)}, u32[]{:S(2)}, u32[]{:S(2)}) collective-permute-start(bf16[48,6144]{1,0:T(8,128)(2,1)S(1)} %collective-permute-done.refs_1_), channel_id=1, source_target_pairs={{0,1},{1,0},{2,3},{3,2},{4,5},{5,4},{6,7},{7,6},{8,9},{9,8},{10,11... | collective-permute-start | bytes 1769480 | tf_op jit(solution)/shard_map/ppermute | solution.py:18
  57.6 25.7 %collective-permute-start.6 = (bf16[48,6144]{1,0:T(8,128)(2,1)S(1)}, bf16[48,6144]{1,0:T(8,128)(2,1)}, u32[]{:S(2)}, u32[]{:S(2)}) collective-permute-start(bf16[48,6144]{1,0:T(8,128)(2,1)S(1)} %collective-permute-done.1.refs_2_), channel_id=1, source_target_pairs={{0,1},{1,0},{2,3},{3,2},{4,5},{5,4},{6,7},{7,6},{8,9},{9,8},{10,11... | collective-permute-start | bytes 1769480 | tf_op jit(solution)/shard_map/ppermute | solution.py:18
  57.7 25.6 %collective-permute-start.7 = (bf16[48,6144]{1,0:T(8,128)(2,1)S(1)}, bf16[48,6144]{1,0:T(8,128)(2,1)}, u32[]{:S(2)}, u32[]{:S(2)}) collective-permute-start(bf16[48,6144]{1,0:T(8,128)(2,1)S(1)} %constant_dynamic-update-slice_fusion.refs_3_), channel_id=1, source_target_pairs={{0,1},{1,0},{2,3},{3,2},{4,5},{5,4},{6,7},{7,6},{8,9},{9,8},{10,11... | collective-permute-start | bytes 1769480 | tf_op jit(solution)/shard_map/ppermute | solution.py:18
  83.1 28.5 %collective-permute-start.24 = (bf16[128,6144]{1,0:T(8,128)(2,1)}, bf16[128,6144]{1,0:T(8,128)(2,1)}, u32[]{:S(2)}, u32[]{:S(2)}) collective-permute-start(bf16[128,6144]{1,0:T(8,128)(2,1)} %get-tuple-element.18), channel_id=1, source_target_pairs={{0,1},{1,0},{2,3},{3,2},{4,5},{5,4},{6,7},{7,6},{8,9},{9,8},{10,11... | collective-permute-start | bytes 4718600 | tf_op jit(solution)/shard_map/ppermute | solution.py:18
  111.1 5.0 %collective-permute-start.8 = (bf16[192,6144]{1,0:T(8,128)(2,1)}, bf16[192,6144]{1,0:T(8,128)(2,1)}, u32[]{:S(2)}, u32[]{:S(2)}) collective-permute-start(bf16[192,6144]{1,0:T(8,128)(2,1)} %get-tuple-element.15), channel_id=1, source_target_pairs={{0,1},{1,0},{2,3},{3,2},{4,5},{5,4},{6,7},{7,6},{8,9},{9,8},{10,11... | collective-permute-start | bytes 7077896 | tf_op jit(solution)/shard_map/ppermute | solution.py:18
  112.8 12.0 %collective-permute-start.27 = (bf16[2,32,3072]{2,1,0:T(8,128)(2,1)S(1)}, bf16[2,32,3072]{2,1,0:T(8,128)(2,1)S(1)}, u32[]{:S(2)}, u32[]{:S(2)}) collective-permute-start(bf16[2,32,3072]{2,1,0:T(8,128)(2,1)S(1)} %pad_maximum_fusion.3), channel_id=1, source_target_pairs={{0,4},{1,5},{2,6},{3,7},{4,0},{5,1},{6,2},{7,3},{8,12},{9,13},{10,... | collective-permute-start | bytes 1179656 | tf_op jit(solution)/shard_map/ppermute | solution.py:18
  117.9 18.7 %collective-permute-start.11 = (bf16[2,48,3072]{2,1,0:T(8,128)(2,1)S(1)}, bf16[2,48,3072]{2,1,0:T(8,128)(2,1)S(1)}, u32[]{:S(2)}, u32[]{:S(2)}) collective-permute-start(bf16[2,48,3072]{2,1,0:T(8,128)(2,1)S(1)} %pad_maximum_fusion.1), channel_id=1, source_target_pairs={{0,4},{1,5},{2,6},{3,7},{4,0},{5,1},{6,2},{7,3},{8,12},{9,13},{10,... | collective-permute-start | bytes 1769480 | tf_op jit(solution)/shard_map/ppermute | solution.py:18
  126.2 14.0 %collective-permute-start.25 = (bf16[2,32,3072]{2,1,0:T(8,128)(2,1)S(1)}, bf16[2,32,3072]{2,1,0:T(8,128)(2,1)S(1)}, u32[]{:S(2)}, u32[]{:S(2)}) collective-permute-start(bf16[2,32,3072]{2,1,0:T(8,128)(2,1)S(1)} %pad_maximum_fusion.2), channel_id=1, source_target_pairs={{0,2},{1,3},{2,0},{3,1},{4,6},{5,7},{6,4},{7,5},{8,10},{9,11},{10,... | collective-permute-start | bytes 1179656 | tf_op jit(solution)/shard_map/ppermute | solution.py:18
  126.5 13.6 %collective-permute-start.28 = (bf16[1,32,3072]{2,1,0:T(8,128)(2,1)S(1)}, bf16[1,32,3072]{2,1,0:T(8,128)(2,1)S(1)}, u32[]{:S(2)}, u32[]{:S(2)}) collective-permute-start(bf16[1,32,3072]{2,1,0:T(8,128)(2,1)S(1)} %get-tuple-element.28), channel_id=1, source_target_pairs={{0,2},{1,3},{2,0},{3,1},{4,6},{5,7},{6,4},{7,5},{8,10},{9,11},{10,... | collective-permute-start | bytes 589832 | tf_op jit(solution)/shard_map/ppermute | solution.py:18
  138.1 20.8 %collective-permute-start.9 = (bf16[2,48,3072]{2,1,0:T(8,128)(2,1)S(1)}, bf16[2,48,3072]{2,1,0:T(8,128)(2,1)S(1)}, u32[]{:S(2)}, u32[]{:S(2)}) collective-permute-start(bf16[2,48,3072]{2,1,0:T(8,128)(2,1)S(1)} %pad_maximum_fusion), channel_id=1, source_target_pairs={{0,2},{1,3},{2,0},{3,1},{4,6},{5,7},{6,4},{7,5},{8,10},{9,11},{10,... | collective-permute-start | bytes 1769480 | tf_op jit(solution)/shard_map/ppermute | solution.py:18
  138.4 20.4 %collective-permute-start.12 = (bf16[1,48,3072]{2,1,0:T(8,128)(2,1)S(1)}, bf16[1,48,3072]{2,1,0:T(8,128)(2,1)S(1)}, u32[]{:S(2)}, u32[]{:S(2)}) collective-permute-start(bf16[1,48,3072]{2,1,0:T(8,128)(2,1)S(1)} %get-tuple-element.21), channel_id=1, source_target_pairs={{0,2},{1,3},{2,0},{3,1},{4,6},{5,7},{6,4},{7,5},{8,10},{9,11},{10,... | collective-permute-start | bytes 884744 | tf_op jit(solution)/shard_map/ppermute | solution.py:18
  141.3 20.5 %collective-permute-start.26 = (bf16[1,32,3072]{2,1,0:T(8,128)(2,1)S(1)}, bf16[1,32,3072]{2,1,0:T(8,128)(2,1)S(1)}, u32[]{:S(2)}, u32[]{:S(2)}) collective-permute-start(bf16[1,32,3072]{2,1,0:T(8,128)(2,1)S(1)} %get-tuple-element.27), channel_id=1, source_target_pairs={{0,4},{1,5},{2,6},{3,7},{4,0},{5,1},{6,2},{7,3},{8,12},{9,13},{10,... | collective-permute-start | bytes 589832 | tf_op jit(solution)/shard_map/ppermute | solution.py:18
  160.2 8.0 %collective-permute-start.10 = (bf16[1,48,3072]{2,1,0:T(8,128)(2,1)S(1)}, bf16[1,48,3072]{2,1,0:T(8,128)(2,1)S(1)}, u32[]{:S(2)}, u32[]{:S(2)}) collective-permute-start(bf16[1,48,3072]{2,1,0:T(8,128)(2,1)S(1)} %get-tuple-element.20), channel_id=1, source_target_pairs={{0,4},{1,5},{2,6},{3,7},{4,0},{5,1},{6,2},{7,3},{8,12},{9,13},{10,... | collective-permute-start | bytes 884744 | tf_op jit(solution)/shard_map/ppermute | solution.py:18
  163.8 10.7 %collective-permute-start.29 = (bf16[32,1536]{1,0:T(8,128)(2,1)S(1)}, bf16[32,1536]{1,0:T(8,128)(2,1)S(1)}, u32[]{:S(2)}, u32[]{:S(2)}) collective-permute-start(bf16[32,1536]{1,0:T(8,128)(2,1)S(1)} %get-tuple-element.39), channel_id=1, source_target_pairs={{0,8},{8,0},{16,24},{24,16},{1,9},{9,1},{17,25},{25,17},{2,10},{10... | collective-permute-start | bytes 294920 | tf_op jit(solution)/shard_map/ppermute | solution.py:18
  165.4 11.2 %collective-permute-start.30 = (bf16[32,1536]{1,0:T(8,128)(2,1)S(1)}, bf16[32,1536]{1,0:T(8,128)(2,1)S(1)}, u32[]{:S(2)}, u32[]{:S(2)}) collective-permute-start(bf16[32,1536]{1,0:T(8,128)(2,1)S(1)} %get-tuple-element.40), channel_id=1, source_target_pairs={{0,16},{8,24},{16,0},{24,8},{1,17},{9,25},{17,1},{25,9},{2,18},{10... | collective-permute-start | bytes 294920 | tf_op jit(solution)/shard_map/ppermute | solution.py:18
  168.0 8.6 %collective-permute-start.31 = (bf16[32,1536]{1,0:T(8,128)(2,1)S(1)}, bf16[32,1536]{1,0:T(8,128)(2,1)S(1)}, u32[]{:S(2)}, u32[]{:S(2)}) collective-permute-start(bf16[32,1536]{1,0:T(8,128)(2,1)S(1)} %get-tuple-element.37), channel_id=1, source_target_pairs={{0,24},{8,16},{16,8},{24,0},{1,25},{9,17},{17,9},{25,1},{2,26},{10... | collective-permute-start | bytes 294920 | tf_op jit(solution)/shard_map/ppermute | solution.py:18
  170.4 6.9 %collective-permute-start.13 = (bf16[48,1536]{1,0:T(8,128)(2,1)S(1)}, bf16[48,1536]{1,0:T(8,128)(2,1)S(1)}, u32[]{:S(2)}, u32[]{:S(2)}) collective-permute-start(bf16[48,1536]{1,0:T(8,128)(2,1)S(1)} %get-tuple-element.35), channel_id=1, source_target_pairs={{0,8},{8,0},{16,24},{24,16},{1,9},{9,1},{17,25},{25,17},{2,10},{10... | collective-permute-start | bytes 442376 | tf_op jit(solution)/shard_map/ppermute | solution.py:18
  171.2 14.7 %collective-permute-start.14 = (bf16[48,1536]{1,0:T(8,128)(2,1)S(1)}, bf16[48,1536]{1,0:T(8,128)(2,1)S(1)}, u32[]{:S(2)}, u32[]{:S(2)}) collective-permute-start(bf16[48,1536]{1,0:T(8,128)(2,1)S(1)} %get-tuple-element.36), channel_id=1, source_target_pairs={{0,16},{8,24},{16,0},{24,8},{1,17},{9,25},{17,1},{25,9},{2,18},{10... | collective-permute-start | bytes 442376 | tf_op jit(solution)/shard_map/ppermute | solution.py:18
  174.6 11.3 %collective-permute-start.15 = (bf16[48,1536]{1,0:T(8,128)(2,1)S(1)}, bf16[48,1536]{1,0:T(8,128)(2,1)S(1)}, u32[]{:S(2)}, u32[]{:S(2)}) collective-permute-start(bf16[48,1536]{1,0:T(8,128)(2,1)S(1)} %get-tuple-element.33), channel_id=1, source_target_pairs={{0,24},{8,16},{16,8},{24,0},{1,25},{9,17},{17,9},{25,1},{2,26},{10... | collective-permute-start | bytes 442376 | tf_op jit(solution)/shard_map/ppermute | solution.py:18
  (19 other events, 304.2 us)

commit v2 on v1

--- a/solution.py
+++ b/solution.py
@@ -10,7 +10,8 @@
 epsilon = 1e-05
 F32 = jnp.float32
 BF16 = jnp.bfloat16
-VMEM_LIMIT = 56 * 1024 * 1024
+VMEM_LIMIT = 16 * 1024 * 1024
+EXPERT_VMEM = 48 * 1024 * 1024
 
 
 def exchange(array, axis, distance):
@@ -21,7 +22,7 @@
 def chunk_rows(slot_total):
     units = slot_total // 16
     first = (units + 1) // 2
-    return (first * 16, (units - first) * 16)
+    return 16 * ((first + 1) // 2), 16 * (first // 2), 16 * (units - first)
 
 
 def route_kernel(rows, slots, expert_count, chunks, *refs):
@@ -74,72 +75,118 @@
     return out[:-1], out[-1]
 
 
-def expert_kernel(block_count, up_steps, tile, *refs):
-    blocks = refs[:block_count]
-    gate_ref, up_ref, down_ref, kept_ref, sent_ref, rows_ref, hidden_ref, sems = refs[block_count:]
-    size = blocks[0].shape[0]
-    half = block_count // 2 * size
-    step = pl.program_id(0)
-
-    @pl.when(step == 0)
-    def _():
-        copies = [
-            pltpu.make_async_copy(b, rows_ref.at[pl.ds(i * size, size)], sems.at[i])
-            for i, b in enumerate(blocks)
-        ]
-        for c in copies:
-            c.start()
-        for c in copies:
+def staged(fetches, ahead):
+    def arrive(n):
+        for c in fetches[n]:
             c.wait()
-
-    @pl.when(step < up_steps)
-    def _():
-        gate = jnp.dot(rows_ref[...], gate_ref[...], preferred_element_type=F32)
-        up = jnp.dot(rows_ref[...], up_ref[...], preferred_element_type=F32)
+        if n + ahead < len(fetches):
+            for c in fetches[n + ahead]:
+                c.start()
+
+    for c in [c for group in fetches[:ahead] for c in group]:
+        c.start()
+    return arrive
+
+
+def up_kernel(block_count, *refs):
+    blocks, refs = refs[:block_count], refs[block_count:]
+    gate_ref, up_ref, hidden_ref, rows_ref, held_ref, sems, held_sems = refs
+    buffers, _, _, tile = held_ref.shape
+    copies, start = [], 0
+    for i, block in enumerate(blocks):
+        target = rows_ref.at[pl.ds(start, block.shape[0])]
+        copies.append(pltpu.make_async_copy(block, target, sems.at[i]))
+        start += block.shape[0]
+    for c in copies:
+        c.start()
+    fetches = []
+    for j in range(gate_ref.shape[1] // tile):
+        part, slot = pl.ds(j * tile, tile), j % buffers
+        fetches.append(
+            [
+                pltpu.make_async_copy(r.at[:, part], held_ref.at[slot, i], held_sems.at[slot, i])
+                for i, r in enumerate((gate_ref, up_ref))
+            ]
+        )
+    arrive = staged(fetches, 2)
+    for c in copies:
+        c.wait()
+    for j in range(len(fetches)):
+        arrive(j)
+        gate = jnp.dot(rows_ref[...], held_ref[j % buffers, 0], preferred_element_type=F32)
+        up = jnp.dot(rows_ref[...], held_ref[j % buffers, 1], preferred_element_type=F32)
         hidden = gate / (1.0 + jnp.exp(-gate)) * up
-        hidden_ref[:, pl.ds(pl.multiple_of(step * tile, tile), tile)] = hidden.astype(BF16)
-
-    @pl.when(step >= up_steps)
-    def _():
-        out = jnp.dot(hidden_ref[...], down_ref[...], preferred_element_type=F32)
-        kept_ref[...] = out[:half]
-        sent_ref[...] = out[half:].astype(BF16)
-
-
-def expert(blocks, gate_matrix, up_matrix, down_matrix):
-    count, (size, width) = len(blocks), blocks[0].shape
-    units = gate_matrix.shape[1]
-    rows = count * size
-    tile, down_tile = 256, 1024
-    up_steps, down_steps = units // tile, width // down_tile
-    up_spec = pl.BlockSpec((width, tile), lambda i: (0, jnp.minimum(i, up_steps - 1)))
-    down_index = lambda i: (0, jnp.maximum(i - up_steps, 0))
+        hidden_ref[:, j * tile : (j + 1) * tile] = hidden.astype(BF16)
+
+
+def up_projection(blocks, gate_matrix, up_matrix):
+    rows, (width, units) = sum(b.shape[0] for b in blocks), gate_matrix.shape
+    buffers, tile = 3, 256
     return pl.pallas_call(
-        functools.partial(expert_kernel, count, up_steps, tile),
-        out_shape=(
-            jax.ShapeDtypeStruct((rows // 2, width), F32),
-            jax.ShapeDtypeStruct((rows // 2, width), BF16),
-        ),
-        grid=(up_steps + down_steps,),
-        in_specs=[pl.BlockSpec(memory_space=pl.ANY)] * count
-        + [up_spec, up_spec, pl.BlockSpec((units, down_tile), down_index)],
-        out_specs=(
-            pl.BlockSpec((rows // 2, down_tile), down_index),
-            pl.BlockSpec((rows // 2, down_tile), down_index),
-        ),
+        functools.partial(up_kernel, len(blocks)),
+        out_shape=jax.ShapeDtypeStruct((rows, units), BF16),
+        in_specs=[pl.BlockSpec(memory_space=pl.ANY)] * (len(blocks) + 2),
+        out_specs=pl.BlockSpec(memory_space=pltpu.VMEM),
         scratch_shapes=[
             pltpu.VMEM((rows, width), BF16),
-            pltpu.VMEM((rows, units), BF16),
-            pltpu.SemaphoreType.DMA((count,)),
+            pltpu.VMEM((buffers, 2, width, tile), BF16),
+            pltpu.SemaphoreType.DMA((len(blocks),)),
+            pltpu.SemaphoreType.DMA((buffers, 2)),
         ],
         cost_estimate=pl.CostEstimate(
-            flops=6 * rows * width * units,
-            bytes_accessed=6 * width * units + 5 * rows * width,
+            flops=4 * rows * width * units,
+            bytes_accessed=4 * width * units + 2 * rows * width,
             transcendentals=rows * units,
         ),
-        compiler_params=pltpu.CompilerParams(vmem_limit_bytes=VMEM_LIMIT),
-        name="expert",
-    )(*blocks, gate_matrix, up_matrix, down_matrix)
+        compiler_params=pltpu.CompilerParams(vmem_limit_bytes=EXPERT_VMEM),
+        name="up",
+    )(*blocks, gate_matrix, up_matrix)
+
+
+def down_kernel(out_count, hidden_ref, down_ref, *refs):
+    out_refs, (held_ref, held_sems) = refs[:out_count], refs[out_count:]
+    buffers, _, tile = held_ref.shape
+    size = hidden_ref.shape[0] // out_count
+    fetches = []
+    for j in range(down_ref.shape[1] // tile):
+        part, slot = pl.ds(j * tile, tile), j % buffers
+        fetches.append(
+            [pltpu.make_async_copy(down_ref.at[:, part], held_ref.at[slot], held_sems.at[slot])]
+        )
+    arrive = staged(fetches, 2)
+    for j in range(len(fetches)):
+        arrive(j)
+        part = slice(j * tile, (j + 1) * tile)
+        out = jnp.dot(hidden_ref[...], held_ref[j % buffers], preferred_element_type=F32)
+        for i, out_ref in enumerate(out_refs):
+            out_ref[:, part] = out[i * size : (i + 1) * size].astype(out_ref.dtype)
+
+
+def down_projection(hidden, count, down_matrix):
+    rows, (units, width) = hidden.shape[0], down_matrix.shape
+    buffers, tile = 3, width // 4
+    vmem = pl.BlockSpec(memory_space=pltpu.VMEM)
+    out = pl.pallas_call(
+        functools.partial(down_kernel, count),
+        out_shape=tuple(
+            jax.ShapeDtypeStruct((rows // count, width), F32 if i < count // 2 else BF16)
+            for i in range(count)
+        ),
+        in_specs=[vmem, pl.BlockSpec(memory_space=pl.ANY)],
+        out_specs=(vmem,) * count,
+        scratch_shapes=[
+            pltpu.VMEM((buffers, units, tile), BF16),
+            pltpu.SemaphoreType.DMA((buffers,)),
+        ],
+        cost_estimate=pl.CostEstimate(
+            flops=2 * rows * width * units,
+            bytes_accessed=2 * width * units + 3 * rows * width,
+            transcendentals=0,
+        ),
+        compiler_params=pltpu.CompilerParams(vmem_limit_bytes=EXPERT_VMEM),
+        name="down",
+    )(hidden, down_matrix)
+    return out[: count // 2], out[count // 2 :]
 
 
 def combine_kernel(rows, slots, count, chunks, *refs):
@@ -188,29 +235,93 @@
     )(me, own, ids, gates, *taken)
 
 
-def gather_blocks(own, bits):
-    held = {0: own}
-    if len(bits) == 2:
-        a, b = bits
-        half = own.shape[0] // 2
-        held[a], held[b] = exchange(own, "dp", a), exchange(own, "dp", b)
-        low, high = exchange(held[b][:half], "dp", a), exchange(held[a][half:], "dp", b)
-        return held, (low, high)
-    for bit in bits:
-        held.update({k | bit: exchange(v, "dp", bit) for k, v in list(held.items())})
-    return held, None
-
-
-def reduce_lane(terms, bits):
-    terms = dict(terms)
-    for bit in bits:
-        leaving = sorted(k for k in terms if k & bit)
-        outgoing = jnp.stack([sum(t.astype(F32) for t in terms[k]).astype(BF16) for k in leaving])
-        incoming = exchange(outgoing, "dp", bit)
-        for i, k in enumerate(leaving):
-            terms[k ^ bit] = terms[k ^ bit] + [incoming[i]]
-            del terms[k]
-    return sum(t.astype(F32) for t in terms[0])
+def together(*groups):
+    flat = lax.optimization_barrier([a for g in groups for a in g])
+    return [[flat.pop(0) for _ in g] for g in groups]
+
+
+def after(array, *earlier):
+    return lax.optimization_barrier((array, *earlier))[0]
+
+
+class Chunk:
+    def __init__(self, pieces, bits):
+        self.own, self.bits = pieces, bits
+
+    def spread(self):
+        self.held = {0: self.own}
+        if len(self.bits) == 2:
+            for bit in self.bits:
+                self.held[bit] = [exchange(p, "dp", bit) for p in self.own]
+        else:
+            for bit in self.bits:
+                for k, v in list(self.held.items()):
+                    self.held[k | bit] = [exchange(p, "dp", bit) for p in v]
+
+    def forward(self):
+        if len(self.bits) == 2:
+            a, b = self.bits
+            last = []
+            for i, (source, bit) in enumerate(((b, a), (a, b))):
+                pieces = self.held[source]
+                if len(pieces) == 1:
+                    half = pieces[0].shape[0] // 2
+                    pieces = [pieces[0][:half], pieces[0][half:]]
+                last.append(exchange(pieces[i], "dp", bit))
+            self.held[a | b] = last
+
+    def up(self, matrices, *earlier):
+        self.order = sorted(self.held)
+        blocks = [p for k in self.order for p in self.held[k]]
+        blocks = blocks + [exchange(block, "dp", 1) for block in blocks]
+        if earlier:
+            blocks[0] = after(blocks[0], *earlier)
+        self.hidden = up_projection(blocks, *matrices[:2])
+
+    def down(self, matrices):
+        self.kept, self.sent = down_projection(self.hidden, 2 * len(self.order), matrices[2])
+
+    def pair_sum(self):
+        partner = [exchange(sent, "dp", 1) for sent in self.sent]
+        width = self.own[0].shape[1]
+        self.lanes = []
+        for lane, bits in enumerate((self.bits, self.bits[::-1])):
+            columns = slice(lane * width // 2, (lane + 1) * width // 2)
+            terms = {
+                k: [kept[:, columns], other[:, columns]]
+                for k, kept, other in zip(self.order, self.kept, partner)
+            }
+            self.lanes.append((terms, bits))
+
+    def leave(self, step):
+        self.outgoing = []
+        for terms, bits in self.lanes:
+            leaving = sorted(k for k in terms if k & bits[step])
+            self.outgoing.append(
+                jnp.stack([sum(t.astype(F32) for t in terms[k]).astype(BF16) for k in leaving])
+            )
+        return self.outgoing
+
+    def send(self, step):
+        self.incoming = [
+            exchange(out, "dp", bits[step]) for out, (_, bits) in zip(self.outgoing, self.lanes)
+        ]
+
+    def arrive(self, step):
+        for incoming, (terms, bits) in zip(self.incoming, self.lanes):
+            for i, k in enumerate(sorted(k for k in terms if k & bits[step])):
+                terms[k ^ bits[step]] = terms[k ^ bits[step]] + [incoming[i]]
+                del terms[k]
+
+    def finish(self):
+        sums = [sum(t.astype(F32) for t in terms[0]) for terms, _ in self.lanes]
+        total = jnp.concatenate(sums, axis=1).astype(BF16)
+        count, segment = lax.axis_size("segment"), lax.axis_index("segment")
+        width = total.shape[1] // count
+        parts = [
+            lax.dynamic_slice_in_dim(total, (segment ^ k) * width, width, 1) for k in range(count)
+        ]
+        return [parts[0]] + [exchange(parts[k], "segment", k) for k in range(1, count)]
 
 
 def per_device(tokens, norm_gain, router_weight, expert_ids, w_gate, w_up, w_down):
@@ -224,37 +335,53 @@
     while 2 ** (len(bits) + 1) < lax.axis_size("dp"):
         bits.append(2 ** (len(bits) + 1))
     slice_width = width // segment_count
-    chunks = chunk_rows(micro_count * slots)
+    sizes = chunk_rows(micro_count * slots)
     flat = tokens.reshape(-1, width)
     ids = expert_ids.reshape(-1, 2)
     own_part = lax.dynamic_slice_in_dim(flat, segment * slice_width, slice_width, 1)
-    routed, gates = route(me, flat, norm_gain, router_weight, ids, rows, slots, chunks)
-    taken = []
-    for own in routed:
-        size = own.shape[0]
-        held, halves = gather_blocks(own, bits)
-        if halves is not None:
-            held[bits[0] | bits[1]] = jnp.concatenate(halves)
-        order = sorted(held)
-        blocks = [held[k] for k in order]
-        blocks = blocks + [exchange(b, "dp", 1) for b in blocks]
-        kept, sent = expert(blocks, w_gate[0], w_up[0], w_down[0])
-        partner = exchange(sent, "dp", 1)
-        lanes = []
-        for lane, lane_bits in enumerate((bits, bits[::-1])):
-            columns = slice(lane * width // 2, (lane + 1) * width // 2)
-            terms = {
-                k: [a[i * size : (i + 1) * size, columns] for a in (kept, partner)]
-                for i, k in enumerate(order)
-            }
-            lanes.append(reduce_lane(terms, lane_bits))
-        total = jnp.concatenate(lanes, axis=1).astype(BF16)
-        for k in range(segment_count):
-            part = lax.dynamic_slice_in_dim(
-                total, (segment ^ k) * slice_width, slice_width, 1
-            )
-            taken.append(part if k == 0 else exchange(part, "segment", k))
-    out = combine(me, own_part, ids, gates, taken, rows, slots, chunks)
+    routed, gates = route(me, flat, norm_gain, router_weight, ids, rows, slots, sizes)
+    matrices = w_gate[0], w_up[0], w_down[0]
+    one, two = Chunk(routed[:2], bits), Chunk(routed[2:], bits)
+    one.spread()
+    two.own = [after(p, *(p for b in bits for p in one.held[b])) for p in two.own]
+    two.spread()
+    one.forward()
+    one.up(matrices)
+    hops = [b for b in sorted(two.held) if b]
+    (one.hidden,), *arrived = together([one.hidden], *(two.held[b] for b in hops))
+    two.held.update(zip(hops, arrived))
+    two.forward()
+    one.down(matrices)
+    last = max(two.held)
+    one.kept, one.sent, two.held[last] = together(one.kept, one.sent, two.held[last])
+    one.pair_sum()
+    steps = len(bits)
+    one.leave(0)
+    one.send(0)
+    two.up(matrices, *one.outgoing)
+    (two.hidden,), one.incoming = together([two.hidden], one.incoming)
+    one.arrive(0)
+    for step in range(1, steps):
+        one.leave(step)
+        one.send(step)
+        if step < steps - 1:
+            one.arrive(step)
+    two.down(matrices)
+    two.kept, two.sent, one.incoming = together(two.kept, two.sent, one.incoming)
+    one.arrive(steps - 1)
+    two.pair_sum()
+    two.leave(0)
+    two.send(0)
+    taken = one.finish()
+    taken[1:], two.incoming = together(taken[1:], two.incoming)
+    two.arrive(0)
+    for step in range(1, steps):
+        two.leave(step)
+        two.send(step)
+        two.arrive(step)
+    taken = taken + two.finish()
+    wholes = sum(sizes[:2]), sizes[2]
+    out = combine(me, own_part, ids, gates, taken, rows, slots, wholes)
     return out.reshape(micro_count, rows, slice_width)
 
 

time: 192 us -> 143 us (0.74)
  waiting for transfers between devices: 79.2 us -> 42.9 us
  Pallas kernels: 59.4 us -> 50.4 us
  other arithmetic: 12.3 us -> 5.52 us
  local copies, waits for them, and re-layouts: 6.04 us -> 8.92 us
    ppermute x32 -> x45, waiting for transfers between devices: 79.2 us -> 42.9 us  [exchange(): return lax.ppermute(array, axis, [(i, i ^ distance) for i in range(count)])]
    pallas_call x2 -> x4, Pallas kernels: 51.4 us -> 45.8 us  [the longest x2 30.2 us: up_projection(): pl.pallas_call(functools.partial(up_kernel, len(blocks)), out_shape=jax.S...]
    another operation x12 -> x16, other arithmetic: 10.2 us -> 4.71 us  [the longest x14 3.15 us: leave(): jnp.stack([sum((t.astype(F32) for t in terms[k])).astype(BF16) for k in l...]
    unnamed x41 -> x31, local copies, waits for them, and re-layouts: 2.25 us -> 7.07 us
    ppermute x32 -> x45, starting transfers between devices: 33.8 us -> 34.6 us  [exchange(): return lax.ppermute(array, axis, [(i, i ^ distance) for i in range(count)])]
  transfers between devices with their start and end apart: 32 -> 45, of which waited for: 13 -> 14; matrix products, arithmetic and copies ran while one was open for 7% -> 4% of each run, Pallas kernels for 27% -> 32%
where the time goes in v2:
time: 143 us
  Pallas kernels  50.4 us (35%)
  waiting for transfers between devices  42.9 us (30%)
  starting transfers between devices  34.6 us (24%)
  local copies, waits for them, and re-layouts  8.92 us (6%)
  other arithmetic  5.52 us (4%)
    ppermute x45, waiting for transfers between devices, exchange(): return lax.ppermute(array, axis, [(i, i ^ distance) for i in range(count)])  42.9 us
    ppermute x45, starting transfers between devices, exchange(): return lax.ppermute(array, axis, [(i, i ^ distance) for i in range(count)])  34.6 us
    pallas_call x2, Pallas kernels, up_projection(): pl.pallas_call(functools.partial(up_kernel, len(blocks)), out_shape=jax.S...  30.2 us
    pallas_call x2, Pallas kernels, down_projection(): pl.pallas_call(functools.partial(down_kernel, count), out_shape=tuple((ja...  15.5 us
    unnamed x31, local copies, waits for them, and re-layouts  7.07 us
    another operation x14, other arithmetic, leave(): jnp.stack([sum((t.astype(F32) for t in terms[k])).astype(BF16) for k in l...  3.15 us
    pallas_call x1, Pallas kernels, combine(): pl.pallas_call(functools.partial(combine_kernel, rows, slots, count, chun...  2.92 us
  transfers between devices with their start and end apart: 45, of which 14 were waited for; matrix products, arithmetic and copies ran while one was open for 4% of the time, Pallas kernels for 32%

profile of v2, /device:TPU:0, one launch (start us, length us, event | category | flops | bytes accessed | tf_op | source)
XLA Modules:
  0.0 142.7 jit_solution(17438582637864550717)
XLA Ops:
  1.6 1.4 copy-done
  3.8 1.7 %route.1 = (bf16[32,6144]{1,0:T(8,128)(2,1)S(1)}, bf16[16,6144]{1,0:T(8,128)(2,1)S(1)}, bf16[32,6144]{1,0:T(8,128)(2,1)S(1)}, f32[128,2]{1,0:T(8,128)S(1)}) custom-call(s32[1]{0:T(128)} %bitcast.refs_0_, bf16[128,6144]{1,0:T(8,128)(2,1)S(1)} %bitcast.71, bf16[1,6144]{1,0:T(2,128)(2,1)S(1)} %reshape.42.refs_2_, bf16[4,6144]{1,0:T(4,128)(2,1)S(1)} %bitcast.75, ...), custom_call_target="tpu_custom_call" | custom-call | tf_op jit(solution)/shard_map/route/pallas_call | solution.py:66
  5.5 3.0 %collective-permute-start.2 = (bf16[32,6144]{1,0:T(8,128)(2,1)S(1)}, bf16[32,6144]{1,0:T(8,128)(2,1)S(1)}, u32[]{:S(2)}, u32[]{:S(2)}) collective-permute-start(bf16[32,6144]{1,0:T(8,128)(2,1)S(1)} %get-tuple-element.59.refs_0_), channel_id=1, source_target_pairs={{0,4},{1,5},{2,6},{3,7},{4,0},{5,1},{6,2},{7,3},{8,12},{9,13},{10,... | collective-permute-start | bytes 1179656 | tf_op jit(solution)/shard_map/ppermute | solution.py:19
  8.6 1.5 %collective-permute-start.1 = (bf16[16,6144]{1,0:T(8,128)(2,1)S(1)}, bf16[16,6144]{1,0:T(8,128)(2,1)S(1)}, u32[]{:S(2)}, u32[]{:S(2)}) collective-permute-start(bf16[16,6144]{1,0:T(8,128)(2,1)S(1)} %get-tuple-element.60.refs_1_), channel_id=1, source_target_pairs={{0,2},{1,3},{2,0},{3,1},{4,6},{5,7},{6,4},{7,5},{8,10},{9,11},{10,... | collective-permute-start | bytes 589832 | tf_op jit(solution)/shard_map/ppermute | solution.py:19
  10.7 7.8 %collective-permute-done.2.refs_4_ = bf16[32,6144]{1,0:T(8,128)(2,1)S(1)} collective-permute-done((bf16[32,6144]{1,0:T(8,128)(2,1)S(1)}, bf16[32,6144]{1,0:T(8,128)(2,1)S(1)}, u32[]{:S(2)}, u32[]{:S(2)}) %collective-permute-start.2) | collective-permute-done | bytes 393248 | tf_op jit(solution)/shard_map/ppermute | solution.py:19
  18.5 2.0 %collective-permute-start.4 = (bf16[32,6144]{1,0:T(8,128)(2,1)S(1)}, bf16[32,6144]{1,0:T(8,128)(2,1)S(1)}, u32[]{:S(2)}, u32[]{:S(2)}) collective-permute-start(bf16[32,6144]{1,0:T(8,128)(2,1)S(1)} %collective-permute-done.2.refs_4_), channel_id=1, source_target_pairs={{0,2},{1,3},{2,0},{3,1},{4,6},{5,7},{6,4},{7,5},{8,10},{9,11},{10,... | collective-permute-start | bytes 1179656 | tf_op jit(solution)/shard_map/ppermute | solution.py:19
  20.5 1.5 %collective-permute-start.5 = (bf16[16,6144]{1,0:T(8,128)(2,1)S(1)}, bf16[16,6144]{1,0:T(8,128)(2,1)S(1)}, u32[]{:S(2)}, u32[]{:S(2)}) collective-permute-start(bf16[16,6144]{1,0:T(8,128)(2,1)S(1)} %collective-permute-done.1.refs_3_), channel_id=1, source_target_pairs={{0,4},{1,5},{2,6},{3,7},{4,0},{5,1},{6,2},{7,3},{8,12},{9,13},{10,... | collective-permute-start | bytes 589832 | tf_op jit(solution)/shard_map/ppermute | solution.py:19
  22.6 5.3 %collective-permute-done.5.refs_7_ = bf16[16,6144]{1,0:T(8,128)(2,1)S(1)} collective-permute-done((bf16[16,6144]{1,0:T(8,128)(2,1)S(1)}, bf16[16,6144]{1,0:T(8,128)(2,1)S(1)}, u32[]{:S(2)}, u32[]{:S(2)}) %collective-permute-start.5) | collective-permute-done | bytes 196640 | tf_op jit(solution)/shard_map/ppermute | solution.py:19
  28.4 3.3 %collective-permute-done.4.refs_6_ = bf16[32,6144]{1,0:T(8,128)(2,1)S(1)} collective-permute-done((bf16[32,6144]{1,0:T(8,128)(2,1)S(1)}, bf16[32,6144]{1,0:T(8,128)(2,1)S(1)}, u32[]{:S(2)}, u32[]{:S(2)}) %collective-permute-start.4) | collective-permute-done | bytes 393248 | tf_op jit(solution)/shard_map/ppermute | solution.py:19
  32.3 1.5 %collective-permute-start.14 = (bf16[32,6144]{1,0:T(8,128)(2,1)S(1)}, bf16[32,6144]{1,0:T(8,128)(2,1)S(1)}, u32[]{:S(2)}, u32[]{:S(2)}) collective-permute-start(bf16[32,6144]{1,0:T(8,128)(2,1)S(1)} %get-tuple-element.82.refs_0_), channel_id=1, source_target_pairs={{0,2},{1,3},{2,0},{3,1},{4,6},{5,7},{6,4},{7,5},{8,10},{9,11},{10,... | collective-permute-start | bytes 1179656 | tf_op jit(solution)/shard_map/ppermute | solution.py:19
  34.3 17.3 %up.2.hidden_ref = bf16[384,1024]{1,0:T(8,128)(2,1)S(1)} custom-call(bf16[32,6144]{1,0:T(8,128)(2,1)S(1)} %get-tuple-element.59.refs_0_, bf16[16,6144]{1,0:T(8,128)(2,1)S(1)} %get-tuple-element.60.refs_1_, bf16[32,6144]{1,0:T(8,128)(2,1)S(1)} %collective-permute-done.refs_2_, bf16[16,6144]{1,0:T(8,128)(2,1)S(1)} %collective-permute-done.1.refs_3_, ...), custom_call_target="tpu_custom_call" | custom-call | flops 9663676416 | bytes 29884416 | tf_op jit(solution)/shard_map/up/pallas_call | solution.py:125
  51.7 1.5 %collective-permute-start.16 = (bf16[16,6144]{1,0:T(8,128)(2,1)S(1)}, bf16[16,6144]{1,0:T(8,128)(2,1)S(1)}, u32[]{:S(2)}, u32[]{:S(2)}) collective-permute-start(bf16[16,6144]{1,0:T(8,128)(2,1)S(1)} %slice.126), channel_id=1, source_target_pairs={{0,2},{1,3},{2,0},{3,1},{4,6},{5,7},{6,4},{7,5},{8,10},{9,11},{10,... | collective-permute-start | bytes 589832 | tf_op jit(solution)/shard_map/ppermute | solution.py:19
  53.3 1.6 %collective-permute-start.17 = (bf16[16,6144]{1,0:T(8,128)(2,1)S(1)}, bf16[16,6144]{1,0:T(8,128)(2,1)S(1)}, u32[]{:S(2)}, u32[]{:S(2)}) collective-permute-start(bf16[16,6144]{1,0:T(8,128)(2,1)S(1)} %slice.127), channel_id=1, source_target_pairs={{0,4},{1,5},{2,6},{3,7},{4,0},{5,1},{6,2},{7,3},{8,12},{9,13},{10,... | collective-permute-start | bytes 589832 | tf_op jit(solution)/shard_map/ppermute | solution.py:19
  54.9 8.8 %down.2 = (f32[48,6144]{1,0:T(8,128)S(1)}, f32[48,6144]{1,0:T(8,128)S(1)}, f32[48,6144]{1,0:T(8,128)}, f32[48,6144]{1,0:T(8,128)}, bf16[48,6144]{1,0:T(8,128)(2,...) custom-call(bf16[384,1024]{1,0:T(8,128)(2,1)S(1)} %up.2.hidden_ref, ...), custom_call_target="tpu_custom_call" | custom-call | flops 4831838208 | bytes 19660800 | tf_op jit(solution)/shard_map/down/pallas_call | solution.py:169
  65.9 1.4 fusion.11
  70.6 12.9 %up.3.hidden_ref = bf16[256,1024]{1,0:T(8,128)(2,1)S(1)} custom-call(bf16[32,6144]{1,0:T(8,128)(2,1)S(1)} %get-tuple-element.82.refs_0_, bf16[32,6144]{1,0:T(8,128)(2,1)S(1)} %collective-permute-done.14.refs_1_, bf16[32,6144]{1,0:T(8,128)(2,1)S(1)} %collective-permute-done.15.refs_2_, bf16[16,6144]{1,0:T(8,128)(2,1)S(1)} %collective-permute-done.16.refs_3_, ...), custom_call_target="tpu_custom_call" | custom-call | flops 6442450944 | bytes 28311552 | tf_op jit(solution)/shard_map/up/pallas_call | solution.py:125
  83.5 1.7 %collective-permute-done.28 = bf16[2,48,3072]{2,1,0:T(8,128)(2,1)S(1)} collective-permute-done((bf16[2,48,3072]{2,1,0:T(8,128)(2,1)S(1)}, bf16[2,48,3072]{2,1,0:T(8,128)(2,1)S(1)}, u32[]{:S(2)}, u32[]{:S(2)}) %collective-permute-start.28) | collective-permute-done | bytes 589856 | tf_op jit(solution)/shard_map/ppermute | solution.py:19
  86.2 1.6 %collective-permute-start.29 = (bf16[1,48,3072]{2,1,0:T(8,128)(2,1)S(1)}, bf16[1,48,3072]{2,1,0:T(8,128)(2,1)}, u32[]{:S(2)}, u32[]{:S(2)}) collective-permute-start(bf16[1,48,3072]{2,1,0:T(8,128)(2,1)S(1)} %fusion.12), channel_id=1, source_target_pairs={{0,4},{1,5},{2,6},{3,7},{4,0},{5,1},{6,2},{7,3},{8,12},{9,13},{10,... | collective-permute-start | bytes 884744 | tf_op jit(solution)/shard_map/ppermute | solution.py:19
  87.8 6.7 %down.3 = (f32[32,6144]{1,0:T(8,128)S(1)}, f32[32,6144]{1,0:T(8,128)S(1)}, f32[32,6144]{1,0:T(8,128)S(1)}, f32[32,6144]{1,0:T(8,128)S(1)}, bf16[32,6144]{1,0:T(8...) custom-call(bf16[256,1024]{1,0:T(8,128)(2,1)S(1)} %up.3.hidden_ref, ...), custom_call_target="tpu_custom_call" | custom-call | flops 3221225472 | bytes 17301504 | tf_op jit(solution)/shard_map/down/pallas_call | solution.py:169
  102.6 1.5 %collective-permute-start.36 = (bf16[2,32,3072]{2,1,0:T(8,128)(2,1)S(1)}, bf16[2,32,3072]{2,1,0:T(8,128)(2,1)S(1)}, u32[]{:S(2)}, u32[]{:S(2)}) collective-permute-start(bf16[2,32,3072]{2,1,0:T(8,128)(2,1)S(1)} %pad_maximum_fusion.2), channel_id=1, source_target_pairs={{0,2},{1,3},{2,0},{3,1},{4,6},{5,7},{6,4},{7,5},{8,10},{9,11},{10,... | collective-permute-start | bytes 1179656 | tf_op jit(solution)/shard_map/ppermute | solution.py:19
  104.2 1.4 fusion
  106.0 1.6 %collective-permute-start.31 = (bf16[48,1536]{1,0:T(8,128)(2,1)S(1)}, bf16[48,1536]{1,0:T(8,128)(2,1)S(1)}, u32[]{:S(2)}, u32[]{:S(2)}) collective-permute-start(bf16[48,1536]{1,0:T(8,128)(2,1)S(1)} %get-tuple-element.121), channel_id=1, source_target_pairs={{0,8},{8,0},{16,24},{24,16},{1,9},{9,1},{17,25},{25,17},{2,10},{10... | collective-permute-start | bytes 442376 | tf_op jit(solution)/shard_map/ppermute | solution.py:19
  107.6 2.6 %collective-permute-start.32 = (bf16[48,1536]{1,0:T(8,128)(2,1)S(1)}, bf16[48,1536]{1,0:T(8,128)(2,1)S(1)}, u32[]{:S(2)}, u32[]{:S(2)}) collective-permute-start(bf16[48,1536]{1,0:T(8,128)(2,1)S(1)} %get-tuple-element.122), channel_id=1, source_target_pairs={{0,16},{8,24},{16,0},{24,8},{1,17},{9,25},{17,1},{25,9},{2,18},{10... | collective-permute-start | bytes 442376 | tf_op jit(solution)/shard_map/ppermute | solution.py:19
  110.4 3.3 %collective-permute-done.31.refs_5_ = bf16[48,1536]{1,0:T(8,128)(2,1)S(1)} collective-permute-done((bf16[48,1536]{1,0:T(8,128)(2,1)S(1)}, bf16[48,1536]{1,0:T(8,128)(2,1)S(1)}, u32[]{:S(2)}, u32[]{:S(2)}) %collective-permute-start.31) | collective-permute-done | bytes 147488 | tf_op jit(solution)/shard_map/ppermute | solution.py:19
  113.7 7.9 %collective-permute-done.32.refs_6_ = bf16[48,1536]{1,0:T(8,128)(2,1)S(1)} collective-permute-done((bf16[48,1536]{1,0:T(8,128)(2,1)S(1)}, bf16[48,1536]{1,0:T(8,128)(2,1)S(1)}, u32[]{:S(2)}, u32[]{:S(2)}) %collective-permute-start.32) | collective-permute-done | bytes 147488 | tf_op jit(solution)/shard_map/ppermute | solution.py:19
  121.7 1.5 %collective-permute-start.40 = (bf16[1,32,3072]{2,1,0:T(8,128)(2,1)S(1)}, bf16[1,32,3072]{2,1,0:T(8,128)(2,1)S(1)}, u32[]{:S(2)}, u32[]{:S(2)}) collective-permute-start(bf16[1,32,3072]{2,1,0:T(8,128)(2,1)S(1)} %fusion.18), channel_id=1, source_target_pairs={{0,4},{1,5},{2,6},{3,7},{4,0},{5,1},{6,2},{7,3},{8,12},{9,13},{10,... | collective-permute-start | bytes 589832 | tf_op jit(solution)/shard_map/ppermute | solution.py:19
  123.8 3.6 %collective-permute-done.40 = bf16[1,32,3072]{2,1,0:T(8,128)(2,1)S(1)} collective-permute-done((bf16[1,32,3072]{2,1,0:T(8,128)(2,1)S(1)}, bf16[1,32,3072]{2,1,0:T(8,128)(2,1)S(1)}, u32[]{:S(2)}, u32[]{:S(2)}) %collective-permute-start.40) | collective-permute-done | bytes 196640 | tf_op jit(solution)/shard_map/ppermute | solution.py:19
  127.4 1.6 %collective-permute-done.41 = bf16[1,32,3072]{2,1,0:T(8,128)(2,1)S(1)} collective-permute-done((bf16[1,32,3072]{2,1,0:T(8,128)(2,1)S(1)}, bf16[1,32,3072]{2,1,0:T(8,128)(2,1)S(1)}, u32[]{:S(2)}, u32[]{:S(2)}) %collective-permute-start.41) | collective-permute-done | bytes 196640 | tf_op jit(solution)/shard_map/ppermute | solution.py:19
  129.6 2.2 %collective-permute-start.42 = (bf16[32,1536]{1,0:T(8,128)(2,1)S(1)}, bf16[32,1536]{1,0:T(8,128)(2,1)S(1)}, u32[]{:S(2)}, u32[]{:S(2)}) collective-permute-start(bf16[32,1536]{1,0:T(8,128)(2,1)S(1)} %get-tuple-element.125), channel_id=1, source_target_pairs={{0,8},{8,0},{16,24},{24,16},{1,9},{9,1},{17,25},{25,17},{2,10},{10... | collective-permute-start | bytes 294920 | tf_op jit(solution)/shard_map/ppermute | solution.py:19
  132.9 1.4 collective-permute-start.44
  135.3 4.5 %collective-permute-done.43.refs_10_ = bf16[32,1536]{1,0:T(8,128)(2,1)S(1)} collective-permute-done((bf16[32,1536]{1,0:T(8,128)(2,1)S(1)}, bf16[32,1536]{1,0:T(8,128)(2,1)S(1)}, u32[]{:S(2)}, u32[]{:S(2)}) %collective-permute-start.43) | collective-permute-done | bytes 98336 | tf_op jit(solution)/shard_map/ppermute | solution.py:19
  139.8 2.9 %combine.1 = bf16[128,1536]{1,0:T(8,128)(2,1)} custom-call(s32[1]{0:T(128)} %bitcast.refs_0_, bf16[128,1536]{1,0:T(8,128)(2,1)S(1)} %constant_dynamic-slice_fusion.refs_1_, s32[128,2]{1,0:T(8,128)S(1)} %bitcast.74, f32[128,2]{1,0:T(8,128)S(1)} %get-tuple-element.58.refs_3_, bf16[48,1536]{1,0:T(8,128)(2,1)S(1)} %get-tuple-element.120.refs_4_, ...), custom_call_target="tpu_custom_call" | custom-call | tf_op jit(solution)/shard_map/combine/pallas_call | solution.py:228
  (118 shorter events, 23.8 us)
Async XLA Ops:
  5.5 13.0 %collective-permute-start.2 = (bf16[32,6144]{1,0:T(8,128)(2,1)S(1)}, bf16[32,6144]{1,0:T(8,128)(2,1)S(1)}, u32[]{:S(2)}, u32[]{:S(2)}) collective-permute-start(bf16[32,6144]{1,0:T(8,128)(2,1)S(1)} %get-tuple-element.59.refs_0_), channel_id=1, source_target_pairs={{0,4},{1,5},{2,6},{3,7},{4,0},{5,1},{6,2},{7,3},{8,12},{9,13},{10,... | collective-permute-start | bytes 1179656 | tf_op jit(solution)/shard_map/ppermute | solution.py:19
  8.6 12.0 %collective-permute-start.1 = (bf16[16,6144]{1,0:T(8,128)(2,1)S(1)}, bf16[16,6144]{1,0:T(8,128)(2,1)S(1)}, u32[]{:S(2)}, u32[]{:S(2)}) collective-permute-start(bf16[16,6144]{1,0:T(8,128)(2,1)S(1)} %get-tuple-element.60.refs_1_), channel_id=1, source_target_pairs={{0,2},{1,3},{2,0},{3,1},{4,6},{5,7},{6,4},{7,5},{8,10},{9,11},{10,... | collective-permute-start | bytes 589832 | tf_op jit(solution)/shard_map/ppermute | solution.py:19
  10.1 12.0 %collective-permute-start.3 = (bf16[16,6144]{1,0:T(8,128)(2,1)S(1)}, bf16[16,6144]{1,0:T(8,128)(2,1)S(1)}, u32[]{:S(2)}, u32[]{:S(2)}) collective-permute-start(bf16[16,6144]{1,0:T(8,128)(2,1)S(1)} %get-tuple-element.60.refs_1_), channel_id=1, source_target_pairs={{0,4},{1,5},{2,6},{3,7},{4,0},{5,1},{6,2},{7,3},{8,12},{9,13},{10,... | collective-permute-start | bytes 589832 | tf_op jit(solution)/shard_map/ppermute | solution.py:19
  10.6 17.8 %collective-permute-start = (bf16[32,6144]{1,0:T(8,128)(2,1)S(1)}, bf16[32,6144]{1,0:T(8,128)(2,1)S(1)}, u32[]{:S(2)}, u32[]{:S(2)}) collective-permute-start(bf16[32,6144]{1,0:T(8,128)(2,1)S(1)} %get-tuple-element.59.refs_0_), channel_id=1, source_target_pairs={{0,2},{1,3},{2,0},{3,1},{4,6},{5,7},{6,4},{7,5},{8,10},{9,11},{10,... | collective-permute-start | bytes 1179656 | tf_op jit(solution)/shard_map/ppermute | solution.py:19
  18.5 13.3 %collective-permute-start.4 = (bf16[32,6144]{1,0:T(8,128)(2,1)S(1)}, bf16[32,6144]{1,0:T(8,128)(2,1)S(1)}, u32[]{:S(2)}, u32[]{:S(2)}) collective-permute-start(bf16[32,6144]{1,0:T(8,128)(2,1)S(1)} %collective-permute-done.2.refs_4_), channel_id=1, source_target_pairs={{0,2},{1,3},{2,0},{3,1},{4,6},{5,7},{6,4},{7,5},{8,10},{9,11},{10,... | collective-permute-start | bytes 1179656 | tf_op jit(solution)/shard_map/ppermute | solution.py:19
  20.5 7.3 %collective-permute-start.5 = (bf16[16,6144]{1,0:T(8,128)(2,1)S(1)}, bf16[16,6144]{1,0:T(8,128)(2,1)S(1)}, u32[]{:S(2)}, u32[]{:S(2)}) collective-permute-start(bf16[16,6144]{1,0:T(8,128)(2,1)S(1)} %collective-permute-done.1.refs_3_), channel_id=1, source_target_pairs={{0,4},{1,5},{2,6},{3,7},{4,0},{5,1},{6,2},{7,3},{8,12},{9,13},{10,... | collective-permute-start | bytes 589832 | tf_op jit(solution)/shard_map/ppermute | solution.py:19
  22.1 5.8 %collective-permute-start.9 = (bf16[16,6144]{1,0:T(8,128)(2,1)S(1)}, bf16[16,6144]{1,0:T(8,128)(2,1)S(1)}, u32[]{:S(2)}, u32[]{:S(2)}) collective-permute-start(bf16[16,6144]{1,0:T(8,128)(2,1)S(1)} %collective-permute-done.1.refs_3_), channel_id=1, source_target_pairs={{0,1},{1,0},{2,3},{3,2},{4,5},{5,4},{6,7},{7,6},{8,9},{9,8},{10,11... | collective-permute-start | bytes 589832 | tf_op jit(solution)/shard_map/ppermute | solution.py:19
  22.3 10.0 %collective-permute-start.6 = (bf16[32,6144]{1,0:T(8,128)(2,1)S(1)}, bf16[32,6144]{1,0:T(8,128)(2,1)S(1)}, u32[]{:S(2)}, u32[]{:S(2)}) collective-permute-start(bf16[32,6144]{1,0:T(8,128)(2,1)S(1)} %get-tuple-element.59.refs_0_), channel_id=1, source_target_pairs={{0,1},{1,0},{2,3},{3,2},{4,5},{5,4},{6,7},{7,6},{8,9},{9,8},{10,11... | collective-permute-start | bytes 1179656 | tf_op jit(solution)/shard_map/ppermute | solution.py:19
  27.9 6.4 %collective-permute-start.10 = (bf16[32,6144]{1,0:T(8,128)(2,1)S(1)}, bf16[32,6144]{1,0:T(8,128)(2,1)S(1)}, u32[]{:S(2)}, u32[]{:S(2)}) collective-permute-start(bf16[32,6144]{1,0:T(8,128)(2,1)S(1)} %collective-permute-done.2.refs_4_), channel_id=1, source_target_pairs={{0,1},{1,0},{2,3},{3,2},{4,5},{5,4},{6,7},{7,6},{8,9},{9,8},{10,11... | collective-permute-start | bytes 1179656 | tf_op jit(solution)/shard_map/ppermute | solution.py:19
  28.4 5.9 %collective-permute-start.8 = (bf16[32,6144]{1,0:T(8,128)(2,1)S(1)}, bf16[32,6144]{1,0:T(8,128)(2,1)S(1)}, u32[]{:S(2)}, u32[]{:S(2)}) collective-permute-start(bf16[32,6144]{1,0:T(8,128)(2,1)S(1)} %collective-permute-done.refs_2_), channel_id=1, source_target_pairs={{0,1},{1,0},{2,3},{3,2},{4,5},{5,4},{6,7},{7,6},{8,9},{9,8},{10,11... | collective-permute-start | bytes 1179656 | tf_op jit(solution)/shard_map/ppermute | solution.py:19
  32.3 19.4 %collective-permute-start.14 = (bf16[32,6144]{1,0:T(8,128)(2,1)S(1)}, bf16[32,6144]{1,0:T(8,128)(2,1)S(1)}, u32[]{:S(2)}, u32[]{:S(2)}) collective-permute-start(bf16[32,6144]{1,0:T(8,128)(2,1)S(1)} %get-tuple-element.82.refs_0_), channel_id=1, source_target_pairs={{0,2},{1,3},{2,0},{3,1},{4,6},{5,7},{6,4},{7,5},{8,10},{9,11},{10,... | collective-permute-start | bytes 1179656 | tf_op jit(solution)/shard_map/ppermute | solution.py:19
  33.8 17.9 %collective-permute-start.15 = (bf16[32,6144]{1,0:T(8,128)(2,1)S(1)}, bf16[32,6144]{1,0:T(8,128)(2,1)S(1)}, u32[]{:S(2)}, u32[]{:S(2)}) collective-permute-start(bf16[32,6144]{1,0:T(8,128)(2,1)S(1)} %get-tuple-element.82.refs_0_), channel_id=1, source_target_pairs={{0,4},{1,5},{2,6},{3,7},{4,0},{5,1},{6,2},{7,3},{8,12},{9,13},{10,... | collective-permute-start | bytes 1179656 | tf_op jit(solution)/shard_map/ppermute | solution.py:19
  51.7 12.0 %collective-permute-start.16 = (bf16[16,6144]{1,0:T(8,128)(2,1)S(1)}, bf16[16,6144]{1,0:T(8,128)(2,1)S(1)}, u32[]{:S(2)}, u32[]{:S(2)}) collective-permute-start(bf16[16,6144]{1,0:T(8,128)(2,1)S(1)} %slice.126), channel_id=1, source_target_pairs={{0,2},{1,3},{2,0},{3,1},{4,6},{5,7},{6,4},{7,5},{8,10},{9,11},{10,... | collective-permute-start | bytes 589832 | tf_op jit(solution)/shard_map/ppermute | solution.py:19
  53.3 10.4 %collective-permute-start.17 = (bf16[16,6144]{1,0:T(8,128)(2,1)S(1)}, bf16[16,6144]{1,0:T(8,128)(2,1)S(1)}, u32[]{:S(2)}, u32[]{:S(2)}) collective-permute-start(bf16[16,6144]{1,0:T(8,128)(2,1)S(1)} %slice.127), channel_id=1, source_target_pairs={{0,4},{1,5},{2,6},{3,7},{4,0},{5,1},{6,2},{7,3},{8,12},{9,13},{10,... | collective-permute-start | bytes 589832 | tf_op jit(solution)/shard_map/ppermute | solution.py:19
  63.8 5.7 %collective-permute-start.22 = (bf16[32,6144]{1,0:T(8,128)(2,1)S(1)}, bf16[32,6144]{1,0:T(8,128)(2,1)S(1)}, u32[]{:S(2)}, u32[]{:S(2)}) collective-permute-start(bf16[32,6144]{1,0:T(8,128)(2,1)S(1)} %get-tuple-element.82.refs_0_), channel_id=1, source_target_pairs={{0,1},{1,0},{2,3},{3,2},{4,5},{5,4},{6,7},{7,6},{8,9},{9,8},{10,11... | collective-permute-start | bytes 1179656 | tf_op jit(solution)/shard_map/ppermute | solution.py:19
  64.3 6.3 %collective-permute-start.23 = (bf16[32,6144]{1,0:T(8,128)(2,1)S(1)}, bf16[32,6144]{1,0:T(8,128)(2,1)S(1)}, u32[]{:S(2)}, u32[]{:S(2)}) collective-permute-start(bf16[32,6144]{1,0:T(8,128)(2,1)S(1)} %collective-permute-done.14.refs_1_), channel_id=1, source_target_pairs={{0,1},{1,0},{2,3},{3,2},{4,5},{5,4},{6,7},{7,6},{8,9},{9,8},{10,11... | collective-permute-start | bytes 1179656 | tf_op jit(solution)/shard_map/ppermute | solution.py:19
  64.4 6.3 %collective-permute-start.24 = (bf16[32,6144]{1,0:T(8,128)(2,1)S(1)}, bf16[32,6144]{1,0:T(8,128)(2,1)S(1)}, u32[]{:S(2)}, u32[]{:S(2)}) collective-permute-start(bf16[32,6144]{1,0:T(8,128)(2,1)S(1)} %collective-permute-done.15.refs_2_), channel_id=1, source_target_pairs={{0,1},{1,0},{2,3},{3,2},{4,5},{5,4},{6,7},{7,6},{8,9},{9,8},{10,11... | collective-permute-start | bytes 1179656 | tf_op jit(solution)/shard_map/ppermute | solution.py:19
  69.5 15.7 %collective-permute-start.28 = (bf16[2,48,3072]{2,1,0:T(8,128)(2,1)S(1)}, bf16[2,48,3072]{2,1,0:T(8,128)(2,1)S(1)}, u32[]{:S(2)}, u32[]{:S(2)}) collective-permute-start(bf16[2,48,3072]{2,1,0:T(8,128)(2,1)S(1)} %pad_maximum_fusion.1), channel_id=1, source_target_pairs={{0,4},{1,5},{2,6},{3,7},{4,0},{5,1},{6,2},{7,3},{8,12},{9,13},{10,... | collective-permute-start | bytes 1769480 | tf_op jit(solution)/shard_map/ppermute | solution.py:19
  70.1 15.3 %collective-permute-start.27 = (bf16[2,48,3072]{2,1,0:T(8,128)(2,1)S(1)}, bf16[2,48,3072]{2,1,0:T(8,128)(2,1)S(1)}, u32[]{:S(2)}, u32[]{:S(2)}) collective-permute-start(bf16[2,48,3072]{2,1,0:T(8,128)(2,1)S(1)} %pad_maximum_fusion), channel_id=1, source_target_pairs={{0,2},{1,3},{2,0},{3,1},{4,6},{5,7},{6,4},{7,5},{8,10},{9,11},{10,... | collective-permute-start | bytes 1769480 | tf_op jit(solution)/shard_map/ppermute | solution.py:19
  85.5 13.1 %collective-permute-start.30 = (bf16[1,48,3072]{2,1,0:T(8,128)(2,1)S(1)}, bf16[1,48,3072]{2,1,0:T(8,128)(2,1)}, u32[]{:S(2)}, u32[]{:S(2)}) collective-permute-start(bf16[1,48,3072]{2,1,0:T(8,128)(2,1)S(1)} %fusion.13), channel_id=1, source_target_pairs={{0,2},{1,3},{2,0},{3,1},{4,6},{5,7},{6,4},{7,5},{8,10},{9,11},{10,... | collective-permute-start | bytes 884744 | tf_op jit(solution)/shard_map/ppermute | solution.py:19
  86.2 12.4 %collective-permute-start.29 = (bf16[1,48,3072]{2,1,0:T(8,128)(2,1)S(1)}, bf16[1,48,3072]{2,1,0:T(8,128)(2,1)}, u32[]{:S(2)}, u32[]{:S(2)}) collective-permute-start(bf16[1,48,3072]{2,1,0:T(8,128)(2,1)S(1)} %fusion.12), channel_id=1, source_target_pairs={{0,4},{1,5},{2,6},{3,7},{4,0},{5,1},{6,2},{7,3},{8,12},{9,13},{10,... | collective-permute-start | bytes 884744 | tf_op jit(solution)/shard_map/ppermute | solution.py:19
  101.9 19.7 %collective-permute-start.38 = (bf16[2,32,3072]{2,1,0:T(8,128)(2,1)S(1)}, bf16[2,32,3072]{2,1,0:T(8,128)(2,1)S(1)}, u32[]{:S(2)}, u32[]{:S(2)}) collective-permute-start(bf16[2,32,3072]{2,1,0:T(8,128)(2,1)S(1)} %pad_maximum_fusion.3), channel_id=1, source_target_pairs={{0,4},{1,5},{2,6},{3,7},{4,0},{5,1},{6,2},{7,3},{8,12},{9,13},{10,... | collective-permute-start | bytes 1179656 | tf_op jit(solution)/shard_map/ppermute | solution.py:19
  102.6 19.0 %collective-permute-start.36 = (bf16[2,32,3072]{2,1,0:T(8,128)(2,1)S(1)}, bf16[2,32,3072]{2,1,0:T(8,128)(2,1)S(1)}, u32[]{:S(2)}, u32[]{:S(2)}) collective-permute-start(bf16[2,32,3072]{2,1,0:T(8,128)(2,1)S(1)} %pad_maximum_fusion.2), channel_id=1, source_target_pairs={{0,2},{1,3},{2,0},{3,1},{4,6},{5,7},{6,4},{7,5},{8,10},{9,11},{10,... | collective-permute-start | bytes 1179656 | tf_op jit(solution)/shard_map/ppermute | solution.py:19
  106.0 7.8 %collective-permute-start.31 = (bf16[48,1536]{1,0:T(8,128)(2,1)S(1)}, bf16[48,1536]{1,0:T(8,128)(2,1)S(1)}, u32[]{:S(2)}, u32[]{:S(2)}) collective-permute-start(bf16[48,1536]{1,0:T(8,128)(2,1)S(1)} %get-tuple-element.121), channel_id=1, source_target_pairs={{0,8},{8,0},{16,24},{24,16},{1,9},{9,1},{17,25},{25,17},{2,10},{10... | collective-permute-start | bytes 442376 | tf_op jit(solution)/shard_map/ppermute | solution.py:19
  107.6 14.0 %collective-permute-start.32 = (bf16[48,1536]{1,0:T(8,128)(2,1)S(1)}, bf16[48,1536]{1,0:T(8,128)(2,1)S(1)}, u32[]{:S(2)}, u32[]{:S(2)}) collective-permute-start(bf16[48,1536]{1,0:T(8,128)(2,1)S(1)} %get-tuple-element.122), channel_id=1, source_target_pairs={{0,16},{8,24},{16,0},{24,8},{1,17},{9,25},{17,1},{25,9},{2,18},{10... | collective-permute-start | bytes 442376 | tf_op jit(solution)/shard_map/ppermute | solution.py:19
  110.2 11.4 %collective-permute-start.33 = (bf16[48,1536]{1,0:T(8,128)(2,1)S(1)}, bf16[48,1536]{1,0:T(8,128)(2,1)S(1)}, u32[]{:S(2)}, u32[]{:S(2)}) collective-permute-start(bf16[48,1536]{1,0:T(8,128)(2,1)S(1)} %get-tuple-element.119), channel_id=1, source_target_pairs={{0,24},{8,16},{16,8},{24,0},{1,25},{9,17},{17,9},{25,1},{2,26},{10... | collective-permute-start | bytes 442376 | tf_op jit(solution)/shard_map/ppermute | solution.py:19
  113.7 10.1 %collective-permute-start.39 = (bf16[32,6144]{1,0:T(8,128)(2,1)S(1)}, bf16[32,6144]{1,0:T(8,128)(2,1)S(1)}, u32[]{:S(2)}, u32[]{:S(2)}) collective-permute-start(bf16[32,6144]{1,0:T(8,128)(2,1)S(1)} %copy-done.7), channel_id=1, source_target_pairs={{0,1},{1,0},{2,3},{3,2},{4,5},{5,4},{6,7},{7,6},{8,9},{9,8},{10,11... | collective-permute-start | bytes 1179656 | tf_op jit(solution)/shard_map/ppermute | solution.py:19
  121.7 5.7 %collective-permute-start.40 = (bf16[1,32,3072]{2,1,0:T(8,128)(2,1)S(1)}, bf16[1,32,3072]{2,1,0:T(8,128)(2,1)S(1)}, u32[]{:S(2)}, u32[]{:S(2)}) collective-permute-start(bf16[1,32,3072]{2,1,0:T(8,128)(2,1)S(1)} %fusion.18), channel_id=1, source_target_pairs={{0,4},{1,5},{2,6},{3,7},{4,0},{5,1},{6,2},{7,3},{8,12},{9,13},{10,... | collective-permute-start | bytes 589832 | tf_op jit(solution)/shard_map/ppermute | solution.py:19
  123.2 5.7 %collective-permute-start.41 = (bf16[1,32,3072]{2,1,0:T(8,128)(2,1)S(1)}, bf16[1,32,3072]{2,1,0:T(8,128)(2,1)S(1)}, u32[]{:S(2)}, u32[]{:S(2)}) collective-permute-start(bf16[1,32,3072]{2,1,0:T(8,128)(2,1)S(1)} %fusion.19), channel_id=1, source_target_pairs={{0,2},{1,3},{2,0},{3,1},{4,6},{5,7},{6,4},{7,5},{8,10},{9,11},{10,... | collective-permute-start | bytes 589832 | tf_op jit(solution)/shard_map/ppermute | solution.py:19
  129.6 5.7 %collective-permute-start.42 = (bf16[32,1536]{1,0:T(8,128)(2,1)S(1)}, bf16[32,1536]{1,0:T(8,128)(2,1)S(1)}, u32[]{:S(2)}, u32[]{:S(2)}) collective-permute-start(bf16[32,1536]{1,0:T(8,128)(2,1)S(1)} %get-tuple-element.125), channel_id=1, source_target_pairs={{0,8},{8,0},{16,24},{24,16},{1,9},{9,1},{17,25},{25,17},{2,10},{10... | collective-permute-start | bytes 294920 | tf_op jit(solution)/shard_map/ppermute | solution.py:19
  131.8 8.0 %collective-permute-start.43 = (bf16[32,1536]{1,0:T(8,128)(2,1)S(1)}, bf16[32,1536]{1,0:T(8,128)(2,1)S(1)}, u32[]{:S(2)}, u32[]{:S(2)}) collective-permute-start(bf16[32,1536]{1,0:T(8,128)(2,1)S(1)} %get-tuple-element.126), channel_id=1, source_target_pairs={{0,16},{8,24},{16,0},{24,8},{1,17},{9,25},{17,1},{25,9},{2,18},{10... | collective-permute-start | bytes 294920 | tf_op jit(solution)/shard_map/ppermute | solution.py:19
  132.9 7.0 %collective-permute-start.44 = (bf16[32,1536]{1,0:T(8,128)(2,1)S(1)}, bf16[32,1536]{1,0:T(8,128)(2,1)S(1)}, u32[]{:S(2)}, u32[]{:S(2)}) collective-permute-start(bf16[32,1536]{1,0:T(8,128)(2,1)S(1)} %get-tuple-element.123), channel_id=1, source_target_pairs={{0,24},{8,16},{16,8},{24,0},{1,25},{9,17},{17,9},{25,1},{2,26},{10... | collective-permute-start | bytes 294920 | tf_op jit(solution)/shard_map/ppermute | solution.py:19
  (28 other events, 87.8 us)

commit v3 on v2

--- a/solution.py
+++ b/solution.py
@@ -11,7 +11,8 @@
 F32 = jnp.float32
 BF16 = jnp.bfloat16
 VMEM_LIMIT = 16 * 1024 * 1024
-EXPERT_VMEM = 48 * 1024 * 1024
+EXPERT_VMEM = 40 * 1024 * 1024
+DOWN_VMEM = 28 * 1024 * 1024
 
 
 def exchange(array, axis, distance):
@@ -22,7 +23,7 @@
 def chunk_rows(slot_total):
     units = slot_total // 16
     first = (units + 1) // 2
-    return 16 * ((first + 1) // 2), 16 * (first // 2), 16 * (units - first)
+    return 16 * first, 16 * (units - first)
 
 
 def route_kernel(rows, slots, expert_count, chunks, *refs):
@@ -92,11 +93,14 @@
     blocks, refs = refs[:block_count], refs[block_count:]
     gate_ref, up_ref, hidden_ref, rows_ref, held_ref, sems, held_sems = refs
     buffers, _, _, tile = held_ref.shape
-    copies, start = [], 0
+    copies, start, column = [], 0, 0
     for i, block in enumerate(blocks):
-        target = rows_ref.at[pl.ds(start, block.shape[0])]
+        size, part = block.shape
+        target = rows_ref.at[pl.ds(start, size), pl.ds(column, part)]
         copies.append(pltpu.make_async_copy(block, target, sems.at[i]))
-        start += block.shape[0]
+        column += part
+        if column == rows_ref.shape[1]:
+            start, column = start + size, 0
     for c in copies:
         c.start()
     fetches = []
@@ -120,7 +124,8 @@
 
 
 def up_projection(blocks, gate_matrix, up_matrix):
-    rows, (width, units) = sum(b.shape[0] for b in blocks), gate_matrix.shape
+    width, units = gate_matrix.shape
+    rows = sum(b.size for b in blocks) // width
     buffers, tile = 3, 256
     return pl.pallas_call(
         functools.partial(up_kernel, len(blocks)),
@@ -162,14 +167,14 @@
             out_ref[:, part] = out[i * size : (i + 1) * size].astype(out_ref.dtype)
 
 
-def down_projection(hidden, count, down_matrix):
+def down_projection(hidden, count, down_matrix, place):
     rows, (units, width) = hidden.shape[0], down_matrix.shape
     buffers, tile = 3, width // 4
     vmem = pl.BlockSpec(memory_space=pltpu.VMEM)
     out = pl.pallas_call(
         functools.partial(down_kernel, count),
         out_shape=tuple(
-            jax.ShapeDtypeStruct((rows // count, width), F32 if i < count // 2 else BF16)
+            place((rows // count, width), F32 if i < count // 2 else BF16)
             for i in range(count)
         ),
         in_specs=[vmem, pl.BlockSpec(memory_space=pl.ANY)],
@@ -183,7 +188,7 @@
             bytes_accessed=2 * width * units + 3 * rows * width,
             transcendentals=0,
         ),
-        compiler_params=pltpu.CompilerParams(vmem_limit_bytes=EXPERT_VMEM),
+        compiler_params=pltpu.CompilerParams(vmem_limit_bytes=DOWN_VMEM),
         name="down",
     )(hidden, down_matrix)
     return out[: count // 2], out[count // 2 :]
@@ -245,14 +250,14 @@
 
 
 class Chunk:
-    def __init__(self, pieces, bits):
-        self.own, self.bits = pieces, bits
+    def __init__(self, own, bits):
+        self.own, self.bits = own, bits
 
     def spread(self):
-        self.held = {0: self.own}
+        self.held = {0: [self.own]}
         if len(self.bits) == 2:
             for bit in self.bits:
-                self.held[bit] = [exchange(p, "dp", bit) for p in self.own]
+                self.held[bit] = [exchange(self.own, "dp", bit)]
         else:
             for bit in self.bits:
                 for k, v in list(self.held.items()):
@@ -261,14 +266,9 @@
     def forward(self):
         if len(self.bits) == 2:
             a, b = self.bits
-            last = []
-            for i, (source, bit) in enumerate(((b, a), (a, b))):
-                pieces = self.held[source]
-                if len(pieces) == 1:
-                    half = pieces[0].shape[0] // 2
-                    pieces = [pieces[0][:half], pieces[0][half:]]
-                last.append(exchange(pieces[i], "dp", bit))
-            self.held[a | b] = last
+            half = self.own.shape[1] // 2
+            left, right = self.held[b][0][:, :half], self.held[a][0][:, half:]
+            self.held[a | b] = [exchange(left, "dp", a), exchange(right, "dp", b)]
 
     def up(self, matrices, *earlier):
         self.order = sorted(self.held)
@@ -278,12 +278,13 @@
             blocks[0] = after(blocks[0], *earlier)
         self.hidden = up_projection(blocks, *matrices[:2])
 
-    def down(self, matrices):
-        self.kept, self.sent = down_projection(self.hidden, 2 * len(self.order), matrices[2])
+    def down(self, matrices, place):
+        count = 2 * len(self.order)
+        self.kept, self.sent = down_projection(self.hidden, count, matrices[2], place)
 
     def pair_sum(self):
         partner = [exchange(sent, "dp", 1) for sent in self.sent]
-        width = self.own[0].shape[1]
+        width = self.own.shape[1]
         self.lanes = []
         for lane, bits in enumerate((self.bits, self.bits[::-1])):
             columns = slice(lane * width // 2, (lane + 1) * width // 2)
@@ -341,9 +342,9 @@
     own_part = lax.dynamic_slice_in_dim(flat, segment * slice_width, slice_width, 1)
     routed, gates = route(me, flat, norm_gain, router_weight, ids, rows, slots, sizes)
     matrices = w_gate[0], w_up[0], w_down[0]
-    one, two = Chunk(routed[:2], bits), Chunk(routed[2:], bits)
+    one, two = (Chunk(own, bits) for own in routed)
     one.spread()
-    two.own = [after(p, *(p for b in bits for p in one.held[b])) for p in two.own]
+    two.own = after(two.own, *(p for b in bits for p in one.held[b]))
     two.spread()
     one.forward()
     one.up(matrices)
@@ -351,7 +352,7 @@
     (one.hidden,), *arrived = together([one.hidden], *(two.held[b] for b in hops))
     two.held.update(zip(hops, arrived))
     two.forward()
-    one.down(matrices)
+    one.down(matrices, jax.ShapeDtypeStruct)
     last = max(two.held)
     one.kept, one.sent, two.held[last] = together(one.kept, one.sent, two.held[last])
     one.pair_sum()
@@ -366,22 +367,23 @@
         one.send(step)
         if step < steps - 1:
             one.arrive(step)
-    two.down(matrices)
+    two.down(matrices, pltpu.HBM)
     two.kept, two.sent, one.incoming = together(two.kept, two.sent, one.incoming)
     one.arrive(steps - 1)
     two.pair_sum()
     two.leave(0)
     two.send(0)
     taken = one.finish()
-    taken[1:], two.incoming = together(taken[1:], two.incoming)
-    two.arrive(0)
-    for step in range(1, steps):
-        two.leave(step)
-        two.send(step)
+    for step in range(steps):
+        if step < 1:
+            share = slice(1, 3)
+            taken[share], two.incoming = together(taken[share], two.incoming)
         two.arrive(step)
+        if step + 1 < steps:
+            two.leave(step + 1)
+            two.send(step + 1)
     taken = taken + two.finish()
-    wholes = sum(sizes[:2]), sizes[2]
-    out = combine(me, own_part, ids, gates, taken, rows, slots, wholes)
+    out = combine(me, own_part, ids, gates, taken, rows, slots, sizes)
     return out.reshape(micro_count, rows, slice_width)
 
 

time: 143 us -> 132 us (0.923)
  waiting for transfers between devices: 42.9 us -> 37 us
  Pallas kernels: 50.4 us -> 47.3 us
  other arithmetic: 5.52 us -> 3.29 us
    ppermute x45 -> x40, waiting for transfers between devices: 42.9 us -> 37 us  [exchange(): return lax.ppermute(array, axis, [(i, i ^ distance) for i in range(count)])]
    pallas_call x2, Pallas kernels: 30.2 us -> 27 us  [up_projection(): pl.pallas_call(functools.partial(up_kernel, len(blocks)), out_shape=jax.S...]
    unnamed x31 -> x55, local copies, waits for them, and re-layouts: 7.07 us -> 6.36 us
    ppermute x45 -> x40, starting transfers between devices: 34.6 us -> 34.9 us  [exchange(): return lax.ppermute(array, axis, [(i, i ^ distance) for i in range(count)])]
  transfers between devices with their start and end apart: 45 -> 40, of which waited for: 14 -> 14; matrix products, arithmetic and copies ran while one was open for 4% -> 3% of each run, Pallas kernels for 32% -> 33%
where the time goes in v3:
time: 132 us; the launch traced here: 131 us
  Pallas kernels  47.3 us (36%)
  waiting for transfers between devices  37 us (28%)
  starting transfers between devices  34.9 us (26%)
  local copies, waits for them, and re-layouts  8.25 us (6%)
  other arithmetic  3.29 us (2%)
    ppermute x40, waiting for transfers between devices, exchange(): return lax.ppermute(array, axis, [(i, i ^ distance) for i in range(count)])  37 us
    ppermute x40, starting transfers between devices, exchange(): return lax.ppermute(array, axis, [(i, i ^ distance) for i in range(count)])  34.9 us
    pallas_call x2, Pallas kernels, up_projection(): pl.pallas_call(functools.partial(up_kernel, len(blocks)), out_shape=jax.S...  27 us
    pallas_call x2, Pallas kernels, down_projection(): pl.pallas_call(functools.partial(down_kernel, count), out_shape=tuple((pl...  15.8 us
    unnamed x55, local copies, waits for them, and re-layouts  6.36 us
    pallas_call x1, Pallas kernels, combine(): pl.pallas_call(functools.partial(combine_kernel, rows, slots, count, chun...  2.92 us
  transfers between devices with their start and end apart: 40, of which 14 were waited for; matrix products, arithmetic and copies ran while one was open for 3% of the time, Pallas kernels for 33%

profile of v3, /device:TPU:0, one launch (start us, length us, event | category | flops | bytes accessed | tf_op | source)
XLA Modules:
  0.0 131.4 jit_solution(8805434940992093500)
XLA Ops:
  1.6 1.4 %copy-done = bf16[4,32,6144]{2,1,0:T(8,128)(2,1)S(1)} copy-done((bf16[4,32,6144]{2,1,0:T(8,128)(2,1)S(1)}, bf16[4,32,6144]{2,1,0:T(8,128)(2,1)}, u32[]{:S(2)}) %copy-start) | copy-done | bytes 1572888
  3.8 1.5 %route.1 = (bf16[48,6144]{1,0:T(8,128)(2,1)S(1)}, bf16[32,6144]{1,0:T(8,128)(2,1)S(1)}, f32[128,2]{1,0:T(8,128)S(1)}) custom-call(s32[1]{0:T(128)} %bitcast.refs_0_, bf16[128,6144]{1,0:T(8,128)(2,1)S(1)} %bitcast.75, bf16[1,6144]{1,0:T(2,128)(2,1)S(1)} %reshape.42.refs_2_, bf16[4,6144]{1,0:T(4,128)(2,1)S(1)} %bitcast.79, s32[128,2]{1,0:T(8,128)S(1)} %bitcast.77, ...), custom_call_target="tpu_custom_call" | custom-call | tf_op jit(solution)/shard_map/route/pallas_call | solution.py:67
  5.4 3.0 %collective-permute-start.1 = (bf16[48,6144]{1,0:T(8,128)(2,1)S(1)}, bf16[48,6144]{1,0:T(8,128)(2,1)S(1)}, u32[]{:S(2)}, u32[]{:S(2)}) collective-permute-start(bf16[48,6144]{1,0:T(8,128)(2,1)S(1)} %get-tuple-element.57.refs_0_), channel_id=1, source_target_pairs={{0,4},{1,5},{2,6},{3,7},{4,0},{5,1},{6,2},{7,3},{8,12},{9,13},{10,... | collective-permute-start | bytes 1769480 | tf_op jit(solution)/shard_map/ppermute | solution.py:20
  8.4 1.5 %collective-permute-start = (bf16[48,6144]{1,0:T(8,128)(2,1)S(1)}, bf16[48,6144]{1,0:T(8,128)(2,1)S(1)}, u32[]{:S(2)}, u32[]{:S(2)}) collective-permute-start(bf16[48,6144]{1,0:T(8,128)(2,1)S(1)} %get-tuple-element.57.refs_0_), channel_id=1, source_target_pairs={{0,2},{1,3},{2,0},{3,1},{4,6},{5,7},{6,4},{7,5},{8,10},{9,11},{10,... | collective-permute-start | bytes 1769480 | tf_op jit(solution)/shard_map/ppermute | solution.py:20
  9.9 11.8 %collective-permute-done.1.refs_2_ = bf16[48,6144]{1,0:T(8,128)(2,1)S(1)} collective-permute-done((bf16[48,6144]{1,0:T(8,128)(2,1)S(1)}, bf16[48,6144]{1,0:T(8,128)(2,1)S(1)}, u32[]{:S(2)}, u32[]{:S(2)}) %collective-permute-start.1) | collective-permute-done | bytes 589856 | tf_op jit(solution)/shard_map/ppermute | solution.py:20
  21.8 1.8 %collective-permute-start.2 = (bf16[48,3072]{1,0:T(8,128)(2,1)S(1)}, bf16[48,3072]{1,0:T(8,128)(2,1)S(1)}, u32[]{:S(2)}, u32[]{:S(2)}) collective-permute-start(bf16[48,3072]{1,0:T(8,128)(2,1)S(1)} %slice.176), channel_id=1, source_target_pairs={{0,2},{1,3},{2,0},{3,1},{4,6},{5,7},{6,4},{7,5},{8,10},{9,11},{10,... | collective-permute-start | bytes 884744 | tf_op jit(solution)/shard_map/ppermute | solution.py:20
  23.6 1.6 %collective-permute-start.3 = (bf16[48,3072]{1,0:T(8,128)(2,1)S(1)}, bf16[48,3072]{1,0:T(8,128)(2,1)S(1)}, u32[]{:S(2)}, u32[]{:S(2)}) collective-permute-start(bf16[48,3072]{1,0:T(8,128)(2,1)S(1)} %slice.177), channel_id=1, source_target_pairs={{0,4},{1,5},{2,6},{3,7},{4,0},{5,1},{6,2},{7,3},{8,12},{9,13},{10,... | collective-permute-start | bytes 884744 | tf_op jit(solution)/shard_map/ppermute | solution.py:20
  25.7 4.4 %collective-permute-done.2.refs_3_ = bf16[48,3072]{1,0:T(8,128)(2,1)S(1)} collective-permute-done((bf16[48,3072]{1,0:T(8,128)(2,1)S(1)}, bf16[48,3072]{1,0:T(8,128)(2,1)S(1)}, u32[]{:S(2)}, u32[]{:S(2)}) %collective-permute-start.2) | collective-permute-done | bytes 294944 | tf_op jit(solution)/shard_map/ppermute | solution.py:20
  30.0 1.2 collective-permute-done.3.refs_4_
  31.2 1.5 %collective-permute-start.10 = (bf16[32,6144]{1,0:T(8,128)(2,1)S(1)}, bf16[32,6144]{1,0:T(8,128)(2,1)S(1)}, u32[]{:S(2)}, u32[]{:S(2)}) collective-permute-start(bf16[32,6144]{1,0:T(8,128)(2,1)S(1)} %get-tuple-element.79.refs_0_), channel_id=1, source_target_pairs={{0,4},{1,5},{2,6},{3,7},{4,0},{5,1},{6,2},{7,3},{8,12},{9,13},{10,... | collective-permute-start | bytes 1179656 | tf_op jit(solution)/shard_map/ppermute | solution.py:20
  33.5 14.9 %up.2.hidden_ref = bf16[384,1024]{1,0:T(8,128)(2,1)S(1)} custom-call(bf16[48,6144]{1,0:T(8,128)(2,1)S(1)} %get-tuple-element.57.refs_0_, bf16[48,6144]{1,0:T(8,128)(2,1)S(1)} %collective-permute-done.refs_1_, bf16[48,6144]{1,0:T(8,128)(2,1)S(1)} %collective-permute-done.1.refs_2_, bf16[48,3072]{1,0:T(8,128)(2,1)S(1)} %collective-permute-done.2.refs_3_, ...), custom_call_target="tpu_custom_call" | custom-call | flops 9663676416 | bytes 29884416 | tf_op jit(solution)/shard_map/up/pallas_call | solution.py:130
  49.4 1.4 %collective-permute-start.11 = (bf16[32,3072]{1,0:T(8,128)(2,1)S(1)}, bf16[32,3072]{1,0:T(8,128)(2,1)S(1)}, u32[]{:S(2)}, u32[]{:S(2)}) collective-permute-start(bf16[32,3072]{1,0:T(8,128)(2,1)S(1)} %slice.134), channel_id=1, source_target_pairs={{0,2},{1,3},{2,0},{3,1},{4,6},{5,7},{6,4},{7,5},{8,10},{9,11},{10,... | collective-permute-start | bytes 589832 | tf_op jit(solution)/shard_map/ppermute | solution.py:20
  52.6 7.5 %down.2 = (f32[48,6144]{1,0:T(8,128)S(1)}, f32[48,6144]{1,0:T(8,128)S(1)}, f32[48,6144]{1,0:T(8,128)S(1)}, f32[48,6144]{1,0:T(8,128)S(1)}, bf16[48,6144]{1,0:T(8...) custom-call(bf16[384,1024]{1,0:T(8,128)(2,1)S(1)} %copy-done.11, ...), custom_call_target="tpu_custom_call" | custom-call | flops 4831838208 | bytes 19660800 | tf_op jit(solution)/shard_map/down/pallas_call | solution.py:174
  62.5 2.3 %collective-permute-done.16 = bf16[48,6144]{1,0:T(8,128)(2,1)S(1)} collective-permute-done((bf16[48,6144]{1,0:T(8,128)(2,1)S(1)}, bf16[48,6144]{1,0:T(8,128)(2,1)S(1)}, u32[]{:S(2)}, u32[]{:S(2)}) %collective-permute-start.16) | collective-permute-done | bytes 589856 | tf_op jit(solution)/shard_map/ppermute | solution.py:20
  66.5 1.6 %collective-permute-start.23 = (bf16[2,48,3072]{2,1,0:T(8,128)(2,1)S(1)}, bf16[2,48,3072]{2,1,0:T(8,128)(2,1)S(1)}, u32[]{:S(2)}, u32[]{:S(2)}) collective-permute-start(bf16[2,48,3072]{2,1,0:T(8,128)(2,1)S(1)} %pad_maximum_fusion.1), channel_id=1, source_target_pairs={{0,4},{1,5},{2,6},{3,7},{4,0},{5,1},{6,2},{7,3},{8,12},{9,13},{10,... | collective-permute-start | bytes 1769480 | tf_op jit(solution)/shard_map/ppermute | solution.py:20
  68.8 12.1 %up.3.hidden_ref = bf16[256,1024]{1,0:T(8,128)(2,1)S(1)} custom-call(bf16[32,6144]{1,0:T(8,128)(2,1)S(1)} %copy-done.4, bf16[32,6144]{1,0:T(8,128)(2,1)S(1)} %collective-permute-done.9.refs_1_, bf16[32,6144]{1,0:T(8,128)(2,1)S(1)} %collective-permute-done.10.refs_2_, bf16[32,3072]{1,0:T(8,128)(2,1)S(1)} %collective-permute-done.11.refs_3_, ...), custom_call_target="tpu_custom_call" | custom-call | flops 6442450944 | bytes 28311552 | tf_op jit(solution)/shard_map/up/pallas_call | solution.py:130
  81.9 1.2 collective-permute-done.22
  85.3 8.3 %down.3 = (f32[32,6144]{1,0:T(8,128)}, f32[32,6144]{1,0:T(8,128)}, f32[32,6144]{1,0:T(8,128)}, f32[32,6144]{1,0:T(8,128)}, bf16[32,6144]{1,0:T(8,128)(2,1)}, /*i...) custom-call(bf16[256,1024]{1,0:T(8,128)(2,1)S(1)} %up.3.hidden_ref, ...), custom_call_target="tpu_custom_call" | custom-call | flops 3221225472 | bytes 17301504 | tf_op jit(solution)/shard_map/down/pallas_call | solution.py:174
  98.1 1.4 %collective-permute-start.30 = (bf16[2,32,3072]{2,1,0:T(8,128)(2,1)S(1)}, bf16[2,32,3072]{2,1,0:T(8,128)(2,1)S(1)}, u32[]{:S(2)}, u32[]{:S(2)}) collective-permute-start(bf16[2,32,3072]{2,1,0:T(8,128)(2,1)S(1)} %pad_maximum_fusion.2), channel_id=1, source_target_pairs={{0,2},{1,3},{2,0},{3,1},{4,6},{5,7},{6,4},{7,5},{8,10},{9,11},{10,... | collective-permute-start | bytes 1179656 | tf_op jit(solution)/shard_map/ppermute | solution.py:20
  100.3 1.6 %collective-permute-start.26 = (bf16[48,1536]{1,0:T(8,128)(2,1)S(1)}, bf16[48,1536]{1,0:T(8,128)(2,1)S(1)}, u32[]{:S(2)}, u32[]{:S(2)}) collective-permute-start(bf16[48,1536]{1,0:T(8,128)(2,1)S(1)} %get-tuple-element.117), channel_id=1, source_target_pairs={{0,8},{8,0},{16,24},{24,16},{1,9},{9,1},{17,25},{25,17},{2,10},{10... | collective-permute-start | bytes 442376 | tf_op jit(solution)/shard_map/ppermute | solution.py:20
  101.9 2.6 %collective-permute-start.27 = (bf16[48,1536]{1,0:T(8,128)(2,1)S(1)}, bf16[48,1536]{1,0:T(8,128)(2,1)S(1)}, u32[]{:S(2)}, u32[]{:S(2)}) collective-permute-start(bf16[48,1536]{1,0:T(8,128)(2,1)S(1)} %get-tuple-element.118), channel_id=1, source_target_pairs={{0,16},{8,24},{16,0},{24,8},{1,17},{9,25},{17,1},{25,9},{2,18},{10... | collective-permute-start | bytes 442376 | tf_op jit(solution)/shard_map/ppermute | solution.py:20
  104.5 3.7 %collective-permute-done.26.refs_5_ = bf16[48,1536]{1,0:T(8,128)(2,1)S(1)} collective-permute-done((bf16[48,1536]{1,0:T(8,128)(2,1)S(1)}, bf16[48,1536]{1,0:T(8,128)(2,1)S(1)}, u32[]{:S(2)}, u32[]{:S(2)}) %collective-permute-start.26) | collective-permute-done | bytes 147488 | tf_op jit(solution)/shard_map/ppermute | solution.py:20
  108.2 2.9 %collective-permute-done.27.refs_6_ = bf16[48,1536]{1,0:T(8,128)(2,1)S(1)} collective-permute-done((bf16[48,1536]{1,0:T(8,128)(2,1)S(1)}, bf16[48,1536]{1,0:T(8,128)(2,1)S(1)}, u32[]{:S(2)}, u32[]{:S(2)}) %collective-permute-start.27) | collective-permute-done | bytes 147488 | tf_op jit(solution)/shard_map/ppermute | solution.py:20
  111.2 1.2 collective-permute-start.35
  113.2 2.5 %collective-permute-start.33 = (bf16[48,1536]{1,0:T(8,128)(2,1)S(1)}, bf16[48,1536]{1,0:T(8,128)(2,1)S(1)}, u32[]{:S(2)}, u32[]{:S(2)}) collective-permute-start(bf16[48,1536]{1,0:T(8,128)(2,1)S(1)} %get-tuple-element.115), channel_id=1, source_target_pairs={{0,24},{8,16},{16,8},{24,0},{1,25},{9,17},{17,9},{25,1},{2,26},{10... | collective-permute-start | bytes 442376 | tf_op jit(solution)/shard_map/ppermute | solution.py:20
  115.7 1.2 collective-permute-done.35
  116.9 1.3 collective-permute-done.36
  119.3 2.6 %collective-permute-start.38 = (bf16[32,1536]{1,0:T(8,128)(2,1)S(1)}, bf16[32,1536]{1,0:T(8,128)(2,1)S(1)}, u32[]{:S(2)}, u32[]{:S(2)}) collective-permute-start(bf16[32,1536]{1,0:T(8,128)(2,1)S(1)} %get-tuple-element.122), channel_id=1, source_target_pairs={{0,16},{8,24},{16,0},{24,8},{1,17},{9,25},{17,1},{25,9},{2,18},{10... | collective-permute-start | bytes 294920 | tf_op jit(solution)/shard_map/ppermute | solution.py:20
  121.9 1.3 %collective-permute-start.39 = (bf16[32,1536]{1,0:T(8,128)(2,1)S(1)}, bf16[32,1536]{1,0:T(8,128)(2,1)S(1)}, u32[]{:S(2)}, u32[]{:S(2)}) collective-permute-start(bf16[32,1536]{1,0:T(8,128)(2,1)S(1)} %get-tuple-element.119), channel_id=1, source_target_pairs={{0,24},{8,16},{16,8},{24,0},{1,25},{9,17},{17,9},{25,1},{2,26},{10... | collective-permute-start | bytes 294920 | tf_op jit(solution)/shard_map/ppermute | solution.py:20
  124.3 2.5 %collective-permute-done.38.refs_10_ = bf16[32,1536]{1,0:T(8,128)(2,1)S(1)} collective-permute-done((bf16[32,1536]{1,0:T(8,128)(2,1)S(1)}, bf16[32,1536]{1,0:T(8,128)(2,1)S(1)}, u32[]{:S(2)}, u32[]{:S(2)}) %collective-permute-start.38) | collective-permute-done | bytes 98336 | tf_op jit(solution)/shard_map/ppermute | solution.py:20
  126.8 1.6 %collective-permute-done.39.refs_11_ = bf16[32,1536]{1,0:T(8,128)(2,1)S(1)} collective-permute-done((bf16[32,1536]{1,0:T(8,128)(2,1)S(1)}, bf16[32,1536]{1,0:T(8,128)(2,1)S(1)}, u32[]{:S(2)}, u32[]{:S(2)}) %collective-permute-start.39) | collective-permute-done | bytes 98336 | tf_op jit(solution)/shard_map/ppermute | solution.py:20
  128.4 2.9 %combine.1 = bf16[128,1536]{1,0:T(8,128)(2,1)} custom-call(s32[1]{0:T(128)} %bitcast.refs_0_, bf16[128,1536]{1,0:T(8,128)(2,1)S(1)} %constant_dynamic-slice_fusion.refs_1_, s32[128,2]{1,0:T(8,128)S(1)} %bitcast.78, f32[128,2]{1,0:T(8,128)S(1)} %copy-done.6, bf16[48,1536]{1,0:T(8,128)(2,1)S(1)} %get-tuple-element.116.refs_4_, ...), custom_call_target="tpu_custom_call" | custom-call | tf_op jit(solution)/shard_map/combine/pallas_call | solution.py:233
  (135 shorter events, 22.3 us)
Async XLA Ops:
  5.4 16.4 %collective-permute-start.1 = (bf16[48,6144]{1,0:T(8,128)(2,1)S(1)}, bf16[48,6144]{1,0:T(8,128)(2,1)S(1)}, u32[]{:S(2)}, u32[]{:S(2)}) collective-permute-start(bf16[48,6144]{1,0:T(8,128)(2,1)S(1)} %get-tuple-element.57.refs_0_), channel_id=1, source_target_pairs={{0,4},{1,5},{2,6},{3,7},{4,0},{5,1},{6,2},{7,3},{8,12},{9,13},{10,... | collective-permute-start | bytes 1769480 | tf_op jit(solution)/shard_map/ppermute | solution.py:20
  8.4 15.1 %collective-permute-start = (bf16[48,6144]{1,0:T(8,128)(2,1)S(1)}, bf16[48,6144]{1,0:T(8,128)(2,1)S(1)}, u32[]{:S(2)}, u32[]{:S(2)}) collective-permute-start(bf16[48,6144]{1,0:T(8,128)(2,1)S(1)} %get-tuple-element.57.refs_0_), channel_id=1, source_target_pairs={{0,2},{1,3},{2,0},{3,1},{4,6},{5,7},{6,4},{7,5},{8,10},{9,11},{10,... | collective-permute-start | bytes 1769480 | tf_op jit(solution)/shard_map/ppermute | solution.py:20
  9.9 21.3 %collective-permute-start.4 = (bf16[48,6144]{1,0:T(8,128)(2,1)S(1)}, bf16[48,6144]{1,0:T(8,128)(2,1)S(1)}, u32[]{:S(2)}, u32[]{:S(2)}) collective-permute-start(bf16[48,6144]{1,0:T(8,128)(2,1)S(1)} %get-tuple-element.57.refs_0_), channel_id=1, source_target_pairs={{0,1},{1,0},{2,3},{3,2},{4,5},{5,4},{6,7},{7,6},{8,9},{9,8},{10,11... | collective-permute-start | bytes 1769480 | tf_op jit(solution)/shard_map/ppermute | solution.py:20
  21.8 8.3 %collective-permute-start.2 = (bf16[48,3072]{1,0:T(8,128)(2,1)S(1)}, bf16[48,3072]{1,0:T(8,128)(2,1)S(1)}, u32[]{:S(2)}, u32[]{:S(2)}) collective-permute-start(bf16[48,3072]{1,0:T(8,128)(2,1)S(1)} %slice.176), channel_id=1, source_target_pairs={{0,2},{1,3},{2,0},{3,1},{4,6},{5,7},{6,4},{7,5},{8,10},{9,11},{10,... | collective-permute-start | bytes 884744 | tf_op jit(solution)/shard_map/ppermute | solution.py:20
  23.6 7.7 %collective-permute-start.3 = (bf16[48,3072]{1,0:T(8,128)(2,1)S(1)}, bf16[48,3072]{1,0:T(8,128)(2,1)S(1)}, u32[]{:S(2)}, u32[]{:S(2)}) collective-permute-start(bf16[48,3072]{1,0:T(8,128)(2,1)S(1)} %slice.177), channel_id=1, source_target_pairs={{0,4},{1,5},{2,6},{3,7},{4,0},{5,1},{6,2},{7,3},{8,12},{9,13},{10,... | collective-permute-start | bytes 884744 | tf_op jit(solution)/shard_map/ppermute | solution.py:20
  25.2 8.3 %collective-permute-start.5 = (bf16[48,6144]{1,0:T(8,128)(2,1)S(1)}, bf16[48,6144]{1,0:T(8,128)(2,1)S(1)}, u32[]{:S(2)}, u32[]{:S(2)}) collective-permute-start(bf16[48,6144]{1,0:T(8,128)(2,1)S(1)} %collective-permute-done.refs_1_), channel_id=1, source_target_pairs={{0,1},{1,0},{2,3},{3,2},{4,5},{5,4},{6,7},{7,6},{8,9},{9,8},{10,11... | collective-permute-start | bytes 1769480 | tf_op jit(solution)/shard_map/ppermute | solution.py:20
  25.2 8.3 %collective-permute-start.6 = (bf16[48,6144]{1,0:T(8,128)(2,1)S(1)}, bf16[48,6144]{1,0:T(8,128)(2,1)S(1)}, u32[]{:S(2)}, u32[]{:S(2)}) collective-permute-start(bf16[48,6144]{1,0:T(8,128)(2,1)S(1)} %collective-permute-done.1.refs_2_), channel_id=1, source_target_pairs={{0,1},{1,0},{2,3},{3,2},{4,5},{5,4},{6,7},{7,6},{8,9},{9,8},{10,11... | collective-permute-start | bytes 1769480 | tf_op jit(solution)/shard_map/ppermute | solution.py:20
  31.2 18.2 %collective-permute-start.10 = (bf16[32,6144]{1,0:T(8,128)(2,1)S(1)}, bf16[32,6144]{1,0:T(8,128)(2,1)S(1)}, u32[]{:S(2)}, u32[]{:S(2)}) collective-permute-start(bf16[32,6144]{1,0:T(8,128)(2,1)S(1)} %get-tuple-element.79.refs_0_), channel_id=1, source_target_pairs={{0,4},{1,5},{2,6},{3,7},{4,0},{5,1},{6,2},{7,3},{8,12},{9,13},{10,... | collective-permute-start | bytes 1179656 | tf_op jit(solution)/shard_map/ppermute | solution.py:20
  32.8 16.6 %collective-permute-start.9 = (bf16[32,6144]{1,0:T(8,128)(2,1)S(1)}, bf16[32,6144]{1,0:T(8,128)(2,1)S(1)}, u32[]{:S(2)}, u32[]{:S(2)}) collective-permute-start(bf16[32,6144]{1,0:T(8,128)(2,1)S(1)} %get-tuple-element.79.refs_0_), channel_id=1, source_target_pairs={{0,2},{1,3},{2,0},{3,1},{4,6},{5,7},{6,4},{7,5},{8,10},{9,11},{10,... | collective-permute-start | bytes 1179656 | tf_op jit(solution)/shard_map/ppermute | solution.py:20
  49.4 10.7 %collective-permute-start.11 = (bf16[32,3072]{1,0:T(8,128)(2,1)S(1)}, bf16[32,3072]{1,0:T(8,128)(2,1)S(1)}, u32[]{:S(2)}, u32[]{:S(2)}) collective-permute-start(bf16[32,3072]{1,0:T(8,128)(2,1)S(1)} %slice.134), channel_id=1, source_target_pairs={{0,2},{1,3},{2,0},{3,1},{4,6},{5,7},{6,4},{7,5},{8,10},{9,11},{10,... | collective-permute-start | bytes 589832 | tf_op jit(solution)/shard_map/ppermute | solution.py:20
  50.8 9.3 %collective-permute-start.12 = (bf16[32,3072]{1,0:T(8,128)(2,1)S(1)}, bf16[32,3072]{1,0:T(8,128)(2,1)S(1)}, u32[]{:S(2)}, u32[]{:S(2)}) collective-permute-start(bf16[32,3072]{1,0:T(8,128)(2,1)S(1)} %slice.135), channel_id=1, source_target_pairs={{0,4},{1,5},{2,6},{3,7},{4,0},{5,1},{6,2},{7,3},{8,12},{9,13},{10,... | collective-permute-start | bytes 589832 | tf_op jit(solution)/shard_map/ppermute | solution.py:20
  60.2 6.3 %collective-permute-start.17 = (bf16[32,6144]{1,0:T(8,128)(2,1)S(1)}, bf16[32,6144]{1,0:T(8,128)(2,1)S(1)}, u32[]{:S(2)}, u32[]{:S(2)}) collective-permute-start(bf16[32,6144]{1,0:T(8,128)(2,1)S(1)} %copy-done.4), channel_id=1, source_target_pairs={{0,1},{1,0},{2,3},{3,2},{4,5},{5,4},{6,7},{7,6},{8,9},{9,8},{10,11... | collective-permute-start | bytes 1179656 | tf_op jit(solution)/shard_map/ppermute | solution.py:20
  60.7 8.1 %collective-permute-start.18 = (bf16[32,6144]{1,0:T(8,128)(2,1)S(1)}, bf16[32,6144]{1,0:T(8,128)(2,1)S(1)}, u32[]{:S(2)}, u32[]{:S(2)}) collective-permute-start(bf16[32,6144]{1,0:T(8,128)(2,1)S(1)} %collective-permute-done.9.refs_1_), channel_id=1, source_target_pairs={{0,1},{1,0},{2,3},{3,2},{4,5},{5,4},{6,7},{7,6},{8,9},{9,8},{10,11... | collective-permute-start | bytes 1179656 | tf_op jit(solution)/shard_map/ppermute | solution.py:20
  60.8 8.0 %collective-permute-start.19 = (bf16[32,6144]{1,0:T(8,128)(2,1)S(1)}, bf16[32,6144]{1,0:T(8,128)(2,1)S(1)}, u32[]{:S(2)}, u32[]{:S(2)}) collective-permute-start(bf16[32,6144]{1,0:T(8,128)(2,1)S(1)} %collective-permute-done.10.refs_2_), channel_id=1, source_target_pairs={{0,1},{1,0},{2,3},{3,2},{4,5},{5,4},{6,7},{7,6},{8,9},{9,8},{10,11... | collective-permute-start | bytes 1179656 | tf_op jit(solution)/shard_map/ppermute | solution.py:20
  61.2 3.5 %collective-permute-start.16 = (bf16[48,6144]{1,0:T(8,128)(2,1)S(1)}, bf16[48,6144]{1,0:T(8,128)(2,1)S(1)}, u32[]{:S(2)}, u32[]{:S(2)}) collective-permute-start(bf16[48,6144]{1,0:T(8,128)(2,1)S(1)} %get-tuple-element.78), channel_id=1, source_target_pairs={{0,1},{1,0},{2,3},{3,2},{4,5},{5,4},{6,7},{7,6},{8,9},{9,8},{10,11... | collective-permute-start | bytes 1769480 | tf_op jit(solution)/shard_map/ppermute | solution.py:20
  66.5 15.4 %collective-permute-start.23 = (bf16[2,48,3072]{2,1,0:T(8,128)(2,1)S(1)}, bf16[2,48,3072]{2,1,0:T(8,128)(2,1)S(1)}, u32[]{:S(2)}, u32[]{:S(2)}) collective-permute-start(bf16[2,48,3072]{2,1,0:T(8,128)(2,1)S(1)} %pad_maximum_fusion.1), channel_id=1, source_target_pairs={{0,4},{1,5},{2,6},{3,7},{4,0},{5,1},{6,2},{7,3},{8,12},{9,13},{10,... | collective-permute-start | bytes 1769480 | tf_op jit(solution)/shard_map/ppermute | solution.py:20
  68.1 15.1 %collective-permute-start.22 = (bf16[2,48,3072]{2,1,0:T(8,128)(2,1)S(1)}, bf16[2,48,3072]{2,1,0:T(8,128)(2,1)S(1)}, u32[]{:S(2)}, u32[]{:S(2)}) collective-permute-start(bf16[2,48,3072]{2,1,0:T(8,128)(2,1)S(1)} %pad_maximum_fusion), channel_id=1, source_target_pairs={{0,2},{1,3},{2,0},{3,1},{4,6},{5,7},{6,4},{7,5},{8,10},{9,11},{10,... | collective-permute-start | bytes 1769480 | tf_op jit(solution)/shard_map/ppermute | solution.py:20
  83.3 10.3 %collective-permute-start.25 = (bf16[1,48,3072]{2,1,0:T(8,128)(2,1)S(1)}, bf16[1,48,3072]{2,1,0:T(8,128)(2,1)S(1)}, u32[]{:S(2)}, u32[]{:S(2)}) collective-permute-start(bf16[1,48,3072]{2,1,0:T(8,128)(2,1)S(1)} %fusion.13), channel_id=1, source_target_pairs={{0,2},{1,3},{2,0},{3,1},{4,6},{5,7},{6,4},{7,5},{8,10},{9,11},{10,... | collective-permute-start | bytes 884744 | tf_op jit(solution)/shard_map/ppermute | solution.py:20
  84.2 9.5 %collective-permute-start.24 = (bf16[1,48,3072]{2,1,0:T(8,128)(2,1)S(1)}, bf16[1,48,3072]{2,1,0:T(8,128)(2,1)S(1)}, u32[]{:S(2)}, u32[]{:S(2)}) collective-permute-start(bf16[1,48,3072]{2,1,0:T(8,128)(2,1)S(1)} %fusion.12), channel_id=1, source_target_pairs={{0,4},{1,5},{2,6},{3,7},{4,0},{5,1},{6,2},{7,3},{8,12},{9,13},{10,... | collective-permute-start | bytes 884744 | tf_op jit(solution)/shard_map/ppermute | solution.py:20
  93.7 5.8 %collective-permute-start.13 = (bf16[48,6144]{1,0:T(8,128)(2,1)S(1)}, bf16[48,6144]{1,0:T(8,128)(2,1)S(1)}, u32[]{:S(2)}, u32[]{:S(2)}) collective-permute-start(bf16[48,6144]{1,0:T(8,128)(2,1)S(1)} %copy-done.9), channel_id=1, source_target_pairs={{0,1},{1,0},{2,3},{3,2},{4,5},{5,4},{6,7},{7,6},{8,9},{9,8},{10,11... | collective-permute-start | bytes 1769480 | tf_op jit(solution)/shard_map/ppermute | solution.py:20
  94.3 3.7 %collective-permute-start.28 = (bf16[32,6144]{1,0:T(8,128)(2,1)}, bf16[32,6144]{1,0:T(8,128)(2,1)S(1)}, u32[]{:S(2)}, u32[]{:S(2)}) collective-permute-start(bf16[32,6144]{1,0:T(8,128)(2,1)} %get-tuple-element.96), channel_id=1, source_target_pairs={{0,1},{1,0},{2,3},{3,2},{4,5},{5,4},{6,7},{7,6},{8,9},{9,8},{10,11... | collective-permute-start | bytes 1179656 | tf_op jit(solution)/shard_map/ppermute | solution.py:20
  97.0 14.1 %collective-permute-start.32 = (bf16[2,32,3072]{2,1,0:T(8,128)(2,1)S(1)}, bf16[2,32,3072]{2,1,0:T(8,128)(2,1)S(1)}, u32[]{:S(2)}, u32[]{:S(2)}) collective-permute-start(bf16[2,32,3072]{2,1,0:T(8,128)(2,1)S(1)} %pad_maximum_fusion.3), channel_id=1, source_target_pairs={{0,4},{1,5},{2,6},{3,7},{4,0},{5,1},{6,2},{7,3},{8,12},{9,13},{10,... | collective-permute-start | bytes 1179656 | tf_op jit(solution)/shard_map/ppermute | solution.py:20
  98.1 13.0 %collective-permute-start.30 = (bf16[2,32,3072]{2,1,0:T(8,128)(2,1)S(1)}, bf16[2,32,3072]{2,1,0:T(8,128)(2,1)S(1)}, u32[]{:S(2)}, u32[]{:S(2)}) collective-permute-start(bf16[2,32,3072]{2,1,0:T(8,128)(2,1)S(1)} %pad_maximum_fusion.2), channel_id=1, source_target_pairs={{0,2},{1,3},{2,0},{3,1},{4,6},{5,7},{6,4},{7,5},{8,10},{9,11},{10,... | collective-permute-start | bytes 1179656 | tf_op jit(solution)/shard_map/ppermute | solution.py:20
  100.3 7.9 %collective-permute-start.26 = (bf16[48,1536]{1,0:T(8,128)(2,1)S(1)}, bf16[48,1536]{1,0:T(8,128)(2,1)S(1)}, u32[]{:S(2)}, u32[]{:S(2)}) collective-permute-start(bf16[48,1536]{1,0:T(8,128)(2,1)S(1)} %get-tuple-element.117), channel_id=1, source_target_pairs={{0,8},{8,0},{16,24},{24,16},{1,9},{9,1},{17,25},{25,17},{2,10},{10... | collective-permute-start | bytes 442376 | tf_op jit(solution)/shard_map/ppermute | solution.py:20
  101.9 9.2 %collective-permute-start.27 = (bf16[48,1536]{1,0:T(8,128)(2,1)S(1)}, bf16[48,1536]{1,0:T(8,128)(2,1)S(1)}, u32[]{:S(2)}, u32[]{:S(2)}) collective-permute-start(bf16[48,1536]{1,0:T(8,128)(2,1)S(1)} %get-tuple-element.118), channel_id=1, source_target_pairs={{0,16},{8,24},{16,0},{24,8},{1,17},{9,25},{17,1},{25,9},{2,18},{10... | collective-permute-start | bytes 442376 | tf_op jit(solution)/shard_map/ppermute | solution.py:20
  104.5 11.2 %collective-permute-start.34 = (bf16[32,6144]{1,0:T(8,128)(2,1)S(1)}, bf16[32,6144]{1,0:T(8,128)(2,1)S(1)}, u32[]{:S(2)}, u32[]{:S(2)}) collective-permute-start(bf16[32,6144]{1,0:T(8,128)(2,1)S(1)} %copy-done.23), channel_id=1, source_target_pairs={{0,1},{1,0},{2,3},{3,2},{4,5},{5,4},{6,7},{7,6},{8,9},{9,8},{10,11... | collective-permute-start | bytes 1179656 | tf_op jit(solution)/shard_map/ppermute | solution.py:20
  111.2 5.7 %collective-permute-start.35 = (bf16[1,32,3072]{2,1,0:T(8,128)(2,1)S(1)}, bf16[1,32,3072]{2,1,0:T(8,128)(2,1)S(1)}, u32[]{:S(2)}, u32[]{:S(2)}) collective-permute-start(bf16[1,32,3072]{2,1,0:T(8,128)(2,1)S(1)} %fusion.18), channel_id=1, source_target_pairs={{0,4},{1,5},{2,6},{3,7},{4,0},{5,1},{6,2},{7,3},{8,12},{9,13},{10,... | collective-permute-start | bytes 589832 | tf_op jit(solution)/shard_map/ppermute | solution.py:20
  112.5 5.7 %collective-permute-start.36 = (bf16[1,32,3072]{2,1,0:T(8,128)(2,1)S(1)}, bf16[1,32,3072]{2,1,0:T(8,128)(2,1)S(1)}, u32[]{:S(2)}, u32[]{:S(2)}) collective-permute-start(bf16[1,32,3072]{2,1,0:T(8,128)(2,1)S(1)} %fusion.19), channel_id=1, source_target_pairs={{0,2},{1,3},{2,0},{3,1},{4,6},{5,7},{6,4},{7,5},{8,10},{9,11},{10,... | collective-permute-start | bytes 589832 | tf_op jit(solution)/shard_map/ppermute | solution.py:20
  113.2 11.1 %collective-permute-start.33 = (bf16[48,1536]{1,0:T(8,128)(2,1)S(1)}, bf16[48,1536]{1,0:T(8,128)(2,1)S(1)}, u32[]{:S(2)}, u32[]{:S(2)}) collective-permute-start(bf16[48,1536]{1,0:T(8,128)(2,1)S(1)} %get-tuple-element.115), channel_id=1, source_target_pairs={{0,24},{8,16},{16,8},{24,0},{1,25},{9,17},{17,9},{25,1},{2,26},{10... | collective-permute-start | bytes 442376 | tf_op jit(solution)/shard_map/ppermute | solution.py:20
  118.8 5.5 %collective-permute-start.37 = (bf16[32,1536]{1,0:T(8,128)(2,1)S(1)}, bf16[32,1536]{1,0:T(8,128)(2,1)S(1)}, u32[]{:S(2)}, u32[]{:S(2)}) collective-permute-start(bf16[32,1536]{1,0:T(8,128)(2,1)S(1)} %get-tuple-element.121), channel_id=1, source_target_pairs={{0,8},{8,0},{16,24},{24,16},{1,9},{9,1},{17,25},{25,17},{2,10},{10... | collective-permute-start | bytes 294920 | tf_op jit(solution)/shard_map/ppermute | solution.py:20
  119.3 7.5 %collective-permute-start.38 = (bf16[32,1536]{1,0:T(8,128)(2,1)S(1)}, bf16[32,1536]{1,0:T(8,128)(2,1)S(1)}, u32[]{:S(2)}, u32[]{:S(2)}) collective-permute-start(bf16[32,1536]{1,0:T(8,128)(2,1)S(1)} %get-tuple-element.122), channel_id=1, source_target_pairs={{0,16},{8,24},{16,0},{24,8},{1,17},{9,25},{17,1},{25,9},{2,18},{10... | collective-permute-start | bytes 294920 | tf_op jit(solution)/shard_map/ppermute | solution.py:20
  121.9 6.5 %collective-permute-start.39 = (bf16[32,1536]{1,0:T(8,128)(2,1)S(1)}, bf16[32,1536]{1,0:T(8,128)(2,1)S(1)}, u32[]{:S(2)}, u32[]{:S(2)}) collective-permute-start(bf16[32,1536]{1,0:T(8,128)(2,1)S(1)} %get-tuple-element.119), channel_id=1, source_target_pairs={{0,24},{8,16},{16,8},{24,0},{1,25},{9,17},{17,9},{25,1},{2,26},{10... | collective-permute-start | bytes 294920 | tf_op jit(solution)/shard_map/ppermute | solution.py:20
  (35 other events, 278.4 us)

commit v4 on v3

--- a/solution.py
+++ b/solution.py
@@ -28,9 +28,12 @@
 
 def route_kernel(rows, slots, expert_count, chunks, *refs):
     me, tokens_ref, gain_ref, router_ref, ids_ref, ids_row_ref = refs[:6]
-    routed_refs, gates_ref = refs[6:-1], refs[-1]
+    routed_refs, (gates_ref, held_ref, sem) = refs[6:-3], refs[-3:]
     token_count = tokens_ref.shape[0]
-    widened = tokens_ref[...].astype(F32)
+    copy = pltpu.make_async_copy(tokens_ref, held_ref, sem)
+    copy.start()
+    copy.wait()
+    widened = held_ref[...].astype(F32)
     inverse_rms = lax.rsqrt(jnp.mean(widened * widened, axis=-1, keepdims=True) + epsilon)
     normed = (widened * inverse_rms * gain_ref[...].astype(F32)).astype(BF16)
     chosen = jnp.any(ids_row_ref[...] == me[0], axis=0, keepdims=True)
@@ -68,8 +71,10 @@
         functools.partial(route_kernel, rows, slots, expert_count, chunks),
         out_shape=tuple(jax.ShapeDtypeStruct((c, width), BF16) for c in chunks)
         + (jax.ShapeDtypeStruct((token_count, 2), F32),),
-        in_specs=[pl.BlockSpec(memory_space=pltpu.SMEM)] + [vmem] * 5,
+        in_specs=[pl.BlockSpec(memory_space=pltpu.SMEM), pl.BlockSpec(memory_space=pl.ANY)]
+        + [vmem] * 4,
         out_specs=(vmem,) * (len(chunks) + 1),
+        scratch_shapes=[pltpu.VMEM(tokens.shape, tokens.dtype), pltpu.SemaphoreType.DMA],
         compiler_params=pltpu.CompilerParams(vmem_limit_bytes=VMEM_LIMIT),
         name="route",
     )(me, tokens, norm_gain.reshape(1, width), router_weight.T, ids, ids.T)
@@ -149,39 +154,61 @@
 
 
 def down_kernel(out_count, hidden_ref, down_ref, *refs):
-    out_refs, (held_ref, held_sems) = refs[:out_count], refs[out_count:]
+    out_refs, refs = refs[:out_count], refs[out_count:]
+    held_ref, kept_ref, sent_ref, held_sems, out_sems = refs
     buffers, _, tile = held_ref.shape
-    size = hidden_ref.shape[0] // out_count
-    fetches = []
+    size, half = hidden_ref.shape[0] // out_count, out_count // 2
+    fetches, stores = [], []
     for j in range(down_ref.shape[1] // tile):
         part, slot = pl.ds(j * tile, tile), j % buffers
         fetches.append(
             [pltpu.make_async_copy(down_ref.at[:, part], held_ref.at[slot], held_sems.at[slot])]
         )
+        slot = j % kept_ref.shape[0]
+        stores.append(
+            [
+                pltpu.make_async_copy(
+                    (kept_ref if i < half else sent_ref).at[slot, pl.ds(i % half * size, size)],
+                    out_ref.at[:, part],
+                    out_sems.at[slot, i],
+                )
+                for i, out_ref in enumerate(out_refs)
+            ]
+        )
     arrive = staged(fetches, 2)
+    slots = kept_ref.shape[0]
     for j in range(len(fetches)):
         arrive(j)
-        part = slice(j * tile, (j + 1) * tile)
         out = jnp.dot(hidden_ref[...], held_ref[j % buffers], preferred_element_type=F32)
-        for i, out_ref in enumerate(out_refs):
-            out_ref[:, part] = out[i * size : (i + 1) * size].astype(out_ref.dtype)
-
-
-def down_projection(hidden, count, down_matrix, place):
+        if j >= slots:
+            for c in stores[j - slots]:
+                c.wait()
+        kept_ref[j % slots] = out[: half * size]
+        sent_ref[j % slots] = out[half * size :].astype(BF16)
+        for c in stores[j]:
+            c.start()
+    for group in stores[-slots:]:
+        for c in group:
+            c.wait()
+
+
+def down_projection(hidden, count, down_matrix):
     rows, (units, width) = hidden.shape[0], down_matrix.shape
-    buffers, tile = 3, width // 4
-    vmem = pl.BlockSpec(memory_space=pltpu.VMEM)
+    buffers, slots, tile = 3, 2, width // 4
     out = pl.pallas_call(
         functools.partial(down_kernel, count),
         out_shape=tuple(
-            place((rows // count, width), F32 if i < count // 2 else BF16)
+            pltpu.HBM((rows // count, width), F32 if i < count // 2 else BF16)
             for i in range(count)
         ),
-        in_specs=[vmem, pl.BlockSpec(memory_space=pl.ANY)],
-        out_specs=(vmem,) * count,
+        in_specs=[pl.BlockSpec(memory_space=pltpu.VMEM), pl.BlockSpec(memory_space=pl.ANY)],
+        out_specs=(pl.BlockSpec(memory_space=pltpu.HBM),) * count,
         scratch_shapes=[
             pltpu.VMEM((buffers, units, tile), BF16),
+            pltpu.VMEM((slots, rows // 2, tile), F32),
+            pltpu.VMEM((slots, rows // 2, tile), BF16),
             pltpu.SemaphoreType.DMA((buffers,)),
+            pltpu.SemaphoreType.DMA((slots, count)),
         ],
         cost_estimate=pl.CostEstimate(
             flops=2 * rows * width * units,
@@ -203,16 +230,17 @@
     same = lax.div(earlier, rows) == lax.div(later, rows)
     before = jnp.where((earlier < later) & same, 1.0, 0.0).astype(BF16)
     token = lax.broadcasted_iota(jnp.int32, (token_count, 1), 0)
+    expert = me[0] ^ lax.broadcasted_iota(jnp.int32, (token_count, 128), 1)
+    named = (ids_ref[:, 0:1] == expert) | (ids_ref[:, 1:2] == expert)
+    positions = jnp.dot(
+        before, jnp.where(named, 1.0, 0.0).astype(BF16), preferred_element_type=F32
+    ).astype(jnp.int32)
     total = own_ref[...].astype(F32)
     for k in range(count):
         which = me[0] ^ k
         first, second = ids_ref[:, 0:1] == which, ids_ref[:, 1:2] == which
         chosen = first | second
-        hits = jnp.where(chosen, 1.0, 0.0).astype(BF16)
-        position = jnp.dot(
-            before, jnp.broadcast_to(hits, (token_count, 128)), preferred_element_type=F32
-        )[:, 0:1].astype(jnp.int32)
-        slot = lax.div(token, rows) * slots + position
+        slot = lax.div(token, rows) * slots + positions[:, k : k + 1]
         weight = jnp.where(first, gates_ref[:, 0:1], 0.0) + jnp.where(
             second, gates_ref[:, 1:2], 0.0
         )
@@ -278,9 +306,8 @@
             blocks[0] = after(blocks[0], *earlier)
         self.hidden = up_projection(blocks, *matrices[:2])
 
-    def down(self, matrices, place):
-        count = 2 * len(self.order)
-        self.kept, self.sent = down_projection(self.hidden, count, matrices[2], place)
+    def down(self, matrices):
+        self.kept, self.sent = down_projection(self.hidden, 2 * len(self.order), matrices[2])
 
     def pair_sum(self):
         partner = [exchange(sent, "dp", 1) for sent in self.sent]
@@ -352,7 +379,7 @@
     (one.hidden,), *arrived = together([one.hidden], *(two.held[b] for b in hops))
     two.held.update(zip(hops, arrived))
     two.forward()
-    one.down(matrices, jax.ShapeDtypeStruct)
+    one.down(matrices)
     last = max(two.held)
     one.kept, one.sent, two.held[last] = together(one.kept, one.sent, two.held[last])
     one.pair_sum()
@@ -367,7 +394,7 @@
         one.send(step)
         if step < steps - 1:
             one.arrive(step)
-    two.down(matrices, pltpu.HBM)
+    two.down(matrices)
     two.kept, two.sent, one.incoming = together(two.kept, two.sent, one.incoming)
     one.arrive(steps - 1)
     two.pair_sum()

time: 132 us -> 129 us (0.977)
  local copies, waits for them, and re-layouts: 8.25 us -> 4.93 us
    unnamed x55 -> x25, local copies, waits for them, and re-layouts: 6.36 us -> 3.03 us
  transfers between devices with their start and end apart: 40 -> 40, of which waited for: 14 -> 16; matrix products, arithmetic and copies ran while one was open for 3% -> 4% of each run, Pallas kernels for 33% -> 34%
where the time goes in v4:
time: 129 us
  Pallas kernels  47.1 us (37%)
  waiting for transfers between devices  37.2 us (29%)
  starting transfers between devices  34.9 us (27%)
  local copies, waits for them, and re-layouts  4.93 us (4%)
  other arithmetic  4.53 us (4%)
    ppermute x40, waiting for transfers between devices, exchange(): return lax.ppermute(array, axis, [(i, i ^ distance) for i in range(count)])  37.2 us
    ppermute x40, starting transfers between devices, exchange(): return lax.ppermute(array, axis, [(i, i ^ distance) for i in range(count)])  34.9 us
    pallas_call x2, Pallas kernels, up_projection(): pl.pallas_call(functools.partial(up_kernel, len(blocks)), out_shape=jax.S...  26.6 us
    pallas_call x2, Pallas kernels, down_projection(): pl.pallas_call(functools.partial(down_kernel, count), out_shape=tuple((pl...  16.8 us
    another operation x14, other arithmetic, leave(): jnp.stack([sum((t.astype(F32) for t in terms[k])).astype(BF16) for k in l...  3.24 us
    unnamed x25, local copies, waits for them, and re-layouts  3.03 us
  transfers between devices with their start and end apart: 40, of which 16 were waited for; matrix products, arithmetic and copies ran while one was open for 4% of the time, Pallas kernels for 34%

profile of v4, /device:TPU:0, one launch (start us, length us, event | category | flops | bytes accessed | tf_op | source)
XLA Modules:
  0.0 129.0 jit_solution(4052110336260152720)
XLA Ops:
  1.6 1.4 %copy-done = bf16[4,32,6144]{2,1,0:T(8,128)(2,1)S(1)} copy-done((bf16[4,32,6144]{2,1,0:T(8,128)(2,1)S(1)}, bf16[4,32,6144]{2,1,0:T(8,128)(2,1)}, u32[]{:S(2)}) %copy-start) | copy-done | bytes 1572888
  3.8 1.7 %route.1 = (bf16[48,6144]{1,0:T(8,128)(2,1)S(1)}, bf16[32,6144]{1,0:T(8,128)(2,1)S(1)}, f32[128,2]{1,0:T(8,128)S(1)}) custom-call(s32[1]{0:T(128)} %bitcast.refs_0_, bf16[128,6144]{1,0:T(8,128)(2,1)S(1)} %bitcast.75, bf16[1,6144]{1,0:T(2,128)(2,1)S(1)} %reshape.42.refs_2_, bf16[4,6144]{1,0:T(4,128)(2,1)S(1)} %bitcast.79, s32[128,2]{1,0:T(8,128)S(1)} %bitcast.77, ...), custom_call_target="tpu_custom_call" | custom-call | tf_op jit(solution)/shard_map/route/pallas_call | solution.py:70
  5.5 3.0 %collective-permute-start.1 = (bf16[48,6144]{1,0:T(8,128)(2,1)S(1)}, bf16[48,6144]{1,0:T(8,128)(2,1)S(1)}, u32[]{:S(2)}, u32[]{:S(2)}) collective-permute-start(bf16[48,6144]{1,0:T(8,128)(2,1)S(1)} %get-tuple-element.57.refs_0_), channel_id=1, source_target_pairs={{0,4},{1,5},{2,6},{3,7},{4,0},{5,1},{6,2},{7,3},{8,12},{9,13},{10,... | collective-permute-start | bytes 1769480 | tf_op jit(solution)/shard_map/ppermute | solution.py:20
  8.5 1.5 %collective-permute-start = (bf16[48,6144]{1,0:T(8,128)(2,1)S(1)}, bf16[48,6144]{1,0:T(8,128)(2,1)S(1)}, u32[]{:S(2)}, u32[]{:S(2)}) collective-permute-start(bf16[48,6144]{1,0:T(8,128)(2,1)S(1)} %get-tuple-element.57.refs_0_), channel_id=1, source_target_pairs={{0,2},{1,3},{2,0},{3,1},{4,6},{5,7},{6,4},{7,5},{8,10},{9,11},{10,... | collective-permute-start | bytes 1769480 | tf_op jit(solution)/shard_map/ppermute | solution.py:20
  10.0 11.8 %collective-permute-done.1.refs_2_ = bf16[48,6144]{1,0:T(8,128)(2,1)S(1)} collective-permute-done((bf16[48,6144]{1,0:T(8,128)(2,1)S(1)}, bf16[48,6144]{1,0:T(8,128)(2,1)S(1)}, u32[]{:S(2)}, u32[]{:S(2)}) %collective-permute-start.1) | collective-permute-done | bytes 589856 | tf_op jit(solution)/shard_map/ppermute | solution.py:20
  21.8 1.8 %collective-permute-start.2 = (bf16[48,3072]{1,0:T(8,128)(2,1)S(1)}, bf16[48,3072]{1,0:T(8,128)(2,1)S(1)}, u32[]{:S(2)}, u32[]{:S(2)}) collective-permute-start(bf16[48,3072]{1,0:T(8,128)(2,1)S(1)} %slice.176), channel_id=1, source_target_pairs={{0,2},{1,3},{2,0},{3,1},{4,6},{5,7},{6,4},{7,5},{8,10},{9,11},{10,... | collective-permute-start | bytes 884744 | tf_op jit(solution)/shard_map/ppermute | solution.py:20
  23.7 1.6 %collective-permute-start.3 = (bf16[48,3072]{1,0:T(8,128)(2,1)S(1)}, bf16[48,3072]{1,0:T(8,128)(2,1)S(1)}, u32[]{:S(2)}, u32[]{:S(2)}) collective-permute-start(bf16[48,3072]{1,0:T(8,128)(2,1)S(1)} %slice.177), channel_id=1, source_target_pairs={{0,4},{1,5},{2,6},{3,7},{4,0},{5,1},{6,2},{7,3},{8,12},{9,13},{10,... | collective-permute-start | bytes 884744 | tf_op jit(solution)/shard_map/ppermute | solution.py:20
  25.8 4.4 %collective-permute-done.2.refs_3_ = bf16[48,3072]{1,0:T(8,128)(2,1)S(1)} collective-permute-done((bf16[48,3072]{1,0:T(8,128)(2,1)S(1)}, bf16[48,3072]{1,0:T(8,128)(2,1)S(1)}, u32[]{:S(2)}, u32[]{:S(2)}) %collective-permute-start.2) | collective-permute-done | bytes 294944 | tf_op jit(solution)/shard_map/ppermute | solution.py:20
  30.1 1.2 collective-permute-done.3.refs_4_
  31.3 1.5 %collective-permute-start.10 = (bf16[32,6144]{1,0:T(8,128)(2,1)S(1)}, bf16[32,6144]{1,0:T(8,128)(2,1)S(1)}, u32[]{:S(2)}, u32[]{:S(2)}) collective-permute-start(bf16[32,6144]{1,0:T(8,128)(2,1)S(1)} %get-tuple-element.79.refs_0_), channel_id=1, source_target_pairs={{0,4},{1,5},{2,6},{3,7},{4,0},{5,1},{6,2},{7,3},{8,12},{9,13},{10,... | collective-permute-start | bytes 1179656 | tf_op jit(solution)/shard_map/ppermute | solution.py:20
  33.6 14.7 %up.2.hidden_ref = bf16[384,1024]{1,0:T(8,128)(2,1)S(1)} custom-call(bf16[48,6144]{1,0:T(8,128)(2,1)S(1)} %get-tuple-element.57.refs_0_, bf16[48,6144]{1,0:T(8,128)(2,1)S(1)} %collective-permute-done.refs_1_, bf16[48,6144]{1,0:T(8,128)(2,1)S(1)} %collective-permute-done.1.refs_2_, bf16[48,3072]{1,0:T(8,128)(2,1)S(1)} %collective-permute-done.2.refs_3_, ...), custom_call_target="tpu_custom_call" | custom-call | flops 9663676416 | bytes 29884416 | tf_op jit(solution)/shard_map/up/pallas_call | solution.py:135
  48.3 1.4 %collective-permute-start.11 = (bf16[32,3072]{1,0:T(8,128)(2,1)S(1)}, bf16[32,3072]{1,0:T(8,128)(2,1)S(1)}, u32[]{:S(2)}, u32[]{:S(2)}) collective-permute-start(bf16[32,3072]{1,0:T(8,128)(2,1)S(1)} %slice.134), channel_id=1, source_target_pairs={{0,2},{1,3},{2,0},{3,1},{4,6},{5,7},{6,4},{7,5},{8,10},{9,11},{10,... | collective-permute-start | bytes 589832 | tf_op jit(solution)/shard_map/ppermute | solution.py:20
  50.3 9.3 %down.2 = (f32[48,6144]{1,0:T(8,128)}, f32[48,6144]{1,0:T(8,128)}, f32[48,6144]{1,0:T(8,128)}, f32[48,6144]{1,0:T(8,128)}, bf16[48,6144]{1,0:T(8,128)(2,1)}, /*i...) custom-call(bf16[384,1024]{1,0:T(8,128)(2,1)S(1)} %up.2.hidden_ref, ...), custom_call_target="tpu_custom_call" | custom-call | flops 4831838208 | bytes 19660800 | tf_op jit(solution)/shard_map/down/pallas_call | solution.py:198
  62.1 1.4 %fusion.11 = (bf16[1,48,3072]{2,1,0:T(8,128)(2,1)S(1)}, bf16[1,48,3072]{2,1,0:T(8,128)(2,1)S(1)}) fusion(f32[48,6144]{1,0:T(8,128)} %get-tuple-element.75, bf16[48,6144]{1,0:T(8,128)(2,1)S(1)} %collective-permute-done.15), kind=kLoop, calls=%fused_computation.51 | loop fusion | flops 884736 | bytes 2359296 | tf_op jit(solution)/shard_map/stack | solution.py:329
  65.7 1.6 %collective-permute-start.23 = (bf16[2,48,3072]{2,1,0:T(8,128)(2,1)S(1)}, bf16[2,48,3072]{2,1,0:T(8,128)(2,1)S(1)}, u32[]{:S(2)}, u32[]{:S(2)}) collective-permute-start(bf16[2,48,3072]{2,1,0:T(8,128)(2,1)S(1)} %pad_maximum_fusion.1), channel_id=1, source_target_pairs={{0,4},{1,5},{2,6},{3,7},{4,0},{5,1},{6,2},{7,3},{8,12},{9,13},{10,... | collective-permute-start | bytes 1769480 | tf_op jit(solution)/shard_map/ppermute | solution.py:20
  68.0 11.9 %up.3.hidden_ref = bf16[256,1024]{1,0:T(8,128)(2,1)S(1)} custom-call(bf16[32,6144]{1,0:T(8,128)(2,1)S(1)} %get-tuple-element.79.refs_0_, bf16[32,6144]{1,0:T(8,128)(2,1)S(1)} %collective-permute-done.9.refs_1_, bf16[32,6144]{1,0:T(8,128)(2,1)S(1)} %collective-permute-done.10.refs_2_, bf16[32,3072]{1,0:T(8,128)(2,1)S(1)} %collective-permute-done.11.refs_3_, ...), custom_call_target="tpu_custom_call" | custom-call | flops 6442450944 | bytes 28311552 | tf_op jit(solution)/shard_map/up/pallas_call | solution.py:135
  79.9 1.5 %collective-permute-done.23 = bf16[2,48,3072]{2,1,0:T(8,128)(2,1)S(1)} collective-permute-done((bf16[2,48,3072]{2,1,0:T(8,128)(2,1)S(1)}, bf16[2,48,3072]{2,1,0:T(8,128)(2,1)S(1)}, u32[]{:S(2)}, u32[]{:S(2)}) %collective-permute-start.23) | collective-permute-done | bytes 589856 | tf_op jit(solution)/shard_map/ppermute | solution.py:20
  81.3 1.3 collective-permute-done.22
  84.7 7.4 %down.3 = (f32[32,6144]{1,0:T(8,128)}, f32[32,6144]{1,0:T(8,128)}, f32[32,6144]{1,0:T(8,128)}, f32[32,6144]{1,0:T(8,128)}, bf16[32,6144]{1,0:T(8,128)(2,1)}, /*i...) custom-call(bf16[256,1024]{1,0:T(8,128)(2,1)S(1)} %up.3.hidden_ref, ...), custom_call_target="tpu_custom_call" | custom-call | flops 3221225472 | bytes 17301504 | tf_op jit(solution)/shard_map/down/pallas_call | solution.py:198
  94.1 1.2 fusion.17
  96.8 1.4 %collective-permute-start.30 = (bf16[2,32,3072]{2,1,0:T(8,128)(2,1)S(1)}, bf16[2,32,3072]{2,1,0:T(8,128)(2,1)S(1)}, u32[]{:S(2)}, u32[]{:S(2)}) collective-permute-start(bf16[2,32,3072]{2,1,0:T(8,128)(2,1)S(1)} %pad_maximum_fusion.2), channel_id=1, source_target_pairs={{0,2},{1,3},{2,0},{3,1},{4,6},{5,7},{6,4},{7,5},{8,10},{9,11},{10,... | collective-permute-start | bytes 1179656 | tf_op jit(solution)/shard_map/ppermute | solution.py:20
  98.9 1.6 %collective-permute-start.26 = (bf16[48,1536]{1,0:T(8,128)(2,1)S(1)}, bf16[48,1536]{1,0:T(8,128)(2,1)S(1)}, u32[]{:S(2)}, u32[]{:S(2)}) collective-permute-start(bf16[48,1536]{1,0:T(8,128)(2,1)S(1)} %get-tuple-element.117), channel_id=1, source_target_pairs={{0,8},{8,0},{16,24},{24,16},{1,9},{9,1},{17,25},{25,17},{2,10},{10... | collective-permute-start | bytes 442376 | tf_op jit(solution)/shard_map/ppermute | solution.py:20
  100.6 2.6 %collective-permute-start.27 = (bf16[48,1536]{1,0:T(8,128)(2,1)S(1)}, bf16[48,1536]{1,0:T(8,128)(2,1)S(1)}, u32[]{:S(2)}, u32[]{:S(2)}) collective-permute-start(bf16[48,1536]{1,0:T(8,128)(2,1)S(1)} %get-tuple-element.118), channel_id=1, source_target_pairs={{0,16},{8,24},{16,0},{24,8},{1,17},{9,25},{17,1},{25,9},{2,18},{10... | collective-permute-start | bytes 442376 | tf_op jit(solution)/shard_map/ppermute | solution.py:20
  103.2 3.6 %collective-permute-done.26.refs_5_ = bf16[48,1536]{1,0:T(8,128)(2,1)S(1)} collective-permute-done((bf16[48,1536]{1,0:T(8,128)(2,1)S(1)}, bf16[48,1536]{1,0:T(8,128)(2,1)S(1)}, u32[]{:S(2)}, u32[]{:S(2)}) %collective-permute-start.26) | collective-permute-done | bytes 147488 | tf_op jit(solution)/shard_map/ppermute | solution.py:20
  106.8 3.0 %collective-permute-done.27.refs_6_ = bf16[48,1536]{1,0:T(8,128)(2,1)S(1)} collective-permute-done((bf16[48,1536]{1,0:T(8,128)(2,1)S(1)}, bf16[48,1536]{1,0:T(8,128)(2,1)S(1)}, u32[]{:S(2)}, u32[]{:S(2)}) %collective-permute-start.27) | collective-permute-done | bytes 147488 | tf_op jit(solution)/shard_map/ppermute | solution.py:20
  111.8 2.5 %collective-permute-start.33 = (bf16[48,1536]{1,0:T(8,128)(2,1)S(1)}, bf16[48,1536]{1,0:T(8,128)(2,1)S(1)}, u32[]{:S(2)}, u32[]{:S(2)}) collective-permute-start(bf16[48,1536]{1,0:T(8,128)(2,1)S(1)} %get-tuple-element.115), channel_id=1, source_target_pairs={{0,24},{8,16},{16,8},{24,0},{1,25},{9,17},{17,9},{25,1},{2,26},{10... | collective-permute-start | bytes 442376 | tf_op jit(solution)/shard_map/ppermute | solution.py:20
  114.2 1.3 %collective-permute-done.35 = bf16[1,32,3072]{2,1,0:T(8,128)(2,1)S(1)} collective-permute-done((bf16[1,32,3072]{2,1,0:T(8,128)(2,1)S(1)}, bf16[1,32,3072]{2,1,0:T(8,128)(2,1)S(1)}, u32[]{:S(2)}, u32[]{:S(2)}) %collective-permute-start.35) | collective-permute-done | bytes 196640 | tf_op jit(solution)/shard_map/ppermute | solution.py:20
  117.8 2.6 %collective-permute-start.38 = (bf16[32,1536]{1,0:T(8,128)(2,1)S(1)}, bf16[32,1536]{1,0:T(8,128)(2,1)S(1)}, u32[]{:S(2)}, u32[]{:S(2)}) collective-permute-start(bf16[32,1536]{1,0:T(8,128)(2,1)S(1)} %get-tuple-element.122), channel_id=1, source_target_pairs={{0,16},{8,24},{16,0},{24,8},{1,17},{9,25},{17,1},{25,9},{2,18},{10... | collective-permute-start | bytes 294920 | tf_op jit(solution)/shard_map/ppermute | solution.py:20
  120.4 1.3 %collective-permute-start.39 = (bf16[32,1536]{1,0:T(8,128)(2,1)S(1)}, bf16[32,1536]{1,0:T(8,128)(2,1)S(1)}, u32[]{:S(2)}, u32[]{:S(2)}) collective-permute-start(bf16[32,1536]{1,0:T(8,128)(2,1)S(1)} %get-tuple-element.119), channel_id=1, source_target_pairs={{0,24},{8,16},{16,8},{24,0},{1,25},{9,17},{17,9},{25,1},{2,26},{10... | collective-permute-start | bytes 294920 | tf_op jit(solution)/shard_map/ppermute | solution.py:20
  122.8 2.5 %collective-permute-done.38.refs_10_ = bf16[32,1536]{1,0:T(8,128)(2,1)S(1)} collective-permute-done((bf16[32,1536]{1,0:T(8,128)(2,1)S(1)}, bf16[32,1536]{1,0:T(8,128)(2,1)S(1)}, u32[]{:S(2)}, u32[]{:S(2)}) %collective-permute-start.38) | collective-permute-done | bytes 98336 | tf_op jit(solution)/shard_map/ppermute | solution.py:20
  125.3 1.6 %collective-permute-done.39.refs_11_ = bf16[32,1536]{1,0:T(8,128)(2,1)S(1)} collective-permute-done((bf16[32,1536]{1,0:T(8,128)(2,1)S(1)}, bf16[32,1536]{1,0:T(8,128)(2,1)S(1)}, u32[]{:S(2)}, u32[]{:S(2)}) %collective-permute-start.39) | collective-permute-done | bytes 98336 | tf_op jit(solution)/shard_map/ppermute | solution.py:20
  126.9 2.1 %combine.1 = bf16[128,1536]{1,0:T(8,128)(2,1)} custom-call(s32[1]{0:T(128)} %bitcast.refs_0_, bf16[128,1536]{1,0:T(8,128)(2,1)S(1)} %constant_dynamic-slice_fusion.refs_1_, s32[128,2]{1,0:T(8,128)S(1)} %bitcast.78, f32[128,2]{1,0:T(8,128)S(1)} %get-tuple-element.56.refs_3_, bf16[48,1536]{1,0:T(8,128)(2,1)S(1)} %get-tuple-element.116.refs_4_, ...), custom_call_target="tpu_custom_call" | custom-call | tf_op jit(solution)/shard_map/combine/pallas_call | solution.py:261
  (105 shorter events, 21.1 us)
Async XLA Ops:
  5.5 16.4 %collective-permute-start.1 = (bf16[48,6144]{1,0:T(8,128)(2,1)S(1)}, bf16[48,6144]{1,0:T(8,128)(2,1)S(1)}, u32[]{:S(2)}, u32[]{:S(2)}) collective-permute-start(bf16[48,6144]{1,0:T(8,128)(2,1)S(1)} %get-tuple-element.57.refs_0_), channel_id=1, source_target_pairs={{0,4},{1,5},{2,6},{3,7},{4,0},{5,1},{6,2},{7,3},{8,12},{9,13},{10,... | collective-permute-start | bytes 1769480 | tf_op jit(solution)/shard_map/ppermute | solution.py:20
  8.5 15.1 %collective-permute-start = (bf16[48,6144]{1,0:T(8,128)(2,1)S(1)}, bf16[48,6144]{1,0:T(8,128)(2,1)S(1)}, u32[]{:S(2)}, u32[]{:S(2)}) collective-permute-start(bf16[48,6144]{1,0:T(8,128)(2,1)S(1)} %get-tuple-element.57.refs_0_), channel_id=1, source_target_pairs={{0,2},{1,3},{2,0},{3,1},{4,6},{5,7},{6,4},{7,5},{8,10},{9,11},{10,... | collective-permute-start | bytes 1769480 | tf_op jit(solution)/shard_map/ppermute | solution.py:20
  10.0 21.3 %collective-permute-start.4 = (bf16[48,6144]{1,0:T(8,128)(2,1)S(1)}, bf16[48,6144]{1,0:T(8,128)(2,1)S(1)}, u32[]{:S(2)}, u32[]{:S(2)}) collective-permute-start(bf16[48,6144]{1,0:T(8,128)(2,1)S(1)} %get-tuple-element.57.refs_0_), channel_id=1, source_target_pairs={{0,1},{1,0},{2,3},{3,2},{4,5},{5,4},{6,7},{7,6},{8,9},{9,8},{10,11... | collective-permute-start | bytes 1769480 | tf_op jit(solution)/shard_map/ppermute | solution.py:20
  21.8 8.3 %collective-permute-start.2 = (bf16[48,3072]{1,0:T(8,128)(2,1)S(1)}, bf16[48,3072]{1,0:T(8,128)(2,1)S(1)}, u32[]{:S(2)}, u32[]{:S(2)}) collective-permute-start(bf16[48,3072]{1,0:T(8,128)(2,1)S(1)} %slice.176), channel_id=1, source_target_pairs={{0,2},{1,3},{2,0},{3,1},{4,6},{5,7},{6,4},{7,5},{8,10},{9,11},{10,... | collective-permute-start | bytes 884744 | tf_op jit(solution)/shard_map/ppermute | solution.py:20
  23.7 7.7 %collective-permute-start.3 = (bf16[48,3072]{1,0:T(8,128)(2,1)S(1)}, bf16[48,3072]{1,0:T(8,128)(2,1)S(1)}, u32[]{:S(2)}, u32[]{:S(2)}) collective-permute-start(bf16[48,3072]{1,0:T(8,128)(2,1)S(1)} %slice.177), channel_id=1, source_target_pairs={{0,4},{1,5},{2,6},{3,7},{4,0},{5,1},{6,2},{7,3},{8,12},{9,13},{10,... | collective-permute-start | bytes 884744 | tf_op jit(solution)/shard_map/ppermute | solution.py:20
  25.2 8.3 %collective-permute-start.5 = (bf16[48,6144]{1,0:T(8,128)(2,1)S(1)}, bf16[48,6144]{1,0:T(8,128)(2,1)S(1)}, u32[]{:S(2)}, u32[]{:S(2)}) collective-permute-start(bf16[48,6144]{1,0:T(8,128)(2,1)S(1)} %collective-permute-done.refs_1_), channel_id=1, source_target_pairs={{0,1},{1,0},{2,3},{3,2},{4,5},{5,4},{6,7},{7,6},{8,9},{9,8},{10,11... | collective-permute-start | bytes 1769480 | tf_op jit(solution)/shard_map/ppermute | solution.py:20
  25.3 8.3 %collective-permute-start.6 = (bf16[48,6144]{1,0:T(8,128)(2,1)S(1)}, bf16[48,6144]{1,0:T(8,128)(2,1)S(1)}, u32[]{:S(2)}, u32[]{:S(2)}) collective-permute-start(bf16[48,6144]{1,0:T(8,128)(2,1)S(1)} %collective-permute-done.1.refs_2_), channel_id=1, source_target_pairs={{0,1},{1,0},{2,3},{3,2},{4,5},{5,4},{6,7},{7,6},{8,9},{9,8},{10,11... | collective-permute-start | bytes 1769480 | tf_op jit(solution)/shard_map/ppermute | solution.py:20
  31.3 17.0 %collective-permute-start.10 = (bf16[32,6144]{1,0:T(8,128)(2,1)S(1)}, bf16[32,6144]{1,0:T(8,128)(2,1)S(1)}, u32[]{:S(2)}, u32[]{:S(2)}) collective-permute-start(bf16[32,6144]{1,0:T(8,128)(2,1)S(1)} %get-tuple-element.79.refs_0_), channel_id=1, source_target_pairs={{0,4},{1,5},{2,6},{3,7},{4,0},{5,1},{6,2},{7,3},{8,12},{9,13},{10,... | collective-permute-start | bytes 1179656 | tf_op jit(solution)/shard_map/ppermute | solution.py:20
  32.9 15.4 %collective-permute-start.9 = (bf16[32,6144]{1,0:T(8,128)(2,1)S(1)}, bf16[32,6144]{1,0:T(8,128)(2,1)S(1)}, u32[]{:S(2)}, u32[]{:S(2)}) collective-permute-start(bf16[32,6144]{1,0:T(8,128)(2,1)S(1)} %get-tuple-element.79.refs_0_), channel_id=1, source_target_pairs={{0,2},{1,3},{2,0},{3,1},{4,6},{5,7},{6,4},{7,5},{8,10},{9,11},{10,... | collective-permute-start | bytes 1179656 | tf_op jit(solution)/shard_map/ppermute | solution.py:20
  48.3 11.3 %collective-permute-start.11 = (bf16[32,3072]{1,0:T(8,128)(2,1)S(1)}, bf16[32,3072]{1,0:T(8,128)(2,1)S(1)}, u32[]{:S(2)}, u32[]{:S(2)}) collective-permute-start(bf16[32,3072]{1,0:T(8,128)(2,1)S(1)} %slice.134), channel_id=1, source_target_pairs={{0,2},{1,3},{2,0},{3,1},{4,6},{5,7},{6,4},{7,5},{8,10},{9,11},{10,... | collective-permute-start | bytes 589832 | tf_op jit(solution)/shard_map/ppermute | solution.py:20
  49.7 9.9 %collective-permute-start.12 = (bf16[32,3072]{1,0:T(8,128)(2,1)S(1)}, bf16[32,3072]{1,0:T(8,128)(2,1)S(1)}, u32[]{:S(2)}, u32[]{:S(2)}) collective-permute-start(bf16[32,3072]{1,0:T(8,128)(2,1)S(1)} %slice.135), channel_id=1, source_target_pairs={{0,4},{1,5},{2,6},{3,7},{4,0},{5,1},{6,2},{7,3},{8,12},{9,13},{10,... | collective-permute-start | bytes 589832 | tf_op jit(solution)/shard_map/ppermute | solution.py:20
  59.8 5.9 %collective-permute-start.17 = (bf16[32,6144]{1,0:T(8,128)(2,1)S(1)}, bf16[32,6144]{1,0:T(8,128)(2,1)S(1)}, u32[]{:S(2)}, u32[]{:S(2)}) collective-permute-start(bf16[32,6144]{1,0:T(8,128)(2,1)S(1)} %get-tuple-element.79.refs_0_), channel_id=1, source_target_pairs={{0,1},{1,0},{2,3},{3,2},{4,5},{5,4},{6,7},{7,6},{8,9},{9,8},{10,11... | collective-permute-start | bytes 1179656 | tf_op jit(solution)/shard_map/ppermute | solution.py:20
  60.2 7.7 %collective-permute-start.18 = (bf16[32,6144]{1,0:T(8,128)(2,1)S(1)}, bf16[32,6144]{1,0:T(8,128)(2,1)S(1)}, u32[]{:S(2)}, u32[]{:S(2)}) collective-permute-start(bf16[32,6144]{1,0:T(8,128)(2,1)S(1)} %collective-permute-done.9.refs_1_), channel_id=1, source_target_pairs={{0,1},{1,0},{2,3},{3,2},{4,5},{5,4},{6,7},{7,6},{8,9},{9,8},{10,11... | collective-permute-start | bytes 1179656 | tf_op jit(solution)/shard_map/ppermute | solution.py:20
  60.3 7.7 %collective-permute-start.19 = (bf16[32,6144]{1,0:T(8,128)(2,1)S(1)}, bf16[32,6144]{1,0:T(8,128)(2,1)S(1)}, u32[]{:S(2)}, u32[]{:S(2)}) collective-permute-start(bf16[32,6144]{1,0:T(8,128)(2,1)S(1)} %collective-permute-done.10.refs_2_), channel_id=1, source_target_pairs={{0,1},{1,0},{2,3},{3,2},{4,5},{5,4},{6,7},{7,6},{8,9},{9,8},{10,11... | collective-permute-start | bytes 1179656 | tf_op jit(solution)/shard_map/ppermute | solution.py:20
  60.8 3.4 %collective-permute-start.16 = (bf16[48,6144]{1,0:T(8,128)(2,1)}, bf16[48,6144]{1,0:T(8,128)(2,1)S(1)}, u32[]{:S(2)}, u32[]{:S(2)}) collective-permute-start(bf16[48,6144]{1,0:T(8,128)(2,1)} %get-tuple-element.78), channel_id=1, source_target_pairs={{0,1},{1,0},{2,3},{3,2},{4,5},{5,4},{6,7},{7,6},{8,9},{9,8},{10,11... | collective-permute-start | bytes 1769480 | tf_op jit(solution)/shard_map/ppermute | solution.py:20
  65.7 15.7 %collective-permute-start.23 = (bf16[2,48,3072]{2,1,0:T(8,128)(2,1)S(1)}, bf16[2,48,3072]{2,1,0:T(8,128)(2,1)S(1)}, u32[]{:S(2)}, u32[]{:S(2)}) collective-permute-start(bf16[2,48,3072]{2,1,0:T(8,128)(2,1)S(1)} %pad_maximum_fusion.1), channel_id=1, source_target_pairs={{0,4},{1,5},{2,6},{3,7},{4,0},{5,1},{6,2},{7,3},{8,12},{9,13},{10,... | collective-permute-start | bytes 1769480 | tf_op jit(solution)/shard_map/ppermute | solution.py:20
  67.3 15.3 %collective-permute-start.22 = (bf16[2,48,3072]{2,1,0:T(8,128)(2,1)S(1)}, bf16[2,48,3072]{2,1,0:T(8,128)(2,1)S(1)}, u32[]{:S(2)}, u32[]{:S(2)}) collective-permute-start(bf16[2,48,3072]{2,1,0:T(8,128)(2,1)S(1)} %pad_maximum_fusion), channel_id=1, source_target_pairs={{0,2},{1,3},{2,0},{3,1},{4,6},{5,7},{6,4},{7,5},{8,10},{9,11},{10,... | collective-permute-start | bytes 1769480 | tf_op jit(solution)/shard_map/ppermute | solution.py:20
  82.7 9.4 %collective-permute-start.25 = (bf16[1,48,3072]{2,1,0:T(8,128)(2,1)S(1)}, bf16[1,48,3072]{2,1,0:T(8,128)(2,1)S(1)}, u32[]{:S(2)}, u32[]{:S(2)}) collective-permute-start(bf16[1,48,3072]{2,1,0:T(8,128)(2,1)S(1)} %fusion.13), channel_id=1, source_target_pairs={{0,2},{1,3},{2,0},{3,1},{4,6},{5,7},{6,4},{7,5},{8,10},{9,11},{10,... | collective-permute-start | bytes 884744 | tf_op jit(solution)/shard_map/ppermute | solution.py:20
  83.5 8.6 %collective-permute-start.24 = (bf16[1,48,3072]{2,1,0:T(8,128)(2,1)S(1)}, bf16[1,48,3072]{2,1,0:T(8,128)(2,1)S(1)}, u32[]{:S(2)}, u32[]{:S(2)}) collective-permute-start(bf16[1,48,3072]{2,1,0:T(8,128)(2,1)S(1)} %fusion.12), channel_id=1, source_target_pairs={{0,4},{1,5},{2,6},{3,7},{4,0},{5,1},{6,2},{7,3},{8,12},{9,13},{10,... | collective-permute-start | bytes 884744 | tf_op jit(solution)/shard_map/ppermute | solution.py:20
  92.2 5.9 %collective-permute-start.13 = (bf16[48,6144]{1,0:T(8,128)(2,1)}, bf16[48,6144]{1,0:T(8,128)(2,1)S(1)}, u32[]{:S(2)}, u32[]{:S(2)}) collective-permute-start(bf16[48,6144]{1,0:T(8,128)(2,1)} %get-tuple-element.72), channel_id=1, source_target_pairs={{0,1},{1,0},{2,3},{3,2},{4,5},{5,4},{6,7},{7,6},{8,9},{9,8},{10,11... | collective-permute-start | bytes 1769480 | tf_op jit(solution)/shard_map/ppermute | solution.py:20
  92.8 3.9 %collective-permute-start.28 = (bf16[32,6144]{1,0:T(8,128)(2,1)}, bf16[32,6144]{1,0:T(8,128)(2,1)S(1)}, u32[]{:S(2)}, u32[]{:S(2)}) collective-permute-start(bf16[32,6144]{1,0:T(8,128)(2,1)} %get-tuple-element.96), channel_id=1, source_target_pairs={{0,1},{1,0},{2,3},{3,2},{4,5},{5,4},{6,7},{7,6},{8,9},{9,8},{10,11... | collective-permute-start | bytes 1179656 | tf_op jit(solution)/shard_map/ppermute | solution.py:20
  95.7 14.1 %collective-permute-start.32 = (bf16[2,32,3072]{2,1,0:T(8,128)(2,1)S(1)}, bf16[2,32,3072]{2,1,0:T(8,128)(2,1)S(1)}, u32[]{:S(2)}, u32[]{:S(2)}) collective-permute-start(bf16[2,32,3072]{2,1,0:T(8,128)(2,1)S(1)} %pad_maximum_fusion.3), channel_id=1, source_target_pairs={{0,4},{1,5},{2,6},{3,7},{4,0},{5,1},{6,2},{7,3},{8,12},{9,13},{10,... | collective-permute-start | bytes 1179656 | tf_op jit(solution)/shard_map/ppermute | solution.py:20
  96.8 12.9 %collective-permute-start.30 = (bf16[2,32,3072]{2,1,0:T(8,128)(2,1)S(1)}, bf16[2,32,3072]{2,1,0:T(8,128)(2,1)S(1)}, u32[]{:S(2)}, u32[]{:S(2)}) collective-permute-start(bf16[2,32,3072]{2,1,0:T(8,128)(2,1)S(1)} %pad_maximum_fusion.2), channel_id=1, source_target_pairs={{0,2},{1,3},{2,0},{3,1},{4,6},{5,7},{6,4},{7,5},{8,10},{9,11},{10,... | collective-permute-start | bytes 1179656 | tf_op jit(solution)/shard_map/ppermute | solution.py:20
  98.9 7.8 %collective-permute-start.26 = (bf16[48,1536]{1,0:T(8,128)(2,1)S(1)}, bf16[48,1536]{1,0:T(8,128)(2,1)S(1)}, u32[]{:S(2)}, u32[]{:S(2)}) collective-permute-start(bf16[48,1536]{1,0:T(8,128)(2,1)S(1)} %get-tuple-element.117), channel_id=1, source_target_pairs={{0,8},{8,0},{16,24},{24,16},{1,9},{9,1},{17,25},{25,17},{2,10},{10... | collective-permute-start | bytes 442376 | tf_op jit(solution)/shard_map/ppermute | solution.py:20
  100.6 9.2 %collective-permute-start.27 = (bf16[48,1536]{1,0:T(8,128)(2,1)S(1)}, bf16[48,1536]{1,0:T(8,128)(2,1)S(1)}, u32[]{:S(2)}, u32[]{:S(2)}) collective-permute-start(bf16[48,1536]{1,0:T(8,128)(2,1)S(1)} %get-tuple-element.118), channel_id=1, source_target_pairs={{0,16},{8,24},{16,0},{24,8},{1,17},{9,25},{17,1},{25,9},{2,18},{10... | collective-permute-start | bytes 442376 | tf_op jit(solution)/shard_map/ppermute | solution.py:20
  103.2 11.1 %collective-permute-start.34 = (bf16[32,6144]{1,0:T(8,128)(2,1)S(1)}, bf16[32,6144]{1,0:T(8,128)(2,1)S(1)}, u32[]{:S(2)}, u32[]{:S(2)}) collective-permute-start(bf16[32,6144]{1,0:T(8,128)(2,1)S(1)} %copy-done.8), channel_id=1, source_target_pairs={{0,1},{1,0},{2,3},{3,2},{4,5},{5,4},{6,7},{7,6},{8,9},{9,8},{10,11... | collective-permute-start | bytes 1179656 | tf_op jit(solution)/shard_map/ppermute | solution.py:20
  109.8 5.7 %collective-permute-start.35 = (bf16[1,32,3072]{2,1,0:T(8,128)(2,1)S(1)}, bf16[1,32,3072]{2,1,0:T(8,128)(2,1)S(1)}, u32[]{:S(2)}, u32[]{:S(2)}) collective-permute-start(bf16[1,32,3072]{2,1,0:T(8,128)(2,1)S(1)} %fusion.18), channel_id=1, source_target_pairs={{0,4},{1,5},{2,6},{3,7},{4,0},{5,1},{6,2},{7,3},{8,12},{9,13},{10,... | collective-permute-start | bytes 589832 | tf_op jit(solution)/shard_map/ppermute | solution.py:20
  111.0 5.7 %collective-permute-start.36 = (bf16[1,32,3072]{2,1,0:T(8,128)(2,1)S(1)}, bf16[1,32,3072]{2,1,0:T(8,128)(2,1)S(1)}, u32[]{:S(2)}, u32[]{:S(2)}) collective-permute-start(bf16[1,32,3072]{2,1,0:T(8,128)(2,1)S(1)} %fusion.19), channel_id=1, source_target_pairs={{0,2},{1,3},{2,0},{3,1},{4,6},{5,7},{6,4},{7,5},{8,10},{9,11},{10,... | collective-permute-start | bytes 589832 | tf_op jit(solution)/shard_map/ppermute | solution.py:20
  111.8 11.0 %collective-permute-start.33 = (bf16[48,1536]{1,0:T(8,128)(2,1)S(1)}, bf16[48,1536]{1,0:T(8,128)(2,1)S(1)}, u32[]{:S(2)}, u32[]{:S(2)}) collective-permute-start(bf16[48,1536]{1,0:T(8,128)(2,1)S(1)} %get-tuple-element.115), channel_id=1, source_target_pairs={{0,24},{8,16},{16,8},{24,0},{1,25},{9,17},{17,9},{25,1},{2,26},{10... | collective-permute-start | bytes 442376 | tf_op jit(solution)/shard_map/ppermute | solution.py:20
  117.3 5.5 %collective-permute-start.37 = (bf16[32,1536]{1,0:T(8,128)(2,1)S(1)}, bf16[32,1536]{1,0:T(8,128)(2,1)S(1)}, u32[]{:S(2)}, u32[]{:S(2)}) collective-permute-start(bf16[32,1536]{1,0:T(8,128)(2,1)S(1)} %get-tuple-element.121), channel_id=1, source_target_pairs={{0,8},{8,0},{16,24},{24,16},{1,9},{9,1},{17,25},{25,17},{2,10},{10... | collective-permute-start | bytes 294920 | tf_op jit(solution)/shard_map/ppermute | solution.py:20
  117.8 7.5 %collective-permute-start.38 = (bf16[32,1536]{1,0:T(8,128)(2,1)S(1)}, bf16[32,1536]{1,0:T(8,128)(2,1)S(1)}, u32[]{:S(2)}, u32[]{:S(2)}) collective-permute-start(bf16[32,1536]{1,0:T(8,128)(2,1)S(1)} %get-tuple-element.122), channel_id=1, source_target_pairs={{0,16},{8,24},{16,0},{24,8},{1,17},{9,25},{17,1},{25,9},{2,18},{10... | collective-permute-start | bytes 294920 | tf_op jit(solution)/shard_map/ppermute | solution.py:20
  120.4 6.5 %collective-permute-start.39 = (bf16[32,1536]{1,0:T(8,128)(2,1)S(1)}, bf16[32,1536]{1,0:T(8,128)(2,1)S(1)}, u32[]{:S(2)}, u32[]{:S(2)}) collective-permute-start(bf16[32,1536]{1,0:T(8,128)(2,1)S(1)} %get-tuple-element.119), channel_id=1, source_target_pairs={{0,24},{8,16},{16,8},{24,0},{1,25},{9,17},{17,9},{25,1},{2,26},{10... | collective-permute-start | bytes 294920 | tf_op jit(solution)/shard_map/ppermute | solution.py:20
  (20 other events, 120.0 us)
